TPU v7x, 32 devices: a whole 2x2x4 slice. The times are simulated.
32 devices in a mesh: dp: 8 (over y, x, core), tensor: 4 (over z).
Axes of the slice: x: 2, y: 2, z: 4, core: 2. Of those that a mesh axis runs over, the one named last changes fastest.
Arguments:
- tokens: bfloat16 [1024, 16384], P(None, ('dp', 'tensor')), may hold values from -6 to 6
- cotangent: bfloat16 [1024, 16384], P(None, ('dp', 'tensor')), may hold values from -6 to 6
- first_gain: float32 [2048], replicated, may hold values from 0.5 to 1.5
- query_weight: bfloat16 [2048, 2048], P(None, 'tensor'), may hold values from -0.125 to 0.125
- key_matrix: bfloat16 [2048, 512], P(None, 'tensor'), may hold values from -0.125 to 0.125
- value_matrix: bfloat16 [2048, 512], P(None, 'tensor'), may hold values from -0.125 to 0.125
- output_weight: bfloat16 [2048, 2048], P('tensor'), may hold values from -1 to 1
- second_gain: float32 [2048], replicated, may hold values from 0.5 to 1.5
- gate_weight: bfloat16 [2048, 5632], P(None, 'tensor'), may hold values from -0.125 to 0.125
- up_weight: bfloat16 [2048, 5632], P(None, 'tensor'), may hold values from -0.125 to 0.125
- down_weight: bfloat16 [5632, 2048], P('tensor'), may hold values from -0.078125 to 0.078125
- seq_lengths: int32 [32], replicated, may hold values from 8 to 1024, as said below
- owner_order: int32 [32], replicated, may hold values from 0 to 31, as said below
- skip_mask: int32 [32], replicated, may hold values 0 or 1
Outputs:
- layer_output: bfloat16 [1024, 16384], P(None, ('dp', 'tensor'))
- input_grad: bfloat16 [1024, 16384], P(None, ('dp', 'tensor'))
- first_gain_grad: float32 [2048], P('dp')
- query_grad: float32 [2048, 2048], P('dp', 'tensor')
- key_grad: float32 [2048, 512], P('dp', 'tensor')
- value_grad: float32 [2048, 512], P('dp', 'tensor')
- output_grad: float32 [2048, 2048], P('tensor', 'dp')
- second_gain_grad: float32 [2048], P('dp')
- gate_grad: float32 [2048, 5632], P('dp', 'tensor')
- up_grad: float32 [2048, 5632], P('dp', 'tensor')
- down_grad: float32 [5632, 2048], P('tensor', 'dp')
Inputs may be any that keep to these rules, and one draw needn't show every extreme that they name: `seq_lengths`: every length is a multiple of 8 and they sum to 8192. Taken in the order owner_order, the running sums meet every multiple of 1024, so that owner j, the j-th run of 1024 tokens in that order, holds whole sequences; the longest is exactly 1024. `owner_order`: each of 0 to 31 appears once.
All inputs are finite; a program needn't handle non-finite values.
Results may differ from a plain program's by a relative error of at most 0.018.
Values may be sent and summed in bfloat16 or wider, within the bound.
A program may use at most 256 MiB of HBM per device.

v0:
```python
import math

import jax
import jax.numpy as jnp
from jax import lax
from jax.sharding import PartitionSpec as P

HEAD_WIDTH = 128


eps = 1e-05
rope_base = 10000.0


def rotary_tables(token_positions, head_size):
    half = head_size // 2
    freqs = rope_base ** (-(jnp.arange(half).astype(jnp.float32) * 2.0) / head_size)
    angles = token_positions.astype(jnp.float32)[:, None] * freqs[None, :]
    angles = jnp.concatenate([angles, angles], axis=1)
    return (jnp.cos(angles), jnp.sin(angles))


def rotate_half(values):
    half = values.shape[-1] // 2
    return jnp.concatenate([-values[..., half:], values[..., :half]], axis=-1)


def rotate_back(values):
    half = values.shape[-1] // 2
    return jnp.concatenate([values[..., half:], -values[..., :half]], axis=-1)


def matmul(left, right):
    return jnp.dot(left, right, preferred_element_type=jnp.float32)


def per_device(
    tokens,
    cotangent,
    first_gain,
    query_weight,
    key_matrix,
    value_matrix,
    output_weight,
    second_gain,
    gate_weight,
    up_weight,
    down_weight,
    seq_lengths,
    owner_order,
    skip_mask,
):
    groups = lax.axis_size("dp")
    member = lax.axis_index("dp")
    width_part = tokens.shape[1]
    row_count = tokens.shape[0]
    per_owner = row_count // groups
    seq_count = seq_lengths.shape[0]
    seq_index = jnp.arange(seq_count, dtype=jnp.int32)
    starts = jnp.cumsum(seq_lengths) - seq_lengths
    placed = (owner_order[:, None] == seq_index[None, :]).astype(jnp.int32)
    owner_lengths = jnp.sum(placed * seq_lengths[None, :], axis=1)
    owner_before = jnp.cumsum(owner_lengths) - owner_lengths
    owner_of = jnp.sum(placed * (owner_before // row_count)[:, None], axis=0)
    global_row = jnp.arange(row_count, dtype=jnp.int32) * groups + member
    inside = (
        (global_row[:, None] >= starts[None, :])
        & (global_row[:, None] < (starts + seq_lengths)[None, :])
    ).astype(jnp.int32)
    row_owner = jnp.sum(inside * owner_of[None, :], axis=1)
    owner_hot = (row_owner[:, None] == jnp.arange(groups, dtype=jnp.int32)[None, :]).astype(
        jnp.int32
    )
    rank_in = jnp.sum((jnp.cumsum(owner_hot, axis=0) - 1) * owner_hot, axis=1)
    slot_of = row_owner * per_owner + rank_in
    send_rows = (
        jnp.zeros((row_count,), jnp.int32).at[slot_of].set(jnp.arange(row_count, dtype=jnp.int32))
    )
    is_mine = (owner_of == member).astype(jnp.int32)
    units_mine = seq_lengths // groups * is_mine
    before_mine = jnp.cumsum(units_mine) - units_mine
    places = jnp.arange(per_owner, dtype=jnp.int32)
    covers = (
        (places[:, None] >= before_mine[None, :])
        & (places[:, None] < (before_mine + units_mine)[None, :])
    ).astype(jnp.int32)
    slot_seq = jnp.sum(covers * seq_index[None, :], axis=1)
    slot_step = places - jnp.sum(covers * before_mine[None, :], axis=1)
    slot_keep = jnp.sum(covers * skip_mask[None, :], axis=1)
    sources = jnp.arange(groups, dtype=jnp.int32)
    token_positions = (sources[:, None] + groups * slot_step[None, :]).reshape(row_count)
    sequence_id = jnp.broadcast_to(slot_seq[None, :], (groups, per_owner)).reshape(row_count)
    keep_rows = (
        jnp.broadcast_to(slot_keep[None, :], (groups, per_owner))
        .reshape(row_count, 1)
        .astype(jnp.float32)
    )
    part_tokens, part_cotangent = (
        lax.all_to_all(tokens[send_rows], "dp", split_axis=0, concat_axis=0, tiled=True),
        lax.all_to_all(cotangent[send_rows], "dp", split_axis=0, concat_axis=0, tiled=True),
    )
    owned_tokens, owned_cotangent = (
        lax.all_gather(part_tokens, "tensor", axis=1, tiled=True),
        lax.all_gather(part_cotangent, "tensor", axis=1, tiled=True),
    )
    local_heads = query_weight.shape[1] // HEAD_WIDTH
    local_kv = key_matrix.shape[1] // HEAD_WIDTH
    group_size = local_heads // local_kv
    score_scale = 1.0 / math.sqrt(HEAD_WIDTH)
    tensor_member = lax.axis_index("tensor")
    inputs = owned_tokens.astype(jnp.float32)
    scale_one = lax.rsqrt(jnp.mean(inputs * inputs, axis=1, keepdims=True) + eps)
    normed_one = (inputs * scale_one * first_gain).astype(jnp.bfloat16)
    query_pre = matmul(normed_one, query_weight)
    key_unrotated = matmul(normed_one, key_matrix)
    value_pre = matmul(normed_one, value_matrix)
    cosine, sine = rotary_tables(token_positions, HEAD_WIDTH)

    def apply_rotation(values):
        return values * cosine[:, None, :] + rotate_half(values) * sine[:, None, :]

    def unrotate(values):
        return values * cosine[:, None, :] + rotate_back(values * sine[:, None, :])

    query_four_axes = (
        apply_rotation(query_pre.reshape(row_count, local_heads, HEAD_WIDTH))
        .astype(jnp.bfloat16)
        .reshape(row_count, local_kv, group_size, HEAD_WIDTH)
    )
    key_low = apply_rotation(key_unrotated.reshape(row_count, local_kv, HEAD_WIDTH)).astype(
        jnp.bfloat16
    )
    value_low = value_pre.reshape(row_count, local_kv, HEAD_WIDTH).astype(jnp.bfloat16)
    allowed = (sequence_id[:, None] == sequence_id[None, :]) & (
        token_positions[None, :] <= token_positions[:, None]
    )

    def scores_of():
        raw = (
            jnp.einsum(
                "qcgd,kcd->cgqk", query_four_axes, key_low, preferred_element_type=jnp.float32
            )
            * score_scale
        )
        return jnp.where(allowed, raw, -1e30)

    scores = scores_of()
    highest = jnp.max(scores, axis=-1, keepdims=True)
    expo = jnp.exp(scores - highest)
    denominator = jnp.sum(expo, axis=-1, keepdims=True)
    logsum = highest + jnp.log(denominator)
    probs_low = (expo / denominator).astype(jnp.bfloat16)
    attended_rows = jnp.einsum(
        "cgqk,kcd->qcgd", probs_low, value_low, preferred_element_type=jnp.float32
    )
    attended_low = attended_rows.reshape(row_count, local_heads * HEAD_WIDTH).astype(jnp.bfloat16)
    attn_term = matmul(attended_low, output_weight)
    attn_out = lax.psum(attn_term, "tensor")
    hidden_res = inputs + keep_rows * attn_out
    scale_two = lax.rsqrt(jnp.mean(hidden_res * hidden_res, axis=1, keepdims=True) + eps)
    normed_two = (hidden_res * scale_two * second_gain).astype(jnp.bfloat16)
    gate = matmul(normed_two, gate_weight)
    upward = matmul(normed_two, up_weight)
    gate_sig = jax.nn.sigmoid(gate)
    silu_val = gate * gate_sig
    inner_low = (silu_val * upward).astype(jnp.bfloat16)
    ffn_term = matmul(inner_low, down_weight)
    ffn_out = lax.psum(ffn_term.astype(jnp.bfloat16), "tensor").astype(jnp.float32)
    result = hidden_res + keep_rows * ffn_out
    grad_out = owned_cotangent.astype(jnp.float32)
    grad_ffn = (keep_rows * grad_out).astype(jnp.bfloat16)
    grad_inner = matmul(grad_ffn, down_weight.T)
    down_grad = matmul(inner_low.T, grad_ffn)
    grad_gate = (grad_inner * upward * gate_sig * (1.0 + gate * (1.0 - gate_sig))).astype(
        jnp.bfloat16
    )
    grad_up = (grad_inner * silu_val).astype(jnp.bfloat16)
    second_term = matmul(grad_gate, gate_weight.T) + matmul(grad_up, up_weight.T)
    gate_grad = matmul(normed_two.T, grad_gate)
    up_grad = matmul(normed_two.T, grad_up)
    second_back = lax.psum(second_term, "tensor")
    second_gain_grad = jnp.sum(second_back * hidden_res * scale_two, axis=0)
    scaled_two = second_back * second_gain
    grad_res = (
        grad_out
        + scale_two * scaled_two
        - hidden_res * scale_two**3 * jnp.mean(scaled_two * hidden_res, axis=1, keepdims=True)
    )
    grad_attn = (keep_rows * grad_res).astype(jnp.bfloat16)
    grad_attended = matmul(grad_attn, output_weight.T)
    output_grad = matmul(attended_low.T, grad_attn)
    grad_attended_low = grad_attended.reshape(row_count, local_kv, group_size, HEAD_WIDTH).astype(
        jnp.bfloat16
    )
    probs = jnp.exp(scores_of() - logsum)
    probs_again = probs.astype(jnp.bfloat16)
    grad_value = jnp.einsum(
        "cgqk,qcgd->kcd", probs_again, grad_attended_low, preferred_element_type=jnp.float32
    )
    grad_probs = jnp.einsum(
        "qcgd,kcd->cgqk", grad_attended_low, value_low, preferred_element_type=jnp.float32
    )
    grad_scores = (
        probs * (grad_probs - jnp.sum(probs * grad_probs, axis=-1, keepdims=True))
    ).astype(jnp.bfloat16)
    grad_query = (
        jnp.einsum("cgqk,kcd->qcgd", grad_scores, key_low, preferred_element_type=jnp.float32)
        * score_scale
    )
    grad_key = (
        jnp.einsum(
            "cgqk,qcgd->kcd", grad_scores, query_four_axes, preferred_element_type=jnp.float32
        )
        * score_scale
    )
    grad_query_low = (
        unrotate(grad_query.reshape(row_count, local_heads, HEAD_WIDTH))
        .reshape(row_count, local_heads * HEAD_WIDTH)
        .astype(jnp.bfloat16)
    )
    grad_key_low = unrotate(grad_key).reshape(row_count, local_kv * HEAD_WIDTH).astype(jnp.bfloat16)
    grad_value_low = grad_value.reshape(row_count, local_kv * HEAD_WIDTH).astype(jnp.bfloat16)
    first_back = lax.psum(
        matmul(grad_query_low, query_weight.T)
        + matmul(grad_key_low, key_matrix.T)
        + matmul(grad_value_low, value_matrix.T),
        "tensor",
    )
    query_grad = matmul(normed_one.T, grad_query_low)
    key_grad = matmul(normed_one.T, grad_key_low)
    value_grad = matmul(normed_one.T, grad_value_low)
    first_gain_grad = jnp.sum(first_back * inputs * scale_one, axis=0)
    scaled_one = first_back * first_gain
    grad_in = (
        grad_res
        + scale_one * scaled_one
        - inputs * scale_one**3 * jnp.mean(scaled_one * inputs, axis=1, keepdims=True)
    )
    out_part = lax.dynamic_slice_in_dim(result, tensor_member * width_part, width_part, 1).astype(
        jnp.bfloat16
    )
    grad_part = lax.dynamic_slice_in_dim(grad_in, tensor_member * width_part, width_part, 1).astype(
        jnp.bfloat16
    )
    back_out, back_grad = (
        lax.all_to_all(out_part, "dp", split_axis=0, concat_axis=0, tiled=True),
        lax.all_to_all(grad_part, "dp", split_axis=0, concat_axis=0, tiled=True),
    )
    layer_output = back_out[slot_of]
    input_grad = back_grad[slot_of]
    gradient_set = (
        first_gain_grad,
        query_grad,
        key_grad,
        value_grad,
        output_grad,
        gate_grad,
        up_grad,
        down_grad,
        second_gain_grad,
    )
    summed = (
        lax.psum_scatter(
            gradient_set[0].astype(jnp.bfloat16), "dp", scatter_dimension=0, tiled=True
        ).astype(jnp.float32),
        lax.psum_scatter(
            gradient_set[1].astype(jnp.bfloat16), "dp", scatter_dimension=0, tiled=True
        ).astype(jnp.float32),
        lax.psum_scatter(
            gradient_set[2].astype(jnp.bfloat16), "dp", scatter_dimension=0, tiled=True
        ).astype(jnp.float32),
        lax.psum_scatter(
            gradient_set[3].astype(jnp.bfloat16), "dp", scatter_dimension=0, tiled=True
        ).astype(jnp.float32),
        lax.psum_scatter(
            gradient_set[4].astype(jnp.bfloat16), "dp", scatter_dimension=1, tiled=True
        ).astype(jnp.float32),
        lax.psum_scatter(
            gradient_set[5].astype(jnp.bfloat16), "dp", scatter_dimension=0, tiled=True
        ).astype(jnp.float32),
        lax.psum_scatter(
            gradient_set[6].astype(jnp.bfloat16), "dp", scatter_dimension=0, tiled=True
        ).astype(jnp.float32),
        lax.psum_scatter(
            gradient_set[7].astype(jnp.bfloat16), "dp", scatter_dimension=1, tiled=True
        ).astype(jnp.float32),
        lax.psum_scatter(
            gradient_set[8].astype(jnp.bfloat16), "dp", scatter_dimension=0, tiled=True
        ).astype(jnp.float32),
    )
    return (
        layer_output,
        input_grad,
        summed[0],
        summed[1],
        summed[2],
        summed[3],
        summed[4],
        summed[8],
        summed[5],
        summed[6],
        summed[7],
    )


def solution(mesh):
    placed = (
        P(None, ("dp", "tensor")),
        P(None, ("dp", "tensor")),
        P(),
        P(None, "tensor"),
        P(None, "tensor"),
        P(None, "tensor"),
        P("tensor", None),
        P(),
        P(None, "tensor"),
        P(None, "tensor"),
        P("tensor", None),
        P(),
        P(),
        P(),
    )
    return jax.shard_map(
        per_device,
        mesh=mesh,
        in_specs=placed,
        out_specs=(
            P(None, ("dp", "tensor")),
            P(None, ("dp", "tensor")),
            P("dp"),
            P("dp", "tensor"),
            P("dp", "tensor"),
            P("dp", "tensor"),
            P("tensor", "dp"),
            P("dp"),
            P("dp", "tensor"),
            P("dp", "tensor"),
            P("tensor", "dp"),
        ),
        check_vma=False,
    )
```

profile of v0, /device:TPU:0, one launch (start us, length us, event | category | flops | bytes accessed | tf_op | source)
XLA Modules:
  0.0 1696.6 jit_solution(17351634925159057777)
XLA Ops:
  11.0 2.3 reduce-window.36
  13.8 4.3 scatter_custom_fusion
  18.2 5.4 gather_fusion
  23.6 20.4 %all_to_all.48 = bf16[8,128,512]{2,1,0:T(8,128)(2,1)} all-to-all(bf16[8,128,512]{2,1,0:T(8,128)(2,1)S(1)} %bitcast.200), channel_id=1, replica_groups=mesh['dp'=8,'tensor'=4] {'dp'}, dimensions={0} | all-to-all | bytes 2097152 | tf_op jit(solution)/shard_map/all_to_all | solution.py:99
  46.6 77.7 %all-gather.3.cloned.1.call-done = bf16[1024,2048]{1,0:T(8,128)(2,1)} async-done(((bf16[1024,512]{1,0:T(8,128)(2,1)}), bf16[1024,2048]{1,0:T(8,128)(2,1)}) %all-gather.3.cloned.1.call-update) | async-done | bytes 4194320 | tf_op jit(solution)/shard_map/all_gather | solution.py:103
  124.3 3.2 fusion.5
  132.4 2.4 fusion.76
  139.1 7.7 fusion.74
  146.8 8.0 fusion.3
  154.8 7.7 fusion.32
  163.4 5.6 fusion.77
  170.3 5.1 gather_fusion.2
  175.3 3.6 all-to-all-start.2
  179.0 15.4 all-to-all-done.2
  195.4 263.1 %all-reduce.8.cloned.1.call-done = f32[1024,2048]{1,0:T(8,128)} async-done(((f32[1024,2048]{1,0:T(8,128)}), f32[1024,2048]{1,0:T(8,128)}) %all-reduce.8.cloned.1.call-update) | async-done | bytes 8388624 | tf_op jit(solution)/shard_map/psum | solution.py:158
  458.5 6.0 multiply_reduce_fusion.2
  465.4 3.5 copy-done.2
  468.9 11.9 fusion.79
  480.9 8.5 fusion.78
  489.4 51.1 %all-gather.5.cloned.1.call-done = bf16[1024,2048]{1,0:T(8,128)(2,1)} async-done(((bf16[1024,512]{1,0:T(8,128)(2,1)}), bf16[1024,2048]{1,0:T(8,128)(2,1)}) %all-gather.5.cloned.1.call-update) | async-done | bytes 4194320 | tf_op jit(solution)/shard_map/all_gather | solution.py:104
  540.5 15.8 multiply_convert_fusion.2
  556.4 10.8 fusion.80
  567.2 10.9 convolution_add_fusion
  578.2 10.9 convolution_convert_fusion.3
  589.2 278.4 %all-reduce.12.cloned.1.call-done = f32[1024,2048]{1,0:T(8,128)} async-done(((f32[1024,2048]{1,0:T(8,128)}), f32[1024,2048]{1,0:T(8,128)}) %all-reduce.12.cloned.1.call-update) | async-done | bytes 8388624 | tf_op jit(solution)/shard_map/psum | solution.py:181
  867.6 7.2 multiply_reduce_fusion
  875.1 9.9 fusion.12
  885.0 6.7 convolution_convert_fusion.8
  891.8 7.5 fusion
  899.3 8.0 fusion.16
  913.2 7.0 fusion.57
  920.3 2.2 fusion.56
  922.5 5.7 fusion.61
  928.2 5.6 fusion.81
  933.8 3.1 fusion.44
  936.9 10.4 add_add_fusion
  947.4 10.8 convolution_convert_fusion
  958.2 11.2 convolution_convert_fusion.1
  969.5 11.1 convolution_convert_fusion.2
  980.6 4.4 convolution_convert_fusion.6
  985.1 4.3 convolution_convert_fusion.7
  989.5 7.2 convolution_convert_fusion.4
  997.0 5.9 convolution_convert_fusion.5
  1002.9 6.5 convert_element_type.201
  1009.4 14.4 all-reduce.10.cloned.1.call-done
  1023.9 3.1 fusion.28
  1027.0 3.7 all-to-all-start.1
  1030.7 285.5 %all-reduce.14.cloned.1.call-done = f32[1024,2048]{1,0:T(8,128)} async-done(((f32[1024,2048]{1,0:T(8,128)}), f32[1024,2048]{1,0:T(8,128)}) %all-reduce.14.cloned.1.call-update) | async-done | bytes 8388624 | tf_op jit(solution)/shard_map/psum | solution.py:223
  1316.2 6.1 fusion.10
  1322.4 3.9 fusion.26
  1326.3 3.6 all-to-all-start.3
  1331.2 5.1 gather_fusion.1
  1336.2 41.9 %reduce-scatter.20.cloned.1.call-done = bf16[1408,256]{1,0:T(8,128)(2,1)} async-done(((bf16[1408,2048]{1,0:T(8,128)(2,1)}), bf16[1408,256]{1,0:T(8,128)(2,1)}) %reduce-scatter.20.cloned.1.call-update) | async-done | bytes 720912 | tf_op jit(solution)/shard_map/reduce_scatter | solution.py:284
  1378.1 2.3 convert_element_type.256
  1380.5 60.2 %reduce-scatter.18.cloned.1.call-done = bf16[256,1408]{1,0:T(8,128)(2,1)} async-done(((bf16[2048,1408]{1,0:T(8,128)(2,1)}), bf16[256,1408]{1,0:T(8,128)(2,1)}) %reduce-scatter.18.cloned.1.call-update) | async-done | bytes 720912 | tf_op jit(solution)/shard_map/reduce_scatter | solution.py:281
  1440.7 2.3 convert_element_type.254
  1443.0 60.6 %reduce-scatter.16.cloned.1.call-done = bf16[256,1408]{1,0:T(8,128)(2,1)} async-done(((bf16[2048,1408]{1,0:T(8,128)(2,1)}), bf16[256,1408]{1,0:T(8,128)(2,1)}) %reduce-scatter.16.cloned.1.call-update) | async-done | bytes 720912 | tf_op jit(solution)/shard_map/reduce_scatter | solution.py:278
  1503.6 2.5 convert_element_type.252
  1506.0 35.2 %reduce-scatter.12.cloned.1.call-done = bf16[256,128]{1,0:T(8,128)(2,1)} async-done(((bf16[2048,128]{1,0:T(8,128)(2,1)}), bf16[256,128]{1,0:T(8,128)(2,1)}) %reduce-scatter.12.cloned.1.call-update) | async-done | bytes 65552 | tf_op jit(solution)/shard_map/reduce_scatter | solution.py:272
  1542.7 36.6 %reduce-scatter.10.cloned.1.call-done = bf16[256,128]{1,0:T(8,128)(2,1)} async-done(((bf16[2048,128]{1,0:T(8,128)(2,1)}), bf16[256,128]{1,0:T(8,128)(2,1)}) %reduce-scatter.10.cloned.1.call-update) | async-done | bytes 65552 | tf_op jit(solution)/shard_map/reduce_scatter | solution.py:269
  1580.9 42.9 %reduce-scatter.14.cloned.1.call-done = bf16[512,256]{1,0:T(8,128)(2,1)} async-done(((bf16[512,2048]{1,0:T(8,128)(2,1)}), bf16[512,256]{1,0:T(8,128)(2,1)}) %reduce-scatter.14.cloned.1.call-update) | async-done | bytes 262160 | tf_op jit(solution)/shard_map/reduce_scatter | solution.py:275
  1625.6 43.1 %reduce-scatter.8.cloned.1.call-done = bf16[256,512]{1,0:T(8,128)(2,1)} async-done(((bf16[2048,512]{1,0:T(8,128)(2,1)}), bf16[256,512]{1,0:T(8,128)(2,1)}) %reduce-scatter.8.cloned.1.call-update) | async-done | bytes 262160 | tf_op jit(solution)/shard_map/reduce_scatter | solution.py:266
  1670.5 13.0 all-reduce.2
  1684.7 5.1 gather_fusion.3
  (187 shorter events, 35.4 us)
Async XLA Ops:
  7.2 156.2 %copy-start = (bf16[512,2048]{1,0:T(8,128)(2,1)S(1)}, bf16[512,2048]{1,0:T(8,128)(2,1)}, u32[]{:S(2)}) copy-start(bf16[512,2048]{1,0:T(8,128)(2,1)} %param.20) | copy-start | bytes 6291460
  7.2 117.1 %all-gather.3.cloned.1.call-start = ((), (), s32[]{:S(2)}) async-start(), calls=%async_computation.11 | async-start | bytes 5242880 | tf_op jit(solution)/shard_map/all_gather | solution.py:103
  13.8 4.3 copy-start.33
  18.2 26.4 %copy-start.35 = (s32[32]{0:T(128)S(1)}, s32[32]{0:T(128)}, u32[]{:S(2)}) copy-start(s32[32]{0:T(128)} %param.27) | copy-start | bytes 388
  23.6 104.6 %copy-start.30 = (f32[2048]{0:T(1024)S(1)}, f32[2048]{0:T(1024)}, u32[]{:S(2)}) copy-start(f32[2048]{0:T(1024)} %param.16) | copy-start | bytes 24580
  44.0 414.5 %all-reduce.8.cloned.1.call-start = ((), (), s32[]{:S(2)}) async-start(), calls=%async_computation.12 | async-start | bytes 16777216 | tf_op jit(solution)/shard_map/psum | solution.py:158
  124.3 3.8 copy-start.3
  124.3 4.9 copy-start.23
  128.2 2.3 copy-start.28
  128.2 2.3 copy-start.21
  129.2 2.9 copy-start.10
  129.2 3.2 copy-start.36
  130.5 24.3 %copy-start.25 = (bf16[1024,128,1]{1,0,2:T(8,128)(2,1)}, bf16[1024,128,1]{1,0,2:T(8,128)(2,1)S(1)}, u32[]{:S(2)}) copy-start(bf16[1024,128,1]{1,0,2:T(8,128)(2,1)S(1)} %fusion.43) | copy-start | bytes 786436
  134.8 2.9 copy-start.6
  137.0 2.1 copy-start.11
  137.0 9.8 copy-start.18
  137.7 1.3 copy-start.8
  162.4 1.0 copy-start.38
  169.0 1.2 copy-start.5
  175.3 19.0 %all-to-all-start.2 = ((bf16[8,128,512]{2,1,0:T(8,128)(2,1)}), bf16[8,128,512]{2,1,0:T(8,128)(2,1)S(1)}, u32[]{:S(2)}, u32[]{:S(2)}) async-start(bf16[8,128,512]{2,1,0:T(8,128)(2,1)} %bitcast.199), calls=%async_computation.2 | async-start | bytes 2097152 | tf_op jit(solution)/shard_map/all_to_all | solution.py:100
  179.0 361.5 %all-gather.5.cloned.1.call-start = ((), (), s32[]{:S(2)}) async-start(), calls=%async_computation.14 | async-start | bytes 5242880 | tf_op jit(solution)/shard_map/all_gather | solution.py:104
  194.4 1.0 copy-start.17
  195.4 672.3 %all-reduce.12.cloned.1.call-start = ((), (), s32[]{:S(2)}) async-start(), calls=%async_computation.15 | async-start | bytes 16777216 | tf_op jit(solution)/shard_map/psum | solution.py:181
  195.4 269.1 %copy-start.27 = (f32[2048]{0:T(1024)S(1)}, f32[2048]{0:T(1024)}, u32[]{:S(2)}) copy-start(f32[2048]{0:T(1024)} %param.21) | copy-start | bytes 24580
  464.5 4.4 copy-start.2
  464.6 16.3 slice-start.4
  468.9 11.9 copy-start.15
  468.9 11.9 slice-start.5
  556.4 10.8 copy-start.42
  556.4 10.8 copy-start.41
  578.1 445.8 %all-reduce.10.cloned.1.call-start = ((), (), s32[]{:S(2)}) async-start(), calls=%async_computation.13 | async-start | bytes 8388608 | tf_op jit(solution)/shard_map/psum | solution.py:168
  589.2 727.1 %all-reduce.14.cloned.1.call-start = ((), (), s32[]{:S(2)}) async-start(), calls=%async_computation.16 | async-start | bytes 16777216 | tf_op jit(solution)/shard_map/psum | solution.py:223
  867.6 7.5 copy-start.16
  875.1 16.6 slice-start
  875.1 16.6 slice-start.1
  875.1 16.6 slice-start.2
  885.0 6.7 slice-start.3
  885.0 6.7 copy-start.26
  899.3 8.1 copy-start.14
  899.3 8.1 copy-start.19
  907.4 3.2 copy-start.4
  910.6 1.0 copy-start.12
  910.8 2.4 copy-start.7
  910.8 2.4 copy-start.9
  910.8 2.4 copy-start.20
  922.4 5.7 copy-start.22
  922.5 5.7 copy-start.37
  933.8 3.1 copy-start.24
  947.3 430.8 %reduce-scatter.20.cloned.1.call-start = ((), (), s32[]{:S(2)}) async-start(), calls=%async_computation.23 | async-start | bytes 6488064 | tf_op jit(solution)/shard_map/reduce_scatter | solution.py:284
  958.2 482.5 %reduce-scatter.18.cloned.1.call-start = ((), (), s32[]{:S(2)}) async-start(), calls=%async_computation.22 | async-start | bytes 6488064 | tf_op jit(solution)/shard_map/reduce_scatter | solution.py:281
  969.4 534.2 %reduce-scatter.16.cloned.1.call-start = ((), (), s32[]{:S(2)}) async-start(), calls=%async_computation.21 | async-start | bytes 6488064 | tf_op jit(solution)/shard_map/reduce_scatter | solution.py:278
  980.5 8.9 copy-start.39
  980.6 560.7 %reduce-scatter.12.cloned.1.call-start = ((), (), s32[]{:S(2)}) async-start(), calls=%async_computation.19 | async-start | bytes 589824 | tf_op jit(solution)/shard_map/reduce_scatter | solution.py:272
  985.0 594.4 %reduce-scatter.10.cloned.1.call-start = ((), (), s32[]{:S(2)}) async-start(), calls=%async_computation.18 | async-start | bytes 589824 | tf_op jit(solution)/shard_map/reduce_scatter | solution.py:269
  989.4 634.4 %reduce-scatter.14.cloned.1.call-start = ((), (), s32[]{:S(2)}) async-start(), calls=%async_computation.20 | async-start | bytes 2359296 | tf_op jit(solution)/shard_map/reduce_scatter | solution.py:275
  996.7 671.9 %reduce-scatter.8.cloned.1.call-start = ((), (), s32[]{:S(2)}) async-start(), calls=%async_computation.17 | async-start | bytes 2359296 | tf_op jit(solution)/shard_map/reduce_scatter | solution.py:266
  1009.4 306.8 %copy-start.29 = (f32[1024]{0:T(1024)S(1)}, f32[1024]{0:T(1024)}, u32[]{:S(2)}) copy-start(f32[1024]{0:T(1024)} %copy-done.28) | copy-start | bytes 12292
  1009.4 306.8 %copy-start.31 = (f32[2048]{0:T(1024)S(1)}, f32[2048]{0:T(1024)}, u32[]{:S(2)}) copy-start(f32[2048]{0:T(1024)} %param.16) | copy-start | bytes 24580
  1027.0 299.3 %all-to-all-start.1 = ((bf16[8,128,512]{2,1,0:T(8,128)(2,1)}), bf16[8,128,512]{2,1,0:T(8,128)(2,1)S(1)}, u32[]{:S(2)}, u32[]{:S(2)}) async-start(bf16[8,128,512]{2,1,0:T(8,128)(2,1)} %bitcast.27), calls=%async_computation.1 | async-start | bytes 2097152 | tf_op jit(solution)/shard_map/all_to_all | solution.py:246
  1030.7 291.7 %copy-start.32 = (f32[1024]{0:T(1024)S(1)}, f32[1024]{0:T(1024)}, u32[]{:S(2)}) copy-start(f32[1024]{0:T(1024)} %get-tuple-element.39) | copy-start | bytes 12292
  1322.3 7.5 copy-start.40
  1322.4 8.8 copy-start.34
  1326.3 358.4 %all-to-all-start.3 = ((bf16[8,128,512]{2,1,0:T(8,128)(2,1)}), bf16[8,128,512]{2,1,0:T(8,128)(2,1)S(1)}, u32[]{:S(2)}, u32[]{:S(2)}) async-start(bf16[8,128,512]{2,1,0:T(8,128)(2,1)} %bitcast.55), calls=%async_computation.3 | async-start | bytes 2097152 | tf_op jit(solution)/shard_map/all_to_all | solution.py:247
  1503.6 186.2 %copy-start.1 = (bf16[512,2048]{1,0:T(8,128)(2,1)S(1)}, bf16[512,2048]{1,0:T(8,128)(2,1)}, u32[]{:S(2)}) copy-start(bf16[512,2048]{1,0:T(8,128)(2,1)} %param.20) | copy-start | bytes 6291460
  (1 other events, 0.8 us)
Sparse Core Ops, SparseCore 0:
  44.2 80.1 all-gather.2
  169.2 289.3 all-reduce.7
  460.7 79.7 all-gather.4
  578.2 289.3 all-reduce.11
  869.8 153.9 all-reduce.9
  1026.3 289.8 all-reduce.13
  1320.0 58.0 reduce-scatter.19
  1381.6 59.0 reduce-scatter.17
  1444.5 59.0 reduce-scatter.15
  1507.1 34.1 reduce-scatter.11
  1545.2 34.1 reduce-scatter.9
  1582.5 41.2 reduce-scatter.13
  1627.4 41.2 reduce-scatter.7
where the time goes:
time: 1700 us
  waiting for transfers between devices  1310 us (77%)
  matrix products  197 us (12%)
  other arithmetic  94.1 us (6%)
  local copies, waits for them, and re-layouts  37.8 us (2%)
  blocking collectives  33.4 us (2%)
    psum x1, waiting for transfers between devices, per_device(): lax.psum(matmul(grad_query_low, query_weight.T) + matmul(grad_key_low, ke...  286 us
    psum x1, waiting for transfers between devices, per_device(): second_back = lax.psum(second_term, 'tensor')  278 us
    psum x1, waiting for transfers between devices, per_device(): attn_out = lax.psum(attn_term, 'tensor')  263 us
    dot_general x21, matrix products, matmul(): return jnp.dot(left, right, preferred_element_type=jnp.float32)  163 us
    all_gather x1, waiting for transfers between devices, per_device(): lax.all_gather(part_tokens, 'tensor', axis=1, tiled=True)  77.7 us
    reduce_scatter x1, waiting for transfers between devices, per_device(): lax.psum_scatter(gradient_set[5].astype(jnp.bfloat16), 'dp', scatter_dime...  60.6 us
    reduce_scatter x1, waiting for transfers between devices, per_device(): lax.psum_scatter(gradient_set[6].astype(jnp.bfloat16), 'dp', scatter_dime...  60.2 us
    all_gather x1, waiting for transfers between devices, per_device(): lax.all_gather(part_cotangent, 'tensor', axis=1, tiled=True)  51.1 us
  transfers between devices with their start and end apart: 16, of which 14 were waited for; matrix products, arithmetic and copies ran while one was open for 13% of the time, Pallas kernels for 0%

commit v1 on v0

--- a/solution.py
+++ b/solution.py
@@ -57,36 +57,34 @@
     per_owner = row_count // groups
     seq_count = seq_lengths.shape[0]
     seq_index = jnp.arange(seq_count, dtype=jnp.int32)
-    starts = jnp.cumsum(seq_lengths) - seq_lengths
+    before = (seq_index[None, :] < seq_index[:, None]).astype(jnp.int32)
+    unit_lengths = seq_lengths // groups
+    unit_starts = jnp.sum(before * unit_lengths[None, :], axis=1)
     placed = (owner_order[:, None] == seq_index[None, :]).astype(jnp.int32)
-    owner_lengths = jnp.sum(placed * seq_lengths[None, :], axis=1)
-    owner_before = jnp.cumsum(owner_lengths) - owner_lengths
-    owner_of = jnp.sum(placed * (owner_before // row_count)[:, None], axis=0)
-    global_row = jnp.arange(row_count, dtype=jnp.int32) * groups + member
-    inside = (
-        (global_row[:, None] >= starts[None, :])
-        & (global_row[:, None] < (starts + seq_lengths)[None, :])
+    order_lengths = jnp.sum(placed * unit_lengths[None, :], axis=1)
+    order_starts = jnp.sum(placed * unit_starts[None, :], axis=1)
+    order_keep = jnp.sum(placed * skip_mask[None, :], axis=1)
+    order_before = jnp.sum(before * order_lengths[None, :], axis=1)
+    places = jnp.arange(row_count, dtype=jnp.int32)
+    covers = (
+        (places[:, None] >= order_before[None, :])
+        & (places[:, None] < (order_before + order_lengths)[None, :])
     ).astype(jnp.int32)
-    row_owner = jnp.sum(inside * owner_of[None, :], axis=1)
-    owner_hot = (row_owner[:, None] == jnp.arange(groups, dtype=jnp.int32)[None, :]).astype(
-        jnp.int32
-    )
-    rank_in = jnp.sum((jnp.cumsum(owner_hot, axis=0) - 1) * owner_hot, axis=1)
-    slot_of = row_owner * per_owner + rank_in
-    send_rows = (
-        jnp.zeros((row_count,), jnp.int32).at[slot_of].set(jnp.arange(row_count, dtype=jnp.int32))
-    )
-    is_mine = (owner_of == member).astype(jnp.int32)
-    units_mine = seq_lengths // groups * is_mine
-    before_mine = jnp.cumsum(units_mine) - units_mine
-    places = jnp.arange(per_owner, dtype=jnp.int32)
-    covers = (
-        (places[:, None] >= before_mine[None, :])
-        & (places[:, None] < (before_mine + units_mine)[None, :])
+    send_rows = places + jnp.sum(covers * (order_starts - order_before)[None, :], axis=1)
+    given_before = jnp.sum(placed * order_before[:, None], axis=0)
+    given_covers = (
+        (places[:, None] >= unit_starts[None, :])
+        & (places[:, None] < (unit_starts + unit_lengths)[None, :])
     ).astype(jnp.int32)
-    slot_seq = jnp.sum(covers * seq_index[None, :], axis=1)
-    slot_step = places - jnp.sum(covers * before_mine[None, :], axis=1)
-    slot_keep = jnp.sum(covers * skip_mask[None, :], axis=1)
+    slot_of = places + jnp.sum(given_covers * (given_before - unit_starts)[None, :], axis=1)
+    my_places = member * per_owner + jnp.arange(per_owner, dtype=jnp.int32)
+    my_covers = (
+        (my_places[:, None] >= order_before[None, :])
+        & (my_places[:, None] < (order_before + order_lengths)[None, :])
+    ).astype(jnp.int32)
+    slot_seq = jnp.sum(my_covers * seq_index[None, :], axis=1)
+    slot_step = my_places - jnp.sum(my_covers * order_before[None, :], axis=1)
+    slot_keep = jnp.sum(my_covers * order_keep[None, :], axis=1)
     sources = jnp.arange(groups, dtype=jnp.int32)
     token_positions = (sources[:, None] + groups * slot_step[None, :]).reshape(row_count)
     sequence_id = jnp.broadcast_to(slot_seq[None, :], (groups, per_owner)).reshape(row_count)
@@ -109,6 +107,16 @@
     score_scale = 1.0 / math.sqrt(HEAD_WIDTH)
     tensor_member = lax.axis_index("tensor")
     inputs = owned_tokens.astype(jnp.float32)
+
+    def all_sum(values):
+        part = lax.psum_scatter(
+            values.astype(jnp.bfloat16), "tensor", scatter_dimension=1, tiled=True
+        )
+        return lax.all_gather(part, "tensor", axis=1, tiled=True).astype(jnp.float32)
+
+    def my_part(values):
+        return lax.dynamic_slice_in_dim(values, tensor_member * width_part, width_part, 1)
+
     scale_one = lax.rsqrt(jnp.mean(inputs * inputs, axis=1, keepdims=True) + eps)
     normed_one = (inputs * scale_one * first_gain).astype(jnp.bfloat16)
     query_pre = matmul(normed_one, query_weight)
@@ -155,7 +163,7 @@
     )
     attended_low = attended_rows.reshape(row_count, local_heads * HEAD_WIDTH).astype(jnp.bfloat16)
     attn_term = matmul(attended_low, output_weight)
-    attn_out = lax.psum(attn_term, "tensor")
+    attn_out = all_sum(attn_term)
     hidden_res = inputs + keep_rows * attn_out
     scale_two = lax.rsqrt(jnp.mean(hidden_res * hidden_res, axis=1, keepdims=True) + eps)
     normed_two = (hidden_res * scale_two * second_gain).astype(jnp.bfloat16)
@@ -165,8 +173,10 @@
     silu_val = gate * gate_sig
     inner_low = (silu_val * upward).astype(jnp.bfloat16)
     ffn_term = matmul(inner_low, down_weight)
-    ffn_out = lax.psum(ffn_term.astype(jnp.bfloat16), "tensor").astype(jnp.float32)
-    result = hidden_res + keep_rows * ffn_out
+    ffn_out = lax.psum_scatter(
+        ffn_term.astype(jnp.bfloat16), "tensor", scatter_dimension=1, tiled=True
+    ).astype(jnp.float32)
+    result = my_part(hidden_res) + keep_rows * ffn_out
     grad_out = owned_cotangent.astype(jnp.float32)
     grad_ffn = (keep_rows * grad_out).astype(jnp.bfloat16)
     grad_inner = matmul(grad_ffn, down_weight.T)
@@ -178,7 +188,7 @@
     second_term = matmul(grad_gate, gate_weight.T) + matmul(grad_up, up_weight.T)
     gate_grad = matmul(normed_two.T, grad_gate)
     up_grad = matmul(normed_two.T, grad_up)
-    second_back = lax.psum(second_term, "tensor")
+    second_back = all_sum(second_term)
     second_gain_grad = jnp.sum(second_back * hidden_res * scale_two, axis=0)
     scaled_two = second_back * second_gain
     grad_res = (
@@ -220,28 +230,27 @@
     )
     grad_key_low = unrotate(grad_key).reshape(row_count, local_kv * HEAD_WIDTH).astype(jnp.bfloat16)
     grad_value_low = grad_value.reshape(row_count, local_kv * HEAD_WIDTH).astype(jnp.bfloat16)
-    first_back = lax.psum(
-        matmul(grad_query_low, query_weight.T)
+    first_back = lax.psum_scatter(
+        (matmul(grad_query_low, query_weight.T)
         + matmul(grad_key_low, key_matrix.T)
-        + matmul(grad_value_low, value_matrix.T),
+        + matmul(grad_value_low, value_matrix.T)).astype(jnp.bfloat16),
         "tensor",
-    )
+        scatter_dimension=1,
+        tiled=True,
+    ).astype(jnp.float32)
     query_grad = matmul(normed_one.T, grad_query_low)
     key_grad = matmul(normed_one.T, grad_key_low)
     value_grad = matmul(normed_one.T, grad_value_low)
-    first_gain_grad = jnp.sum(first_back * inputs * scale_one, axis=0)
-    scaled_one = first_back * first_gain
-    grad_in = (
-        grad_res
-        + scale_one * scaled_one
-        - inputs * scale_one**3 * jnp.mean(scaled_one * inputs, axis=1, keepdims=True)
-    )
-    out_part = lax.dynamic_slice_in_dim(result, tensor_member * width_part, width_part, 1).astype(
-        jnp.bfloat16
-    )
-    grad_part = lax.dynamic_slice_in_dim(grad_in, tensor_member * width_part, width_part, 1).astype(
-        jnp.bfloat16
-    )
+    my_inputs = my_part(inputs)
+    first_gain_part = jnp.sum(first_back * my_inputs * scale_one, axis=0)
+    scaled_one = first_back * lax.dynamic_slice_in_dim(
+        first_gain, tensor_member * width_part, width_part, 0
+    )
+    along = lax.psum(jnp.sum(scaled_one * my_inputs, axis=1, keepdims=True), "tensor") / inputs.shape[1]
+    grad_in = my_part(grad_res) + scale_one * scaled_one - my_inputs * scale_one**3 * along
+    out_part = result.astype(jnp.bfloat16)
+    grad_part = grad_in.astype(jnp.bfloat16)
+    first_gain_grad = lax.all_gather(first_gain_part, "tensor", axis=0, tiled=True)
     back_out, back_grad = (
         lax.all_to_all(out_part, "dp", split_axis=0, concat_axis=0, tiled=True),
         lax.all_to_all(grad_part, "dp", split_axis=0, concat_axis=0, tiled=True),
@@ -259,34 +268,24 @@
         down_grad,
         second_gain_grad,
     )
+    by_width = [gradient_set[k] for k in (1, 2, 3, 5, 6)] + [gradient_set[k].T for k in (4, 7)]
+    gains = jnp.stack([first_gain_grad, second_gain_grad], axis=1)
+    joined = jnp.concatenate([g.astype(jnp.bfloat16) for g in by_width] + [gains.astype(jnp.bfloat16)], axis=1)
+    shared = lax.psum_scatter(joined, "dp", scatter_dimension=0, tiled=True).astype(jnp.float32)
+    cuts, at = [], 0
+    for g in by_width:
+        cuts.append(shared[:, at : at + g.shape[1]])
+        at += g.shape[1]
     summed = (
-        lax.psum_scatter(
-            gradient_set[0].astype(jnp.bfloat16), "dp", scatter_dimension=0, tiled=True
-        ).astype(jnp.float32),
-        lax.psum_scatter(
-            gradient_set[1].astype(jnp.bfloat16), "dp", scatter_dimension=0, tiled=True
-        ).astype(jnp.float32),
-        lax.psum_scatter(
-            gradient_set[2].astype(jnp.bfloat16), "dp", scatter_dimension=0, tiled=True
-        ).astype(jnp.float32),
-        lax.psum_scatter(
-            gradient_set[3].astype(jnp.bfloat16), "dp", scatter_dimension=0, tiled=True
-        ).astype(jnp.float32),
-        lax.psum_scatter(
-            gradient_set[4].astype(jnp.bfloat16), "dp", scatter_dimension=1, tiled=True
-        ).astype(jnp.float32),
-        lax.psum_scatter(
-            gradient_set[5].astype(jnp.bfloat16), "dp", scatter_dimension=0, tiled=True
-        ).astype(jnp.float32),
-        lax.psum_scatter(
-            gradient_set[6].astype(jnp.bfloat16), "dp", scatter_dimension=0, tiled=True
-        ).astype(jnp.float32),
-        lax.psum_scatter(
-            gradient_set[7].astype(jnp.bfloat16), "dp", scatter_dimension=1, tiled=True
-        ).astype(jnp.float32),
-        lax.psum_scatter(
-            gradient_set[8].astype(jnp.bfloat16), "dp", scatter_dimension=0, tiled=True
-        ).astype(jnp.float32),
+        shared[:, at],
+        cuts[0],
+        cuts[1],
+        cuts[2],
+        cuts[5].T,
+        cuts[3],
+        cuts[4],
+        cuts[6].T,
+        shared[:, at + 1],
     )
     return (
         layer_output,

time: 1700 us -> 1060 us (0.62)
  waiting for transfers between devices: 1310 us -> 593 us
  local copies, waits for them, and re-layouts: 37.8 us -> 142 us
  matrix products: 197 us -> 158 us
  blocking collectives: 33.4 us -> 61.9 us
  other arithmetic: 94.1 us -> 73.8 us
    psum x4 -> x0, waiting for transfers between devices: 841 us -> none  [the longest x1 286 us: per_device(): lax.psum(matmul(grad_query_low, query_weight.T) + matmul(grad_key_low, ke...]
    all_gather x0 -> x2, waiting for transfers between devices: none -> 141 us  [all_sum(): lax.all_gather(part, 'tensor', axis=1, tiled=True).astype(jnp.float32)]
    concatenate x0 -> x1, local copies, waits for them, and re-layouts: none -> 95 us  [per_device(): jnp.concatenate([g.astype(jnp.bfloat16) for g in by_width] + [gains.astyp...]
    dot_general x21, matrix products: 163 us -> 127 us  [matmul(): return jnp.dot(left, right, preferred_element_type=jnp.float32)]
    all_to_all x0 -> x1, blocking collectives: none -> 19.6 us  [per_device(): lax.all_to_all(cotangent[send_rows], 'dp', split_axis=0, concat_axis=0, t...]
    reduce_scatter x7 -> x5, waiting for transfers between devices: 321 us -> 312 us  [the longest x2 151 us: all_sum(): lax.psum_scatter(values.astype(jnp.bfloat16), 'tensor', scatter_dimension...]
  transfers between devices with their start and end apart: 16 -> 11, of which waited for: 14 -> 10; matrix products, arithmetic and copies ran while one was open for 13% -> 19% of each run, Pallas kernels for 0% -> 0%
where the time goes in v1:
time: 1060 us; the launch traced here: 1050 us
  waiting for transfers between devices  593 us (56%)
  matrix products  158 us (15%)
  local copies, waits for them, and re-layouts  142 us (13%)
  other arithmetic  73.8 us (7%)
  blocking collectives  61.9 us (6%)
  between operations  15 us (1%)
    reduce_scatter x2, waiting for transfers between devices, all_sum(): lax.psum_scatter(values.astype(jnp.bfloat16), 'tensor', scatter_dimension...  151 us
    all_gather x2, waiting for transfers between devices, all_sum(): lax.all_gather(part, 'tensor', axis=1, tiled=True).astype(jnp.float32)  141 us
    reduce_scatter x1, waiting for transfers between devices, per_device(): lax.psum_scatter(joined, 'dp', scatter_dimension=0, tiled=True)  139 us
    dot_general x21, matrix products, matmul(): return jnp.dot(left, right, preferred_element_type=jnp.float32)  127 us
    concatenate x1, local copies, waits for them, and re-layouts, per_device(): jnp.concatenate([g.astype(jnp.bfloat16) for g in by_width] + [gains.astyp...  95 us
    all_gather x1, waiting for transfers between devices, per_device(): lax.all_gather(part_tokens, 'tensor', axis=1, tiled=True)  78.1 us
    all_gather x1, waiting for transfers between devices, per_device(): lax.all_gather(part_cotangent, 'tensor', axis=1, tiled=True)  51.1 us
    reduce_scatter x1, waiting for transfers between devices, per_device(): lax.psum_scatter((matmul(grad_query_low, query_weight.T) + matmul(grad_ke...  22.4 us
  transfers between devices with their start and end apart: 11, of which 10 were waited for; matrix products, arithmetic and copies ran while one was open for 19% of the time, Pallas kernels for 0%

profile of v1, /device:TPU:0, one launch (start us, length us, event | category | flops | bytes accessed | tf_op | source)
XLA Modules:
  0.0 1052.1 jit_solution(1160948737653253536)
XLA Ops:
  11.2 5.4 gather_fusion
  16.6 20.4 %all_to_all.48 = bf16[8,128,512]{2,1,0:T(8,128)(2,1)} all-to-all(bf16[8,128,512]{2,1,0:T(8,128)(2,1)S(1)} %bitcast.195), channel_id=1, replica_groups=mesh['dp'=8,'tensor'=4] {'dp'}, dimensions={0} | all-to-all | bytes 2097152 | tf_op jit(solution)/shard_map/all_to_all | solution.py:97
  39.2 78.1 %all-gather.6.cloned.1.call-done = bf16[1024,2048]{1,0:T(8,128)(2,1)} async-done(((bf16[1024,512]{1,0:T(8,128)(2,1)}), bf16[1024,2048]{1,0:T(8,128)(2,1)}) %all-gather.6.cloned.1.call-update) | async-done | bytes 4194320 | tf_op jit(solution)/shard_map/all_gather | solution.py:101
  117.3 3.2 multiply_reduce_fusion.1
  122.2 1.2 fusion.46
  123.6 1.5 fusion.78
  125.5 2.4 fusion.79
  128.1 2.0 fusion.52
  132.2 7.7 fusion.77
  139.9 8.0 fusion.3
  147.9 7.6 fusion.35
  156.5 4.4 convolution_convert_fusion.4
  160.9 75.4 %reduce-scatter.6.cloned.1.call-done = bf16[1024,512]{1,0:T(8,128)(2,1)} async-done(((bf16[1024,2048]{1,0:T(8,128)(2,1)}), bf16[1024,512]{1,0:T(8,128)(2,1)}) %reduce-scatter.6.cloned.1.call-update) | async-done | bytes 1048592 | tf_op jit(solution)/shard_map/reduce_scatter | solution.py:112
  236.4 5.1 gather_fusion.2
  241.5 19.6 %all_to_all.49 = bf16[8,128,512]{2,1,0:T(8,128)(2,1)} all-to-all(bf16[8,128,512]{2,1,0:T(8,128)(2,1)} %bitcast.194), channel_id=1, replica_groups=mesh['dp'=8,'tensor'=4] {'dp'}, dimensions={0} | all-to-all | bytes 2097152 | tf_op jit(solution)/shard_map/all_to_all | solution.py:98
  261.2 58.1 %all-gather.8.cloned.1.call-done = bf16[1024,2048]{1,0:T(8,128)(2,1)} async-done(((bf16[1024,512]{1,0:T(8,128)(2,1)}), bf16[1024,2048]{1,0:T(8,128)(2,1)}) %all-gather.8.cloned.1.call-update) | async-done | bytes 4194320 | tf_op jit(solution)/shard_map/all_gather | solution.py:115
  319.3 4.9 multiply_reduce_fusion
  325.0 3.5 copy-done.2
  328.6 12.0 %fusion.80 = f32[1024,1408]{1,0:T(8,128)} fusion(bf16[1024,2048]{1,0:T(8,128)(2,1)S(1)} %multiply_convert_fusion.1, bf16[2048,1408]{1,0:T(8,128)(2,1)} %param.22), kind=kOutput, calls=%fused_computation.168 | convolution fusion | flops 5905580032 | bytes 15728640 | tf_op jit(solution)/shard_map/dot_general | solution.py:34
  340.5 8.5 fusion.81
  349.0 51.1 %all-gather.10.cloned.1.call-done = bf16[1024,2048]{1,0:T(8,128)(2,1)} async-done(((bf16[1024,512]{1,0:T(8,128)(2,1)}), bf16[1024,2048]{1,0:T(8,128)(2,1)}) %all-gather.10.cloned.1.call-update) | async-done | bytes 4194320 | tf_op jit(solution)/shard_map/all_gather | solution.py:102
  400.1 15.9 %multiply_convert_fusion.3 = (bf16[1024,1408]{1,0:T(8,128)(2,1)S(1)}, bf16[1024,1408]{1,0:T(8,128)(2,1)S(1)}, bf16[1024,1408]{1,0:T(8,128)(2,1)}) fusion(f32[1024,1408]{1,0:T(8,128)} %fusion.80, f32[1024,1408]{1,0:T(8,128)} %fusion.81, bf16[1408,2048]{1,0:T(8,128)(2,1)} %param.24, bf16[1024,2048]{1,0:T(8,128)(2,1)} %all-gather.10.cloned.1.call-done, ...), kind=kOutput, calls=%fused_computation.43 | convolution fusion | flops 5933498368 | bytes 30150656 | tf_op jit(solution)/shard_map/dot_general | solution.py:34
  416.0 10.8 %fusion.82 = f32[1024,2048]{1,0:T(8,128)S(1)} fusion(bf16[1024,1408]{1,0:T(8,128)(2,1)S(1)} %get-tuple-element.70, bf16[2048,1408]{1,0:T(8,128)(2,1)} %param.22), kind=kOutput, calls=%fused_computation.170 | convolution fusion | flops 5905580032 | bytes 17039360 | tf_op jit(solution)/shard_map/dot_general | solution.py:34
  426.8 11.0 %add_convert_fusion.1 = bf16[1024,2048]{1,0:T(8,128)(2,1)} fusion(f32[1024,2048]{1,0:T(8,128)S(1)} %fusion.82, bf16[1024,1408]{1,0:T(8,128)(2,1)S(1)} %get-tuple-element.69, bf16[2048,1408]{1,0:T(8,128)(2,1)} %param.23), kind=kOutput, calls=%fused_computation.34 | convolution fusion | flops 5909774336 | bytes 21233664 | tf_op jit(solution)/shard_map/dot_general | solution.py:34
  437.9 75.4 %reduce-scatter.10.cloned.1.call-done = bf16[1024,512]{1,0:T(8,128)(2,1)} async-done(((bf16[1024,2048]{1,0:T(8,128)(2,1)}), bf16[1024,512]{1,0:T(8,128)(2,1)}) %reduce-scatter.10.cloned.1.call-update) | async-done | bytes 1048592 | tf_op jit(solution)/shard_map/reduce_scatter | solution.py:112
  513.4 82.6 %all-gather.12.cloned.1.call-done = bf16[1024,2048]{1,0:T(8,128)(2,1)} async-done(((bf16[1024,512]{1,0:T(8,128)(2,1)}), bf16[1024,2048]{1,0:T(8,128)(2,1)}) %all-gather.12.cloned.1.call-update) | async-done | bytes 4194320 | tf_op jit(solution)/shard_map/all_gather | solution.py:115
  596.0 7.1 fusion.11
  603.1 7.8 fusion.9
  610.9 6.7 convolution_convert_fusion.9
  617.6 7.5 fusion
  625.1 3.1 fusion.47
  628.2 8.4 fusion.15
  636.6 1.4 bitcast_multiply_fusion.3
  638.1 1.8 copy-done.3
  641.8 2.4 fusion.83
  646.0 4.4 fusion.60
  650.5 1.8 fusion.59
  652.3 1.3 fusion.64
  653.6 3.5 add_convert_fusion
  657.2 11.1 %convolution_convert_fusion.3 = bf16[1024,2048]{1,0:T(8,128)(2,1)} fusion(bf16[1024,1408]{1,0:T(8,128)(2,1)} %get-tuple-element.71, bf16[1408,2048]{1,0:T(8,128)(2,1)} %param.24), kind=kOutput, calls=%fused_computation.49 | convolution fusion | flops 5907677184 | bytes 12845056 | tf_op jit(solution)/shard_map/dot_general | solution.py:34
  669.1 6.8 convert_element_type.185
  675.9 8.2 convolution_convert_fusion.2
  684.1 8.2 convolution_convert_fusion.1
  692.3 8.7 convolution_convert_fusion
  702.6 3.7 convolution_convert_fusion.6
  706.3 3.9 convolution_convert_fusion.5
  710.2 22.4 %reduce-scatter.12.cloned.1.call-done = bf16[1024,512]{1,0:T(8,128)(2,1)} async-done(((bf16[1024,2048]{1,0:T(8,128)(2,1)}), bf16[1024,512]{1,0:T(8,128)(2,1)}) %reduce-scatter.12.cloned.1.call-update) | async-done | bytes 1048592 | tf_op jit(solution)/shard_map/reduce_scatter | solution.py:233
  732.6 2.7 fusion.27
  735.3 12.6 %all-gather = bf16[4,1,512]{2,1,0:T(2,128)(2,1)S(1)} all-gather(bf16[1,1,512]{2,1,0:T(2,128)(2,1)S(1)} %convert.16), channel_id=1, replica_groups=mesh['dp'=8,'tensor'=4] {'tensor'}, dimensions={0}, use_global_device_ids=true | all-gather | bytes 5120 | tf_op jit(solution)/shard_map/all_gather | solution.py:253
  747.9 95.0 %concatenate.59 = bf16[2048,5506]{0,1:T(8,128)(2,1)} concatenate(bf16[2048,512]{0,1:T(8,128)(2,1)} %convolution_convert_fusion.6, bf16[2048,128]{0,1:T(8,128)(2,1)S(1)} %convolution_convert_fusion.8, bf16[2048,128]{0,1:T(8,128)(2,1)S(1)} %convolution_convert_fusion.7, bf16[2048,1408]{0,1:T(8,128)(2,1)} %convolution_convert_fusion.2, ...), dimensions={1} | concatenate | bytes 45105152 | tf_op jit(solution)/shard_map/concatenate | solution.py:273
  843.0 3.3 add_convert_fusion.3
  846.2 3.6 all-to-all-start.1
  849.9 9.3 psum.7
  859.2 5.0 fusion.24
  865.3 3.6 all-to-all-start.3
  869.0 5.1 gather_fusion.1
  874.1 10.1 all-to-all-done.3
  884.2 5.1 gather_fusion.3
  889.3 138.9 %reduce-scatter.14.cloned.1.call-done = bf16[256,5506]{0,1:T(8,128)(2,1)} async-done(((bf16[2048,5506]{0,1:T(8,128)(2,1)}), bf16[256,5506]{0,1:T(8,128)(2,1)}) %reduce-scatter.14.cloned.1.call-update) | async-done | bytes 2819088 | tf_op jit(solution)/shard_map/reduce_scatter | solution.py:274
  1028.2 2.2 convert_element_type.236
  1036.8 2.8 fusion.70
  1039.6 2.9 copy.75
  1042.5 1.5 copy.76
  1044.1 1.3 fusion.71
  (192 shorter events, 26.3 us)
Async XLA Ops:
  7.2 149.3 %copy-start = (bf16[512,2048]{1,0:T(8,128)(2,1)S(1)}, bf16[512,2048]{1,0:T(8,128)(2,1)}, u32[]{:S(2)}) copy-start(bf16[512,2048]{1,0:T(8,128)(2,1)} %param.20) | copy-start | bytes 6291460
  7.2 110.1 %all-gather.6.cloned.1.call-start = ((), (), s32[]{:S(2)}) async-start(), calls=%async_computation.9 | async-start | bytes 5242880 | tf_op jit(solution)/shard_map/all_gather | solution.py:101
  8.9 2.2 copy-start.38
  16.6 104.6 %copy-start.37 = (f32[2048]{0:T(1024)S(1)}, f32[2048]{0:T(1024)}, u32[]{:S(2)}) copy-start(f32[2048]{0:T(1024)} %param.16) | copy-start | bytes 24580
  37.0 199.3 %reduce-scatter.6.cloned.1.call-start = ((), (), s32[]{:S(2)}) async-start(), calls=%async_computation.10 | async-start | bytes 5242880 | tf_op jit(solution)/shard_map/reduce_scatter | solution.py:112
  117.3 3.8 copy-start.6
  122.2 3.0 copy-start.4
  122.2 1.4 copy-start.25
  123.6 24.2 %copy-start.31 = (bf16[1024,128,1]{1,0,2:T(8,128)(2,1)}, bf16[1024,128,1]{1,0,2:T(8,128)(2,1)S(1)}, u32[]{:S(2)}) copy-start(bf16[1024,128,1]{1,0,2:T(8,128)(2,1)S(1)} %fusion.46) | copy-start | bytes 786436
  123.6 1.8 copy-start.42
  127.9 2.9 copy-start.8
  130.1 2.1 copy-start.22
  160.9 75.5 %copy-start.7 = (bf16[1024,512]{1,0:T(8,128)(2,1)S(1)}, bf16[1024,512]{1,0:T(8,128)(2,1)}, u32[]{:S(2)}) copy-start(bf16[1024,512]{1,0:T(8,128)(2,1)} %param.15) | copy-start | bytes 3145732
  160.9 158.4 %all-gather.8.cloned.1.call-start = ((), (), s32[]{:S(2)}) async-start(), calls=%async_computation.11 | async-start | bytes 5242880 | tf_op jit(solution)/shard_map/all_gather | solution.py:115
  236.3 163.8 %all-gather.10.cloned.1.call-start = ((), (), s32[]{:S(2)}) async-start(), calls=%async_computation.13 | async-start | bytes 5242880 | tf_op jit(solution)/shard_map/all_gather | solution.py:102
  261.1 252.2 %reduce-scatter.10.cloned.1.call-start = ((), (), s32[]{:S(2)}) async-start(), calls=%async_computation.14 | async-start | bytes 5242880 | tf_op jit(solution)/shard_map/reduce_scatter | solution.py:112
  261.2 63.0 %copy-start.33 = (f32[2048]{0:T(1024)S(1)}, f32[2048]{0:T(1024)}, u32[]{:S(2)}) copy-start(f32[2048]{0:T(1024)} %param.21) | copy-start | bytes 24580
  324.2 4.4 copy-start.2
  324.2 16.3 %slice-start.8 = ((s8[5767168]{0:T(1024)(128)(4,1)}), s8[4194304]{0:T(1024)(128)(4,1)S(1)}, s32[]{:S(2)}) async-start(s8[5767168]{0:T(1024)(128)(4,1)} %bitcast.208), calls=%async_computation.26 | async-start | bytes 8388608
  328.6 12.0 %copy-start.17 = (bf16[1024,2048]{1,0:T(8,128)(2,1)}, bf16[1024,2048]{1,0:T(8,128)(2,1)S(1)}, u32[]{:S(2)}) copy-start(bf16[1024,2048]{1,0:T(8,128)(2,1)S(1)} %multiply_convert_fusion.1) | copy-start | bytes 12582916
  328.6 12.0 %slice-start.9 = ((s8[5767168]{0:T(1024)(128)(4,1)}), s8[1572864]{0:T(1024)(128)(4,1)S(1)}, s32[]{:S(2)}) async-start(s8[5767168]{0:T(1024)(128)(4,1)} %bitcast.208), calls=%async_computation.27 | async-start | bytes 3145728
  416.0 10.8 %copy-start.47 = (bf16[1024,1408]{1,0:T(8,128)(2,1)}, bf16[1024,1408]{1,0:T(8,128)(2,1)S(1)}, u32[]{:S(2)}) copy-start(bf16[1024,1408]{1,0:T(8,128)(2,1)S(1)} %get-tuple-element.70) | copy-start | bytes 8650756
  416.0 10.8 %copy-start.49 = (bf16[1024,1408]{1,0:T(8,128)(2,1)}, bf16[1024,1408]{1,0:T(8,128)(2,1)S(1)}, u32[]{:S(2)}) copy-start(bf16[1024,1408]{1,0:T(8,128)(2,1)S(1)} %get-tuple-element.69) | copy-start | bytes 8650756
  437.8 158.2 %all-gather.12.cloned.1.call-start = ((), (), s32[]{:S(2)}) async-start(), calls=%async_computation.15 | async-start | bytes 5242880 | tf_op jit(solution)/shard_map/all_gather | solution.py:115
  513.3 219.2 %reduce-scatter.12.cloned.1.call-start = ((), (), s32[]{:S(2)}) async-start(), calls=%async_computation.16 | async-start | bytes 5242880 | tf_op jit(solution)/shard_map/reduce_scatter | solution.py:233
  596.0 7.1 copy-start.12
  596.0 7.1 copy-start.19
  603.1 14.4 %slice-start = ((s8[16777216]{0:T(1024)(128)(4,1)}), s8[4194304]{0:T(1024)(128)(4,1)S(1)}, s32[]{:S(2)}) async-start(s8[16777216]{0:T(1024)(128)(4,1)} %bitcast.180), calls=%async_computation.18 | async-start | bytes 8388608
  603.1 14.4 %slice-start.1 = ((s8[16777216]{0:T(1024)(128)(4,1)}), s8[4194304]{0:T(1024)(128)(4,1)S(1)}, s32[]{:S(2)}) async-start(s8[16777216]{0:T(1024)(128)(4,1)} %bitcast.180), calls=%async_computation.19 | async-start | bytes 8388608
  603.1 14.5 %slice-start.2 = ((s8[16777216]{0:T(1024)(128)(4,1)}), s8[4194304]{0:T(1024)(128)(4,1)S(1)}, s32[]{:S(2)}) async-start(s8[16777216]{0:T(1024)(128)(4,1)} %bitcast.180), calls=%async_computation.20 | async-start | bytes 8388608
  610.9 6.7 slice-start.3
  610.9 6.7 copy-start.32
  628.2 8.4 copy-start.16
  628.2 8.4 copy-start.23
  636.6 3.3 copy-start.3
  640.2 1.6 copy-start.43
  641.0 3.3 slice-start.4
  641.8 2.4 copy-start.27
  641.8 3.0 slice-start.5
  641.8 3.6 copy-start.9
  641.8 4.2 copy-start.11
  641.8 4.2 copy-start.24
  646.0 6.2 copy-start.26
  657.1 185.8 %reduce-scatter.8.cloned.1.call-start = ((), (), s32[]{:S(2)}) async-start(), calls=%async_computation.12 | async-start | bytes 5242880 | tf_op jit(solution)/shard_map/reduce_scatter | solution.py:176
  668.3 359.9 %reduce-scatter.14.cloned.1.call-start = ((), (), s32[]{:S(2)}) async-start(), calls=%async_computation.17 | async-start | bytes 25399296 | tf_op jit(solution)/shard_map/reduce_scatter | solution.py:274
  669.1 6.8 copy-start.18
  669.1 6.8 copy-start.48
  675.9 8.2 copy-start.50
  684.1 8.2 copy-start.20
  684.1 8.2 copy-start.46
  692.3 8.7 copy-start.5
  701.0 1.5 copy-start.28
  701.8 4.5 slice-start.6
  702.6 3.7 slice-start.7
  702.6 3.7 copy-start.45
  706.3 26.3 %copy-start.35 = (f32[1024]{0:T(1024)S(1)}, f32[1024]{0:T(1024)}, u32[]{:S(2)}) copy-start(f32[1024]{0:T(1024)} %copy-done.34) | copy-start | bytes 12292
  842.9 16.3 %copy-start.21 = (bf16[1024,512]{1,0:T(8,128)(2,1)S(1)}, bf16[1024,512]{1,0:T(8,128)(2,1)}, u32[]{:S(2)}) copy-start(bf16[1024,512]{1,0:T(8,128)(2,1)} %reduce-scatter.12.cloned.1.call-done) | copy-start | bytes 3145732
  842.9 16.3 %copy-start.36 = (f32[1024]{0:T(1024)S(1)}, f32[1024]{0:T(1024)}, u32[]{:S(2)}) copy-start(f32[1024]{0:T(1024)} %get-tuple-element.91) | copy-start | bytes 12292
  846.2 19.0 %all-to-all-start.1 = ((bf16[8,128,512]{2,1,0:T(8,128)(2,1)}), bf16[8,128,512]{2,1,0:T(8,128)(2,1)S(1)}, u32[]{:S(2)}, u32[]{:S(2)}) async-start(bf16[8,128,512]{2,1,0:T(8,128)(2,1)} %bitcast.22), calls=%async_computation.3 | async-start | bytes 2097152 | tf_op jit(solution)/shard_map/all_to_all | solution.py:255
  859.2 9.6 copy-start.39
  859.2 9.6 copy-start.40
  859.2 9.6 copy-start.41
  865.3 18.9 %all-to-all-start.3 = ((bf16[8,128,512]{2,1,0:T(8,128)(2,1)}), bf16[8,128,512]{2,1,0:T(8,128)(2,1)S(1)}, u32[]{:S(2)}, u32[]{:S(2)}) async-start(bf16[8,128,512]{2,1,0:T(8,128)(2,1)} %bitcast.54), calls=%async_computation.7 | async-start | bytes 2097152 | tf_op jit(solution)/shard_map/all_to_all | solution.py:256
  1036.8 8.5 copy-start.1
  (8 other events, 8.9 us)
Sparse Core Ops, SparseCore 0:
  37.1 80.1 all-gather.5
  161.0 75.2 reduce-scatter.5
  238.0 81.2 all-gather.7
  320.8 79.2 all-gather.9
  438.0 75.2 reduce-scatter.9
  514.7 81.2 all-gather.11
  657.2 75.2 reduce-scatter.11
  735.0 77.3 reduce-scatter.7
  843.0 185.0 reduce-scatter.13

commit v2 on v1

--- a/solution.py
+++ b/solution.py
@@ -1,11 +1,162 @@
+import functools
 import math
 
 import jax
 import jax.numpy as jnp
 from jax import lax
+from jax.experimental import pallas as pl
+from jax.experimental.pallas import tpu as pltpu
 from jax.sharding import PartitionSpec as P
 
 HEAD_WIDTH = 128
+
+MESH = pl.DeviceIdType.MESH
+VM = pl.BlockSpec(memory_space=pltpu.VMEM)
+F32 = jnp.float32
+BF = jnp.bfloat16
+
+def neighbour_barrier(z, n, axis):
+    barrier = pltpu.get_barrier_semaphore()
+    @pl.when(z > 0)
+    def _():
+        pl.semaphore_signal(barrier, inc=1, device_id={axis: z - 1}, device_id_type=MESH)
+    @pl.when(z < n - 1)
+    def _():
+        pl.semaphore_signal(barrier, inc=1, device_id={axis: z + 1}, device_id_type=MESH)
+    ends = jnp.where(z > 0, 1, 0) + jnp.where(z < n - 1, 1, 0)
+    pl.semaphore_wait(barrier, ends)
+
+def rcopy(src, dst, ss, rs, dev):
+    return pltpu.make_async_remote_copy(src_ref=src, dst_ref=dst, send_sem=ss, recv_sem=rs, device_id={"tensor": dev}, device_id_type=MESH)
+
+def ar_kernel(n, R, lag, part, out, upin, upout, us, ur, ds, dr):
+    z = lax.axis_index("tensor")
+    rows = part.shape[0]; half = rows // 2; C = half // R
+    neighbour_barrier(z, n, "tensor")
+    def body(t, _):
+        for f in range(2):
+            p = z if f == 0 else n - 1 - z
+            step = 1 if f == 0 else -1
+            c = t - lag * p
+            @pl.when((c >= 0) & (c < C))
+            def _():
+                r = pl.ds(pl.multiple_of(f * half + c * R, R), R)
+                @pl.when(p == 0)
+                def _():
+                    rcopy(part.at[r], upin.at[r], us.at[f, c], ur.at[f, c], z + step).start()
+                @pl.when(p > 0)
+                def _():
+                    rcopy(upin.at[r], upin.at[r], us.at[f, c], ur.at[f, c], z).wait_recv()
+                    s = (part[r, :].astype(F32) + upin[r, :].astype(F32)).astype(BF)
+                    @pl.when(p < n - 1)
+                    def _():
+                        upout[r, :] = s
+                        rcopy(upout.at[r], upin.at[r], us.at[f, c], ur.at[f, c], z + step).start()
+                    @pl.when(p == n - 1)
+                    def _():
+                        out[r, :] = s
+                        rcopy(out.at[r], out.at[r], ds.at[f, c], dr.at[f, c], z - step).start()
+        for f in range(2):
+            p = z if f == 0 else n - 1 - z
+            step = 1 if f == 0 else -1
+            c = t - lag * (2 * (n - 1) - p)
+            @pl.when((c >= 0) & (c < C) & (p < n - 1))
+            def _():
+                r = pl.ds(pl.multiple_of(f * half + c * R, R), R)
+                rcopy(out.at[r], out.at[r], ds.at[f, c], dr.at[f, c], z).wait_recv()
+                @pl.when(p > 0)
+                def _():
+                    rcopy(out.at[r], out.at[r], ds.at[f, c], dr.at[f, c], z - step).start()
+        return 0
+    lax.fori_loop(0, C + 2 * lag * (n - 1), body, 0)
+    def drain(c, _):
+        for f in range(2):
+            p = z if f == 0 else n - 1 - z
+            r = pl.ds(pl.multiple_of(f * half + c * R, R), R)
+            @pl.when(p < n - 1)
+            def _():
+                rcopy(upout.at[r], upin.at[r], us.at[f, c], ur.at[f, c], z).wait_send()
+            @pl.when(p > 0)
+            def _():
+                rcopy(out.at[r], out.at[r], ds.at[f, c], dr.at[f, c], z).wait_send()
+        return 0
+    lax.fori_loop(0, C, drain, 0)
+
+def ar(part, n, R=32, lag=5, cid=3):
+    rows, w = part.shape
+    C = rows // 2 // R
+    return pl.pallas_call(
+        functools.partial(ar_kernel, n, R, lag),
+        out_shape=jax.ShapeDtypeStruct((rows, w), BF),
+        in_specs=[VM], out_specs=VM,
+        scratch_shapes=[pltpu.VMEM((rows, w), BF), pltpu.VMEM((rows, w), BF)] + [pltpu.SemaphoreType.DMA((2, C))] * 4,
+        compiler_params=pltpu.CompilerParams(collective_id=cid, has_side_effects=True, vmem_limit_bytes=60 << 20),
+    )(part)
+
+def rs_kernel(n, R, lag, part, out, right, left, ss, rs):
+    z = lax.axis_index("tensor")
+    rows, w = out.shape; C = rows // R
+    neighbour_barrier(z, n, "tensor")
+    def at(ref, c, b):
+        return ref.at[pl.ds(pl.multiple_of(c * R, R), R), pl.ds(b * w, w)]
+    def body(t, _):
+        for d, buf, step in ((0, right, 1), (1, left, -1)):
+            p = z if d == 0 else n - 1 - z
+            c = t - lag * p
+            @pl.when((c >= 0) & (c < C))
+            def _():
+                r = pl.ds(pl.multiple_of(c * R, R), R)
+                for b in (range(n - 1, 0, -1) if d == 0 else range(n - 1)):
+                    on = (b > z) if d == 0 else (b < z)
+                    k = pl.ds(b * w, w)
+                    @pl.when(on)
+                    def _():
+                        @pl.when(p == 0)
+                        def _():
+                            rcopy(at(part, c, b), at(buf, c, b), ss.at[d, b, c], rs.at[d, b, c], z + step).start()
+                        @pl.when(p > 0)
+                        def _():
+                            rcopy(at(buf, c, b), at(buf, c, b), ss.at[d, b, c], rs.at[d, b, c], z).wait_recv()
+                            buf[r, k] = (part[r, k].astype(F32) + buf[r, k].astype(F32)).astype(BF)
+                            rcopy(at(buf, c, b), at(buf, c, b), ss.at[d, b, c], rs.at[d, b, c], z + step).start()
+        c = t - lag * (n - 1)
+        @pl.when((c >= 0) & (c < C))
+        def _():
+            r = pl.ds(pl.multiple_of(c * R, R), R)
+            for b in range(n):
+                k = pl.ds(b * w, w)
+                @pl.when(z == b)
+                def _():
+                    s = part[r, k].astype(F32)
+                    if b > 0:
+                        rcopy(at(right, c, b), at(right, c, b), ss.at[0, b, c], rs.at[0, b, c], z).wait_recv()
+                        s = s + right[r, k].astype(F32)
+                    if b < n - 1:
+                        rcopy(at(left, c, b), at(left, c, b), ss.at[1, b, c], rs.at[1, b, c], z).wait_recv()
+                        s = s + left[r, k].astype(F32)
+                    out[r, :] = s.astype(BF)
+        return 0
+    lax.fori_loop(0, C + lag * (n - 1), body, 0)
+    def drain(c, _):
+        for d, buf in ((0, right), (1, left)):
+            for b in range(n):
+                @pl.when((b > z) if d == 0 else (b < z))
+                def _():
+                    rcopy(at(buf, c, b), at(buf, c, b), ss.at[d, b, c], rs.at[d, b, c], z).wait_send()
+        return 0
+    lax.fori_loop(0, C, drain, 0)
+
+def rs(part, n, R=64, lag=1, cid=5):
+    rows, nw = part.shape
+    w = nw // n
+    C = rows // R
+    return pl.pallas_call(
+        functools.partial(rs_kernel, n, R, lag),
+        out_shape=jax.ShapeDtypeStruct((rows, w), BF),
+        in_specs=[VM], out_specs=VM,
+        scratch_shapes=[pltpu.VMEM((rows, nw), BF), pltpu.VMEM((rows, nw), BF)] + [pltpu.SemaphoreType.DMA((2, n, C))] * 2,
+        compiler_params=pltpu.CompilerParams(collective_id=cid, has_side_effects=True, vmem_limit_bytes=60 << 20),
+    )(part)
 
 
 eps = 1e-05
@@ -108,11 +259,12 @@
     tensor_member = lax.axis_index("tensor")
     inputs = owned_tokens.astype(jnp.float32)
 
+    ids = iter((3, 4))
+
     def all_sum(values):
-        part = lax.psum_scatter(
-            values.astype(jnp.bfloat16), "tensor", scatter_dimension=1, tiled=True
+        return ar(values.astype(jnp.bfloat16), lax.axis_size("tensor"), cid=next(ids)).astype(
+            jnp.float32
         )
-        return lax.all_gather(part, "tensor", axis=1, tiled=True).astype(jnp.float32)
 
     def my_part(values):
         return lax.dynamic_slice_in_dim(values, tensor_member * width_part, width_part, 1)
@@ -180,7 +332,7 @@
     grad_out = owned_cotangent.astype(jnp.float32)
     grad_ffn = (keep_rows * grad_out).astype(jnp.bfloat16)
     grad_inner = matmul(grad_ffn, down_weight.T)
-    down_grad = matmul(inner_low.T, grad_ffn)
+    down_grad = matmul(grad_ffn.T, inner_low)
     grad_gate = (grad_inner * upward * gate_sig * (1.0 + gate * (1.0 - gate_sig))).astype(
         jnp.bfloat16
     )
@@ -198,7 +350,7 @@
     )
     grad_attn = (keep_rows * grad_res).astype(jnp.bfloat16)
     grad_attended = matmul(grad_attn, output_weight.T)
-    output_grad = matmul(attended_low.T, grad_attn)
+    output_grad = matmul(grad_attn.T, attended_low)
     grad_attended_low = grad_attended.reshape(row_count, local_kv, group_size, HEAD_WIDTH).astype(
         jnp.bfloat16
     )
@@ -230,13 +382,13 @@
     )
     grad_key_low = unrotate(grad_key).reshape(row_count, local_kv * HEAD_WIDTH).astype(jnp.bfloat16)
     grad_value_low = grad_value.reshape(row_count, local_kv * HEAD_WIDTH).astype(jnp.bfloat16)
-    first_back = lax.psum_scatter(
-        (matmul(grad_query_low, query_weight.T)
-        + matmul(grad_key_low, key_matrix.T)
-        + matmul(grad_value_low, value_matrix.T)).astype(jnp.bfloat16),
-        "tensor",
-        scatter_dimension=1,
-        tiled=True,
+    first_back = rs(
+        (
+            matmul(grad_query_low, query_weight.T)
+            + matmul(grad_key_low, key_matrix.T)
+            + matmul(grad_value_low, value_matrix.T)
+        ).astype(jnp.bfloat16),
+        lax.axis_size("tensor"),
     ).astype(jnp.float32)
     query_grad = matmul(normed_one.T, grad_query_low)
     key_grad = matmul(normed_one.T, grad_key_low)
@@ -268,24 +420,30 @@
         down_grad,
         second_gain_grad,
     )
-    by_width = [gradient_set[k] for k in (1, 2, 3, 5, 6)] + [gradient_set[k].T for k in (4, 7)]
-    gains = jnp.stack([first_gain_grad, second_gain_grad], axis=1)
-    joined = jnp.concatenate([g.astype(jnp.bfloat16) for g in by_width] + [gains.astype(jnp.bfloat16)], axis=1)
-    shared = lax.psum_scatter(joined, "dp", scatter_dimension=0, tiled=True).astype(jnp.float32)
-    cuts, at = [], 0
-    for g in by_width:
-        cuts.append(shared[:, at : at + g.shape[1]])
-        at += g.shape[1]
+    def shared(*values):
+        low = [v.astype(jnp.bfloat16) for v in values]
+        joined = jnp.concatenate(low, axis=1) if len(low) > 1 else low[0]
+        return lax.psum_scatter(joined, "dp", scatter_dimension=0, tiled=True).astype(jnp.float32)
+
+    gate_share, up_share, down_share, output_share = map(
+        shared, (gate_grad, up_grad, down_grad, output_grad)
+    )
+    first = shared(
+        query_grad, key_grad, value_grad, first_gain_grad[:, None], second_gain_grad[:, None]
+    )
+    a = query_grad.shape[1]
+    b = a + key_grad.shape[1]
+    c = b + value_grad.shape[1]
     summed = (
-        shared[:, at],
-        cuts[0],
-        cuts[1],
-        cuts[2],
-        cuts[5].T,
-        cuts[3],
-        cuts[4],
-        cuts[6].T,
-        shared[:, at + 1],
+        first[:, c],
+        first[:, :a],
+        first[:, a:b],
+        first[:, b:c],
+        output_share.T,
+        gate_share,
+        up_share,
+        down_share.T,
+        first[:, c + 1],
     )
     return (
         layer_output,

time: 1060 us -> 1010 us (0.953)
  Pallas kernels: 0 us -> 372 us
  waiting for transfers between devices: 593 us -> 239 us
  local copies, waits for them, and re-layouts: 142 us -> 59.6 us
  matrix products: 158 us -> 191 us
  blocking collectives: 61.9 us -> 41.4 us
    pallas_call x0 -> x3, Pallas kernels: none -> 372 us  [the longest x2 260 us: ar(): pl.pallas_call(functools.partial(ar_kernel, n, R, lag), out_shape=jax.Sha...]
    reduce_scatter x4 -> x5, waiting for transfers between devices: 312 us -> 155 us  [shared(): lax.psum_scatter(joined, 'dp', scatter_dimension=0, tiled=True)]
    all_gather x2 -> x0, waiting for transfers between devices: 141 us -> none  [all_sum(): lax.all_gather(part, 'tensor', axis=1, tiled=True).astype(jnp.float32)]
    concatenate x1, local copies, waits for them, and re-layouts: 95 us -> 13 us  [shared(): joined = jnp.concatenate(low, axis=1) if len(low) > 1 else low[0]]
    all_gather x1, waiting for transfers between devices: 51.1 us -> 0.01 us  [per_device(): lax.all_gather(part_cotangent, 'tensor', axis=1, tiled=True)]
    all_gather x1, waiting for transfers between devices: 78.1 us -> 55.7 us  [per_device(): lax.all_gather(part_tokens, 'tensor', axis=1, tiled=True)]
    dot_general x21, matrix products: 127 us -> 148 us  [matmul(): return jnp.dot(left, right, preferred_element_type=jnp.float32)]
    all_to_all x1 -> x0, blocking collectives: 19.6 us -> none  [per_device(): lax.all_to_all(cotangent[send_rows], 'dp', split_axis=0, concat_axis=0, t...]
  transfers between devices with their start and end apart: 11 -> 11, of which waited for: 10 -> 6; matrix products, arithmetic and copies ran while one was open for 19% -> 24% of each run, Pallas kernels for 0% -> 26%
where the time goes in v2:
time: 1010 us; the launch traced here: 1000 us
  Pallas kernels  372 us (37%)
  waiting for transfers between devices  239 us (24%)
  matrix products  191 us (19%)
  other arithmetic  71.8 us (7%)
  local copies, waits for them, and re-layouts  59.6 us (6%)
  blocking collectives  41.4 us (4%)
  between operations  15.2 us (2%)
  starting transfers between devices  11.9 us (1%)
    pallas_call x2, Pallas kernels, ar(): pl.pallas_call(functools.partial(ar_kernel, n, R, lag), out_shape=jax.Sha...  260 us
    reduce_scatter x5, waiting for transfers between devices, shared(): lax.psum_scatter(joined, 'dp', scatter_dimension=0, tiled=True)  155 us
    dot_general x21, matrix products, matmul(): return jnp.dot(left, right, preferred_element_type=jnp.float32)  148 us
    pallas_call x1, Pallas kernels, rs(): pl.pallas_call(functools.partial(rs_kernel, n, R, lag), out_shape=jax.Sha...  112 us
    all_gather x1, waiting for transfers between devices, per_device(): lax.all_gather(part_tokens, 'tensor', axis=1, tiled=True)  55.7 us
    unnamed x113, local copies, waits for them, and re-layouts  20.8 us
    all_to_all x1, blocking collectives, per_device(): lax.all_to_all(tokens[send_rows], 'dp', split_axis=0, concat_axis=0, tile...  20.6 us
  transfers between devices with their start and end apart: 11, of which 6 were waited for; matrix products, arithmetic and copies ran while one was open for 24% of the time, Pallas kernels for 26%

profile of v2, /device:TPU:0, one launch (start us, length us, event | category | flops | bytes accessed | tf_op | source)
XLA Modules:
  0.0 1002.1 jit_solution(2891952587374531784)
XLA Ops:
  11.2 6.6 gather_fusion
  17.8 20.6 %all_to_all.48 = bf16[8,128,512]{2,1,0:T(8,128)(2,1)} all-to-all(bf16[8,128,512]{2,1,0:T(8,128)(2,1)} %bitcast.191), channel_id=1, replica_groups=mesh['dp'=8,'tensor'=4] {'dp'}, dimensions={0} | all-to-all | bytes 2097152 | tf_op jit(solution)/shard_map/all_to_all | solution.py:248
  38.4 5.1 gather_fusion.2
  43.5 4.4 all-to-all-start.2
  50.1 13.2 %all-to-all-done.2 = bf16[8,128,512]{2,1,0:T(8,128)(2,1)} async-done(((bf16[8,128,512]{2,1,0:T(8,128)(2,1)}), bf16[8,128,512]{2,1,0:T(8,128)(2,1)}, u32[]{:S(2)}, u32[]{:S(2)}) %all-to-all-start.2) | async-done | bytes 1048608 | tf_op jit(solution)/shard_map/all_to_all | solution.py:249
  63.4 55.7 %all-gather.4.cloned.1.call-done = bf16[1024,2048]{1,0:T(8,128)(2,1)} async-done(((bf16[1024,512]{1,0:T(8,128)(2,1)}), bf16[1024,2048]{1,0:T(8,128)(2,1)}) %all-gather.4.cloned.1.call-update) | async-done | bytes 4194320 | tf_op jit(solution)/shard_map/all_gather | solution.py:252
  119.1 3.2 multiply_reduce_fusion.1
  125.4 1.5 fusion.77
  127.7 2.4 fusion.78
  130.3 2.1 fusion.52
  134.6 7.6 fusion.76
  142.1 8.1 fusion.3
  150.2 7.7 fusion.35
  158.9 4.4 convolution_convert_fusion.4.part
  163.3 145.7 %shard_map.221 = bf16[1024,2048]{1,0:T(8,128)(2,1)} custom-call(bf16[1024,2048]{1,0:T(8,128)(2,1)} %convolution_convert_fusion.4.part), custom_call_target="tpu_custom_call" | custom-call | tf_op jit(solution)/shard_map/pallas_call | solution.py:88
  309.0 4.5 multiply_reduce_fusion
  314.3 3.4 copy-done.2
  317.8 11.9 %fusion.80 = f32[1024,1408]{1,0:T(8,128)} fusion(bf16[1024,2048]{1,0:T(8,128)(2,1)S(1)} %multiply_convert_fusion.1, bf16[2048,1408]{1,0:T(8,128)(2,1)} %param.23), kind=kOutput, calls=%fused_computation.168 | convolution fusion | flops 5905580032 | bytes 15728640 | tf_op jit(solution)/shard_map/dot_general | solution.py:185
  329.6 8.5 fusion.79
  338.1 15.8 %multiply_convert_fusion.3 = (bf16[1024,1408]{1,0:T(8,128)(2,1)S(1)}, bf16[1024,1408]{1,0:T(8,128)(2,1)S(1)}, bf16[1024,1408]{1,0:T(8,128)(2,1)}) fusion(f32[1024,1408]{1,0:T(8,128)} %fusion.79, f32[1024,1408]{1,0:T(8,128)} %fusion.80, bf16[1408,2048]{1,0:T(8,128)(2,1)} %param.24, bf16[1024,2048]{1,0:T(8,128)(2,1)} %all-gather.6.cloned.1.call-done, ...), kind=kOutput, calls=%fused_computation.43 | convolution fusion | flops 5933498368 | bytes 30150656 | tf_op jit(solution)/shard_map/dot_general | solution.py:185
  353.9 10.8 %fusion.81 = f32[1024,2048]{1,0:T(8,128)S(1)} fusion(bf16[1024,1408]{1,0:T(8,128)(2,1)S(1)} %get-tuple-element.70, bf16[2048,1408]{1,0:T(8,128)(2,1)} %param.22), kind=kOutput, calls=%fused_computation.169 | convolution fusion | flops 5905580032 | bytes 17039360 | tf_op jit(solution)/shard_map/dot_general | solution.py:185
  364.7 11.0 %add_convert_fusion.1.part = bf16[1024,2048]{1,0:T(8,128)(2,1)} fusion(f32[1024,2048]{1,0:T(8,128)S(1)} %fusion.81, bf16[1024,1408]{1,0:T(8,128)(2,1)S(1)} %get-tuple-element.69, bf16[2048,1408]{1,0:T(8,128)(2,1)} %param.23), kind=kOutput, calls=%fused_computation.34 | convolution fusion | flops 5909774336 | bytes 21233664 | tf_op jit(solution)/shard_map/dot_general | solution.py:185
  375.7 114.6 %shard_map.222 = bf16[1024,2048]{1,0:T(8,128)(2,1)} custom-call(bf16[1024,2048]{1,0:T(8,128)(2,1)} %add_convert_fusion.1.part), custom_call_target="tpu_custom_call" | custom-call | tf_op jit(solution)/shard_map/pallas_call | solution.py:88
  490.4 7.2 fusion.11
  497.6 4.9 fusion.9
  502.5 3.2 copy-done.14
  505.7 4.2 convolution_convert_fusion.6
  510.7 6.0 convolution_convert_fusion.9
  516.7 11.3 %convolution_convert_fusion.3 = bf16[1024,2048]{1,0:T(8,128)(2,1)} fusion(bf16[1024,1408]{1,0:T(8,128)(2,1)S(1)} %copy-done.45, bf16[1408,2048]{1,0:T(8,128)(2,1)} %param.24), kind=kOutput, calls=%fused_computation.49 | convolution fusion | flops 5907677184 | bytes 12845056 | tf_op jit(solution)/shard_map/dot_general | solution.py:185
  529.0 13.8 %fusion = (f32[4,1024]{1,0:T(4,128)S(1)}, f32[1024,1024,4]{1,0,2:T(8,128)}) fusion(f32[1,4,1024,1024]{2,3,1,0:T(8,128)} %get-tuple-element.100, f32[4,1024]{1,0:T(4,128)S(1)} %log_add_fusion, bf16[1024,128,1]{1,0,2:T(8,128)(2,1)S(1)} %copy-done.31, bf16[1024,4,128]{0,2,1:T(8,128)(2,1)S(1)} %bitcast.186), kind=kOutput, calls=%fused_computation.7 | convolution fusion | flops 1086320640 | bytes 34897920 | tf_op jit(solution)/shard_map/qcgd,kcd->cgqk/dot_general | solution.py:362
  542.8 1.4 slice-done.2
  545.4 8.2 fusion.15
  553.6 1.4 bitcast_multiply_fusion.3
  555.1 1.8 copy-done.3
  557.9 1.6 fusion.31
  559.5 9.4 fusion.60
  570.0 2.2 fusion.59
  572.1 5.7 fusion.64
  577.9 5.7 fusion.82
  583.5 3.2 fusion.47
  586.7 9.1 add_convert_fusion.part
  595.9 111.9 %shard_map.223 = bf16[1024,512]{1,0:T(8,128)(2,1)} custom-call(bf16[1024,2048]{1,0:T(8,128)(2,1)} %add_convert_fusion.part), custom_call_target="tpu_custom_call" | custom-call | tf_op jit(solution)/shard_map/pallas_call | solution.py:153
  707.8 3.4 convert_element_type.212
  712.1 11.9 %all-gather = bf16[4,1,512]{2,1,0:T(2,128)(2,1)S(1)} all-gather(bf16[1,1,512]{2,1,0:T(2,128)(2,1)S(1)} %convert.7), channel_id=1, replica_groups=mesh['dp'=8,'tensor'=4] {'tensor'}, dimensions={0}, use_global_device_ids=true | all-gather | bytes 5120 | tf_op jit(solution)/shard_map/all_gather | solution.py:405
  725.5 3.7 convolution_convert_fusion.5
  729.2 13.0 %concatenate.58 = bf16[2048,770]{0,1:T(8,128)(2,1)} concatenate(bf16[2048,512]{0,1:T(8,128)(2,1)} %convolution_convert_fusion.5, bf16[2048,128]{0,1:T(8,128)(2,1)S(1)} %convolution_convert_fusion.8, bf16[2048,128]{0,1:T(8,128)(2,1)S(1)} %convolution_convert_fusion.7, bf16[2048,1]{0,1:T(2,128)(2,1)S(1)} %bitcast.193, bf16[2048,1]{0,1:T(2,128)(2,1)S(1)} %convert_element_type.262), dimensions={1} | concatenate | bytes 6307840 | tf_op jit(solution)/shard_map/concatenate | solution.py:425
  742.3 11.5 %convolution_convert_fusion = bf16[2048,1408]{1,0:T(8,128)(2,1)} fusion(bf16[1024,1408]{1,0:T(8,128)(2,1)} %get-tuple-element.71, bf16[1024,2048]{1,0:T(8,128)(2,1)} %all-gather.6.cloned.1.call-done, f32[1024]{0:T(1024)S(1)} %broadcast_bitcast_fusion.1), kind=kOutput, calls=%fused_computation.40 | convolution fusion | flops 5914755072 | bytes 12849152 | tf_op jit(solution)/shard_map/dot_general | solution.py:185
  753.8 11.1 %convolution_convert_fusion.1 = bf16[2048,1408]{1,0:T(8,128)(2,1)} fusion(bf16[1024,2048]{1,0:T(8,128)(2,1)} %copy-done.20, bf16[1024,1408]{1,0:T(8,128)(2,1)} %copy-done.47), kind=kOutput, calls=%fused_computation.41 | convolution fusion | flops 5908463616 | bytes 12845056 | tf_op jit(solution)/shard_map/dot_general | solution.py:185
  765.0 11.0 %convolution_convert_fusion.2 = bf16[2048,1408]{1,0:T(8,128)(2,1)} fusion(bf16[1024,2048]{1,0:T(8,128)(2,1)} %copy-done.20, bf16[1024,1408]{1,0:T(8,128)(2,1)} %copy-done.46), kind=kOutput, calls=%fused_computation.42 | convolution fusion | flops 5908463616 | bytes 12845056 | tf_op jit(solution)/shard_map/dot_general | solution.py:185
  776.1 8.9 psum.7
  785.0 3.9 fusion.24
  788.8 3.6 all-to-all-start.3
  792.6 15.2 %all-to-all-done.3 = bf16[8,128,512]{2,1,0:T(8,128)(2,1)S(1)} async-done(((bf16[8,128,512]{2,1,0:T(8,128)(2,1)}), bf16[8,128,512]{2,1,0:T(8,128)(2,1)S(1)}, u32[]{:S(2)}, u32[]{:S(2)}) %all-to-all-start.3) | async-done | bytes 1048608 | tf_op jit(solution)/shard_map/all_to_all | solution.py:408
  807.9 5.1 gather_fusion.3
  814.9 3.8 add_convert_fusion.3
  818.7 3.6 all-to-all-start.1
  826.7 1.3 fusion.72
  828.1 34.1 %reduce-scatter.17.cloned.1.call-done = bf16[256,1408]{1,0:T(8,128)(2,1)} async-done(((bf16[2048,1408]{1,0:T(8,128)(2,1)}), bf16[256,1408]{1,0:T(8,128)(2,1)}) %reduce-scatter.17.cloned.1.call-update) | async-done | bytes 720912 | tf_op jit(solution)/shard_map/reduce_scatter | solution.py:426
  863.4 1.5 copy.76
  864.9 59.8 %reduce-scatter.15.cloned.1.call-done = bf16[256,1408]{1,0:T(8,128)(2,1)} async-done(((bf16[2048,1408]{1,0:T(8,128)(2,1)}), bf16[256,1408]{1,0:T(8,128)(2,1)}) %reduce-scatter.15.cloned.1.call-update) | async-done | bytes 720912 | tf_op jit(solution)/shard_map/reduce_scatter | solution.py:426
  924.7 2.3 convert_element_type.268
  927.0 60.6 %reduce-scatter.13.cloned.1.call-done = bf16[256,1408]{1,0:T(8,128)(2,1)} async-done(((bf16[2048,1408]{1,0:T(8,128)(2,1)}), bf16[256,1408]{1,0:T(8,128)(2,1)}) %reduce-scatter.13.cloned.1.call-update) | async-done | bytes 720912 | tf_op jit(solution)/shard_map/reduce_scatter | solution.py:426
  987.6 2.3 convert_element_type.266
  990.0 5.1 gather_fusion.1
  (177 shorter events, 29.4 us)
Async XLA Ops:
  7.2 151.7 %copy-start = (bf16[512,2048]{1,0:T(8,128)(2,1)S(1)}, bf16[512,2048]{1,0:T(8,128)(2,1)}, u32[]{:S(2)}) copy-start(bf16[512,2048]{1,0:T(8,128)(2,1)} %param.20) | copy-start | bytes 6291460
  7.2 111.9 %all-gather.4.cloned.1.call-start = ((), (), s32[]{:S(2)}) async-start(), calls=%async_computation.10 | async-start | bytes 5242880 | tf_op jit(solution)/shard_map/all_gather | solution.py:252
  8.9 2.2 copy-start.37
  11.2 27.2 %copy-start.7 = (bf16[1024,512]{1,0:T(8,128)(2,1)S(1)}, bf16[1024,512]{1,0:T(8,128)(2,1)}, u32[]{:S(2)}) copy-start(bf16[1024,512]{1,0:T(8,128)(2,1)} %param.15) | copy-start | bytes 3145732
  43.5 79.4 %copy-start.36 = (f32[2048]{0:T(1024)S(1)}, f32[2048]{0:T(1024)}, u32[]{:S(2)}) copy-start(f32[2048]{0:T(1024)} %param.16) | copy-start | bytes 24580
  43.5 19.8 %all-to-all-start.2 = ((bf16[8,128,512]{2,1,0:T(8,128)(2,1)}), bf16[8,128,512]{2,1,0:T(8,128)(2,1)}, u32[]{:S(2)}, u32[]{:S(2)}) async-start(bf16[8,128,512]{2,1,0:T(8,128)(2,1)} %bitcast.190), calls=%async_computation.3 | async-start | bytes 2097152 | tf_op jit(solution)/shard_map/all_to_all | solution.py:249
  47.9 290.2 %all-gather.6.cloned.1.call-start = ((), (), s32[]{:S(2)}) async-start(), calls=%async_computation.12 | async-start | bytes 5242880 | tf_op jit(solution)/shard_map/all_gather | solution.py:253
  63.4 749.6 %reduce-scatter.11.cloned.1.call-start = ((), (), s32[]{:S(2)}) async-start(), calls=%async_computation.14 | async-start | bytes 2359296 | tf_op jit(solution)/shard_map/reduce_scatter | solution.py:426
  119.1 3.8 copy-start.6
  123.0 1.0 copy-start.33
  123.0 1.0 copy-start.28
  124.0 3.0 copy-start.4
  124.0 1.4 copy-start.25
  125.4 24.8 %copy-start.30 = (bf16[1024,128,1]{1,0,2:T(8,128)(2,1)}, bf16[1024,128,1]{1,0,2:T(8,128)(2,1)S(1)}, u32[]{:S(2)}) copy-start(bf16[1024,128,1]{1,0,2:T(8,128)(2,1)S(1)} %fusion.46) | copy-start | bytes 786436
  125.4 2.2 copy-start.41
  130.1 3.1 copy-start.10
  132.5 1.3 copy-start.16
  132.5 2.1 copy-start.22
  133.2 1.3 copy-start.12
  157.9 1.0 copy-start.43
  309.0 4.6 copy-start.32
  313.5 4.3 copy-start.2
  313.5 16.1 %slice-start.4 = ((s8[5767168]{0:T(1024)(128)(4,1)}), s8[4194304]{0:T(1024)(128)(4,1)S(1)}, s32[]{:S(2)}) async-start(s8[5767168]{0:T(1024)(128)(4,1)} %bitcast.203), calls=%async_computation.22 | async-start | bytes 8388608
  317.8 11.9 %copy-start.20 = (bf16[1024,2048]{1,0:T(8,128)(2,1)}, bf16[1024,2048]{1,0:T(8,128)(2,1)S(1)}, u32[]{:S(2)}) copy-start(bf16[1024,2048]{1,0:T(8,128)(2,1)S(1)} %multiply_convert_fusion.1) | copy-start | bytes 12582916
  317.8 11.9 %slice-start.5 = ((s8[5767168]{0:T(1024)(128)(4,1)}), s8[1572864]{0:T(1024)(128)(4,1)S(1)}, s32[]{:S(2)}) async-start(s8[5767168]{0:T(1024)(128)(4,1)} %bitcast.203), calls=%async_computation.23 | async-start | bytes 3145728
  353.9 10.8 %copy-start.46 = (bf16[1024,1408]{1,0:T(8,128)(2,1)}, bf16[1024,1408]{1,0:T(8,128)(2,1)S(1)}, u32[]{:S(2)}) copy-start(bf16[1024,1408]{1,0:T(8,128)(2,1)S(1)} %get-tuple-element.70) | copy-start | bytes 8650756
  353.9 10.8 %copy-start.47 = (bf16[1024,1408]{1,0:T(8,128)(2,1)}, bf16[1024,1408]{1,0:T(8,128)(2,1)S(1)}, u32[]{:S(2)}) copy-start(bf16[1024,1408]{1,0:T(8,128)(2,1)S(1)} %get-tuple-element.69) | copy-start | bytes 8650756
  490.3 7.2 copy-start.8
  490.3 7.2 copy-start.21
  497.6 8.1 copy-start.44
  502.5 3.2 copy-start.14
  509.9 305.1 %reduce-scatter.7.cloned.1.call-start = ((), (), s32[]{:S(2)}) async-start(), calls=%async_computation.11 | async-start | bytes 5242880 | tf_op jit(solution)/shard_map/reduce_scatter | solution.py:328
  510.7 6.0 copy-start.45
  528.0 0.9 copy-start.31
  528.1 294.2 %reduce-scatter.9.cloned.1.call-start = ((), (), s32[]{:S(2)}) async-start(), calls=%async_computation.13 | async-start | bytes 3575808 | tf_op jit(solution)/shard_map/reduce_scatter | solution.py:426
  528.1 14.6 %slice-start = ((s8[16777216]{0:T(1024)(128)(4,1)}), s8[4194304]{0:T(1024)(128)(4,1)S(1)}, s32[]{:S(2)}) async-start(s8[16777216]{0:T(1024)(128)(4,1)} %bitcast.180), calls=%async_computation.18 | async-start | bytes 8388608
  529.0 13.8 %slice-start.1 = ((s8[16777216]{0:T(1024)(128)(4,1)}), s8[4194304]{0:T(1024)(128)(4,1)S(1)}, s32[]{:S(2)}) async-start(s8[16777216]{0:T(1024)(128)(4,1)} %bitcast.180), calls=%async_computation.19 | async-start | bytes 8388608
  529.0 15.2 %slice-start.2 = ((s8[16777216]{0:T(1024)(128)(4,1)}), s8[4194304]{0:T(1024)(128)(4,1)S(1)}, s32[]{:S(2)}) async-start(s8[16777216]{0:T(1024)(128)(4,1)} %bitcast.180), calls=%async_computation.20 | async-start | bytes 8388608
  529.0 16.4 %slice-start.3 = ((s8[16777216]{0:T(1024)(128)(4,1)}), s8[4194304]{0:T(1024)(128)(4,1)S(1)}, s32[]{:S(2)}) async-start(s8[16777216]{0:T(1024)(128)(4,1)} %bitcast.180), calls=%async_computation.21 | async-start | bytes 8388608
  545.4 8.2 copy-start.19
  545.4 8.2 copy-start.23
  553.6 3.3 copy-start.3
  556.9 1.0 copy-start.17
  557.0 2.4 copy-start.11
  557.0 2.4 copy-start.13
  557.1 2.4 copy-start.24
  572.1 5.7 copy-start.26
  572.1 5.7 copy-start.42
  583.5 3.2 copy-start.29
  707.7 3.5 copy-start.15
  707.7 3.5 copy-start.34
  707.7 16.3 %copy-start.5 = (bf16[1024,2048]{1,0:T(8,128)(2,1)S(1)}, bf16[1024,2048]{1,0:T(8,128)(2,1)}, u32[]{:S(2)}) copy-start(bf16[1024,2048]{1,0:T(8,128)(2,1)} %copy-done.4) | copy-start | bytes 12582916
  711.2 14.3 %copy-start.9 = (f32[1024,2048]{1,0:T(8,128)}, f32[1024,2048]{1,0:T(8,128)S(1)}, u32[]{:S(2)}) copy-start(f32[1024,2048]{1,0:T(8,128)S(1)} %convert_element_type.212) | copy-start | bytes 25165828
  724.0 1.5 copy-start.27
  742.2 119.9 %reduce-scatter.17.cloned.1.call-start = ((), (), s32[]{:S(2)}) async-start(), calls=%async_computation.17 | async-start | bytes 6488064 | tf_op jit(solution)/shard_map/reduce_scatter | solution.py:426
  753.8 171.0 %reduce-scatter.15.cloned.1.call-start = ((), (), s32[]{:S(2)}) async-start(), calls=%async_computation.16 | async-start | bytes 6488064 | tf_op jit(solution)/shard_map/reduce_scatter | solution.py:426
  765.0 222.7 %reduce-scatter.13.cloned.1.call-start = ((), (), s32[]{:S(2)}) async-start(), calls=%async_computation.15 | async-start | bytes 6488064 | tf_op jit(solution)/shard_map/reduce_scatter | solution.py:426
  776.0 8.9 copy-start.35
  784.9 7.5 copy-start.38
  784.9 7.5 copy-start.39
  785.0 7.5 copy-start.40
  788.8 19.0 %all-to-all-start.3 = ((bf16[8,128,512]{2,1,0:T(8,128)(2,1)}), bf16[8,128,512]{2,1,0:T(8,128)(2,1)S(1)}, u32[]{:S(2)}, u32[]{:S(2)}) async-start(bf16[8,128,512]{2,1,0:T(8,128)(2,1)} %bitcast.54), calls=%async_computation.4 | async-start | bytes 2097152 | tf_op jit(solution)/shard_map/all_to_all | solution.py:408
  818.7 171.2 %all-to-all-start.1 = ((bf16[8,128,512]{2,1,0:T(8,128)(2,1)}), bf16[8,128,512]{2,1,0:T(8,128)(2,1)S(1)}, u32[]{:S(2)}, u32[]{:S(2)}) async-start(bf16[8,128,512]{2,1,0:T(8,128)(2,1)} %bitcast.22), calls=%async_computation.2 | async-start | bytes 2097152 | tf_op jit(solution)/shard_map/all_to_all | solution.py:407
  990.0 5.1 copy-start.1
  (1 other events, 0.8 us)
Sparse Core Ops, SparseCore 0:
  38.5 80.5 all-gather.3
  120.7 104.9 all-gather.5
  510.0 42.9 reduce-scatter.10
  555.3 107.7 reduce-scatter.6
  742.4 45.8 reduce-scatter.8
  792.0 70.1 reduce-scatter.16
  865.6 59.0 reduce-scatter.14
  928.6 59.0 reduce-scatter.12

commit v3 on v2

v3 whole, which is shorter than its diff:
```python
import functools
import math

import jax
import jax.numpy as jnp
from jax import lax
from jax.experimental import pallas as pl
from jax.experimental.pallas import tpu as pltpu
from jax.sharding import PartitionSpec as P

HEAD_WIDTH = 128

MESH = pl.DeviceIdType.MESH
VM = pl.BlockSpec(memory_space=pltpu.VMEM)
F32 = jnp.float32
BF = jnp.bfloat16

def neighbour_barrier(z, n, axis):
    barrier = pltpu.get_barrier_semaphore()
    @pl.when(z > 0)
    def _():
        pl.semaphore_signal(barrier, inc=1, device_id={axis: z - 1}, device_id_type=MESH)
    @pl.when(z < n - 1)
    def _():
        pl.semaphore_signal(barrier, inc=1, device_id={axis: z + 1}, device_id_type=MESH)
    ends = jnp.where(z > 0, 1, 0) + jnp.where(z < n - 1, 1, 0)
    pl.semaphore_wait(barrier, ends)

def rcopy(src, dst, ss, rs, dev):
    return pltpu.make_async_remote_copy(src_ref=src, dst_ref=dst, send_sem=ss, recv_sem=rs, device_id={"tensor": dev}, device_id_type=MESH)

def rs_kernel(n, R, lag, part, out, right, left, ss, rs):
    z = lax.axis_index("tensor")
    rows, w = out.shape; C = rows // R
    neighbour_barrier(z, n, "tensor")
    def at(ref, c, b):
        return ref.at[pl.ds(pl.multiple_of(c * R, R), R), pl.ds(b * w, w)]
    def body(t, _):
        for d, buf, step in ((0, right, 1), (1, left, -1)):
            p = z if d == 0 else n - 1 - z
            c = t - lag * p
            @pl.when((c >= 0) & (c < C))
            def _():
                r = pl.ds(pl.multiple_of(c * R, R), R)
                for b in (range(n - 1, 0, -1) if d == 0 else range(n - 1)):
                    on = (b > z) if d == 0 else (b < z)
                    k = pl.ds(b * w, w)
                    @pl.when(on)
                    def _():
                        @pl.when(p == 0)
                        def _():
                            rcopy(at(part, c, b), at(buf, c, b), ss.at[d, b, c], rs.at[d, b, c], z + step).start()
                        @pl.when(p > 0)
                        def _():
                            rcopy(at(buf, c, b), at(buf, c, b), ss.at[d, b, c], rs.at[d, b, c], z).wait_recv()
                            buf[r, k] = (part[r, k].astype(F32) + buf[r, k].astype(F32)).astype(BF)
                            rcopy(at(buf, c, b), at(buf, c, b), ss.at[d, b, c], rs.at[d, b, c], z + step).start()
        c = t - lag * (n - 1)
        @pl.when((c >= 0) & (c < C))
        def _():
            r = pl.ds(pl.multiple_of(c * R, R), R)
            for b in range(n):
                k = pl.ds(b * w, w)
                @pl.when(z == b)
                def _():
                    s = part[r, k].astype(F32)
                    if b > 0:
                        rcopy(at(right, c, b), at(right, c, b), ss.at[0, b, c], rs.at[0, b, c], z).wait_recv()
                        s = s + right[r, k].astype(F32)
                    if b < n - 1:
                        rcopy(at(left, c, b), at(left, c, b), ss.at[1, b, c], rs.at[1, b, c], z).wait_recv()
                        s = s + left[r, k].astype(F32)
                    out[r, :] = s.astype(BF)
        return 0
    lax.fori_loop(0, C + lag * (n - 1), body, 0)
    def drain(c, _):
        for d, buf in ((0, right), (1, left)):
            for b in range(n):
                @pl.when((b > z) if d == 0 else (b < z))
                def _():
                    rcopy(at(buf, c, b), at(buf, c, b), ss.at[d, b, c], rs.at[d, b, c], z).wait_send()
        return 0
    lax.fori_loop(0, C, drain, 0)

def rs(part, n, R=64, lag=1, cid=5):
    rows, nw = part.shape
    w = nw // n
    C = rows // R
    return pl.pallas_call(
        functools.partial(rs_kernel, n, R, lag),
        out_shape=jax.ShapeDtypeStruct((rows, w), BF),
        in_specs=[VM], out_specs=VM,
        scratch_shapes=[pltpu.VMEM((rows, nw), BF), pltpu.VMEM((rows, nw), BF)] + [pltpu.SemaphoreType.DMA((2, n, C))] * 2,
        compiler_params=pltpu.CompilerParams(collective_id=cid, has_side_effects=True, vmem_limit_bytes=60 << 20),
    )(part)


eps = 1e-05
rope_base = 10000.0


def nt(left, right):
    return lax.dot_general(left, right, (((1,), (1,)), ((), ())), preferred_element_type=F32)


def tn(left, right):
    return lax.dot_general(left, right, (((0,), (0,)), ((), ())), preferred_element_type=F32)


def mm(left, right):
    return jnp.dot(left, right, preferred_element_type=F32)


def spin(values, cosine, signed_sine):
    return values * cosine + pltpu.roll(values, HEAD_WIDTH // 2, 1) * signed_sine


def visible(code_row, code_col, low_col):
    return jnp.where((code_row <= code_col) & (code_row >= low_col), 0.0, -1e30)


def attend_kernel(tiles, x, gain, wq, wk, wv, wo, cosine, sine, code_row, code_col, low_col,
                  part, normed, q, k, v, o, lse):
    rows = x.shape[0]
    tile = rows // tiles
    heads = wq.shape[1] // HEAD_WIDTH
    kv = wk.shape[1] // HEAD_WIDTH
    group = heads // kv
    factor = math.log2(math.e) / math.sqrt(HEAD_WIDTH)
    for t in range(tiles):
        r = pl.ds(t * tile, tile)
        xt = x[r, :].astype(F32)
        scale = lax.rsqrt(jnp.mean(xt * xt, axis=1, keepdims=True) + eps)
        n1 = (xt * scale * gain[...]).astype(BF)
        normed[r, :] = n1
        c, s = cosine[r, :], sine[r, :]
        pre = mm(n1, wq[...])
        for h in range(heads):
            cut = slice(h * HEAD_WIDTH, (h + 1) * HEAD_WIDTH)
            q[r, cut] = spin(pre[:, cut], c, s).astype(BF)
        pre = mm(n1, wk[...])
        for h in range(kv):
            cut = slice(h * HEAD_WIDTH, (h + 1) * HEAD_WIDTH)
            k[r, cut] = spin(pre[:, cut], c, s).astype(BF)
        v[r, :] = mm(n1, wv[...]).astype(BF)
        seen = (t + 1) * tile
        bias = visible(code_row[:, :seen], code_col[r, :], low_col[r, :])
        logs = []
        for h in range(heads):
            cut = slice(h * HEAD_WIDTH, (h + 1) * HEAD_WIDTH)
            mine = slice(h // group * HEAD_WIDTH, (h // group + 1) * HEAD_WIDTH)
            scores = nt(q[r, cut], k[:seen, mine]) * factor + bias
            top = jnp.max(scores, axis=1, keepdims=True)
            expo = jnp.exp2(scores - top)
            total = jnp.sum(expo, axis=1, keepdims=True)
            probs = (expo * (1.0 / total)).astype(BF)
            o[r, cut] = mm(probs, v[:seen, mine]).astype(BF)
            logs.append(top + jnp.log2(total))
        lse[r, :] = jnp.concatenate(logs, axis=1)
        part[r, :] = mm(o[r, :], wo[...]).astype(BF)


def attend(tiles, x, gain, wq, wk, wv, wo, *tables):
    rows, width = x.shape
    heads = wq.shape[1] // HEAD_WIDTH
    shapes = [(rows, width), (rows, width), (rows, wq.shape[1]), (rows, wk.shape[1]), (rows, wv.shape[1]), (rows, wq.shape[1])]
    return pl.pallas_call(
        functools.partial(attend_kernel, tiles),
        out_shape=[jax.ShapeDtypeStruct(s, BF) for s in shapes] + [jax.ShapeDtypeStruct((rows, heads), F32)],
        in_specs=[VM] * 11,
        out_specs=[VM] * 7,
        compiler_params=pltpu.CompilerParams(vmem_limit_bytes=56 << 20),
    )(x, gain, wq, wk, wv, wo, *tables)


def attend_back_kernel(tiles, ga, wq, wk, wv, wo, q, k, v, o, lse, cosine, sine, code_row, code_col, low_col,
                       part, dqkv, dk, dv):
    rows = ga.shape[0]
    tile = rows // tiles
    heads = wq.shape[1] // HEAD_WIDTH
    kv = wk.shape[1] // HEAD_WIDTH
    group = heads // kv
    wide = heads * HEAD_WIDTH
    narrow = kv * HEAD_WIDTH
    score_scale = 1.0 / math.sqrt(HEAD_WIDTH)
    factor = math.log2(math.e) / math.sqrt(HEAD_WIDTH)
    for t in range(tiles):
        r = pl.ds(t * tile, tile)
        do = nt(ga[r, :], wo[...]).astype(BF)
        c, s = cosine[r, :], sine[r, :]
        seen = (t + 1) * tile
        bias = visible(code_row[:, :seen], code_col[r, :], low_col[r, :])
        logs = lse[r, :]
        for h in range(heads):
            cut = slice(h * HEAD_WIDTH, (h + 1) * HEAD_WIDTH)
            mine = slice(h // group * HEAD_WIDTH, (h // group + 1) * HEAD_WIDTH)
            do_h = do[:, cut]
            qh = q[r, cut]
            probs = jnp.exp2(nt(qh, k[:seen, mine]) * factor + bias - logs[:, h : h + 1])
            along = jnp.sum(do_h.astype(F32) * o[r, cut].astype(F32), axis=1, keepdims=True)
            ds = (probs * (nt(do_h, v[:seen, mine]) - along)).astype(BF)
            pb = probs.astype(BF)
            dq = mm(ds, k[:seen, mine]) * score_scale
            dqkv[r, cut] = spin(dq, c, -s).astype(BF)
            more_k = tn(ds, qh)
            more_v = tn(pb, do_h)
            if h % group == 0:
                if t > 0:
                    dk[: t * tile, mine] += more_k[: t * tile]
                    dv[: t * tile, mine] += more_v[: t * tile]
                dk[r, mine] = more_k[t * tile :]
                dv[r, mine] = more_v[t * tile :]
            else:
                dk[:seen, mine] += more_k
                dv[:seen, mine] += more_v
    for t in range(tiles):
        r = pl.ds(t * tile, tile)
        c, s = cosine[r, :], sine[r, :]
        for h in range(kv):
            cut = slice(h * HEAD_WIDTH, (h + 1) * HEAD_WIDTH)
            dqkv[r, wide + h * HEAD_WIDTH : wide + (h + 1) * HEAD_WIDTH] = spin(dk[r, cut] * score_scale, c, -s).astype(BF)
        dqkv[r, wide + narrow :] = dv[r, :].astype(BF)
        part[r, :] = (
            nt(dqkv[r, :wide], wq[...])
            + nt(dqkv[r, wide : wide + narrow], wk[...])
            + nt(dqkv[r, wide + narrow :], wv[...])
        ).astype(BF)


def attend_back(tiles, ga, wq, wk, wv, wo, *rest):
    rows, width = ga.shape
    joined = wq.shape[1] + wk.shape[1] + wv.shape[1]
    return pl.pallas_call(
        functools.partial(attend_back_kernel, tiles),
        out_shape=[jax.ShapeDtypeStruct((rows, width), BF), jax.ShapeDtypeStruct((rows, joined), BF)],
        in_specs=[VM] * 15,
        out_specs=[VM] * 2,
        scratch_shapes=[pltpu.VMEM((rows, wk.shape[1]), F32), pltpu.VMEM((rows, wv.shape[1]), F32)],
        compiler_params=pltpu.CompilerParams(vmem_limit_bytes=56 << 20),
    )(ga, wq, wk, wv, wo, *rest)


ANY = pl.BlockSpec(memory_space=pl.ANY)
LAG = 2
CHUNK = 32
BLOCK = 128


def line_row(f, c):
    per = BLOCK // CHUNK
    return pl.ds(pl.multiple_of(lax.div(c, per) * (2 * BLOCK) + f * BLOCK + lax.rem(c, per) * CHUNK, CHUNK), CHUNK)


def line_steps(n, rows):
    return rows // 2 // CHUNK + 2 * LAG * (n - 1)


def line_sum_step(n, z, t, part, up, out, sems):
    us, ur, ds, dr = sems
    count = part.shape[0] // 2 // CHUNK
    for f in range(2):
        p = z if f == 0 else n - 1 - z
        step = 1 if f == 0 else -1
        c = t - LAG * p

        @pl.when((c >= 0) & (c < count))
        def _():
            r = line_row(f, c)

            @pl.when(p == 0)
            def _():
                rcopy(part.at[r], up.at[r], us.at[f, c], ur.at[f, c], z + step).start()

            @pl.when(p > 0)
            def _():
                rcopy(up.at[r], up.at[r], us.at[f, c], ur.at[f, c], z).wait_recv()
                s = (part[r, :].astype(F32) + up[r, :].astype(F32)).astype(BF)

                @pl.when(p < n - 1)
                def _():
                    up[r, :] = s
                    rcopy(up.at[r], up.at[r], us.at[f, c], ur.at[f, c], z + step).start()

                @pl.when(p == n - 1)
                def _():
                    out[r, :] = s
                    rcopy(out.at[r], out.at[r], ds.at[f, c], dr.at[f, c], z - step).start()

    for f in range(2):
        p = z if f == 0 else n - 1 - z
        step = 1 if f == 0 else -1
        c = t - LAG * (2 * (n - 1) - p)

        @pl.when((c >= 0) & (c < count) & (p < n - 1))
        def _():
            r = line_row(f, c)
            rcopy(out.at[r], out.at[r], ds.at[f, c], dr.at[f, c], z).wait_recv()

            @pl.when(p > 0)
            def _():
                rcopy(out.at[r], out.at[r], ds.at[f, c], dr.at[f, c], z - step).start()


def line_sum_drain(n, z, part, up, out, sems):
    us, ur, ds, dr = sems
    count = part.shape[0] // 2 // CHUNK

    def drain(c, _):
        for f in range(2):
            p = z if f == 0 else n - 1 - z
            r = line_row(f, c)

            @pl.when(p < n - 1)
            def _():
                rcopy(up.at[r], up.at[r], us.at[f, c], ur.at[f, c], z).wait_send()

            @pl.when(p > 0)
            def _():
                rcopy(out.at[r], out.at[r], ds.at[f, c], dr.at[f, c], z).wait_send()

        return 0

    lax.fori_loop(0, count, drain, 0)


def line_sum_sems(rows):
    return [pltpu.SemaphoreType.DMA((2, rows // 2 // CHUNK))] * 4


def gather_cut(ref, o, c, w):
    return ref.at[pl.ds(pl.multiple_of(c * BLOCK, BLOCK), BLOCK), pl.ds(pl.multiple_of(o * w, w), w)]


def line_gather_step(n, z, t, src, out, ss, rs):
    rows, w = src.shape
    count = rows // BLOCK

    @pl.when(t < count)
    def _():
        mine = src.at[pl.ds(pl.multiple_of(t * BLOCK, BLOCK), BLOCK)]

        @pl.when(z < n - 1)
        def _():
            rcopy(mine, gather_cut(out, z, t, w), ss.at[0, z, t], rs.at[0, z, t], z + 1).start()

        @pl.when(z > 0)
        def _():
            rcopy(mine, gather_cut(out, z, t, w), ss.at[1, z, t], rs.at[1, z, t], z - 1).start()

    for hop in range(1, n):
        c = t - hop
        for d, step in ((0, 1), (1, -1)):
            o = z - hop * step

            @pl.when((c >= 0) & (c < count) & (o >= 0) & (o < n))
            def _():
                cut = gather_cut(out, o, c, w)
                rcopy(cut, cut, ss.at[d, o, c], rs.at[d, o, c], z).wait_recv()
                after = z + step

                @pl.when((after >= 0) & (after < n))
                def _():
                    rcopy(cut, cut, ss.at[d, o, c], rs.at[d, o, c], after).start()


def line_gather_drain(n, z, src, out, ss, rs):
    rows, w = src.shape

    def drain(c, _):
        for d in range(2):
            for o in range(n):
                on = (o <= z) & (z < n - 1) if d == 0 else (o >= z) & (z > 0)

                @pl.when(on)
                def _():
                    cut = gather_cut(out, o, c, w)
                    rcopy(cut, cut, ss.at[d, o, c], rs.at[d, o, c], z).wait_send()

        return 0

    lax.fori_loop(0, rows // BLOCK, drain, 0)


def middle_kernel(n, part, x, g_part, keep, gain, wg_far, wu_far, wd_far,
                  a_far, g_far, n2_far, inner_far, both_far, f_far, dn2_far,
                  wg, wu, wd, up, total, g, gate_s, upper_s, n2_s, inner_s, both_s, f_s, dn2_s,
                  us, ur, ds, dr, ss, rs, load, own, save, late):
    z = lax.axis_index("tensor")
    rows, width = part.shape
    w = g_part.shape[1]
    hidden = wg.shape[1]
    tile = 2 * BLOCK
    sums = (us, ur, ds, dr)
    loads = [pltpu.make_async_copy(a, b, load.at[i]) for i, (a, b) in enumerate(((wg_far, wg), (wu_far, wu), (wd_far, wd)))]
    for copy in loads:
        copy.start()
    mine = pltpu.make_async_copy(g_part, g.at[:, pl.ds(pl.multiple_of(z * w, w), w)], own)
    mine.start()
    neighbour_barrier(z, n, "tensor")

    def saves(d):
        r = pl.ds(pl.multiple_of(d * tile, tile), tile)
        pairs = ((n2_s, n2_far), (inner_s, inner_far), (both_s, both_far), (f_s, f_far), (dn2_s, dn2_far))
        return [pltpu.make_async_copy(a, b.at[r], save.at[i]) for i, (a, b) in enumerate(pairs)]

    first = BLOCK // CHUNK - 1 + 2 * LAG * (n - 1)

    def body(t, _):
        line_sum_step(n, z, t, part, up, total, sums)
        line_gather_step(n, z, t, g_part, g, ss, rs)
        q = t - first
        d = lax.div(jnp.maximum(q, 0), 4)
        k = lax.rem(jnp.maximum(q, 0), 4)
        r = pl.ds(pl.multiple_of(d * tile, tile), tile)

        @pl.when((q >= 0) & (k == 0))
        def _():
            @pl.when(d == 0)
            def _():
                for copy in loads:
                    copy.wait()
                mine.wait()

            @pl.when(d > 0)
            def _():
                for copy in saves(d - 1):
                    copy.wait()

            h = x[r, :].astype(F32) + keep[r, :] * total[r, :].astype(F32)
            scale = lax.rsqrt(jnp.mean(h * h, axis=1, keepdims=True) + eps)
            n2_s[...] = (h * scale * gain[...]).astype(BF)
            gate_s[...] = mm(n2_s[...], wg[...])

        @pl.when((q >= 0) & (k == 1))
        def _():
            upper_s[...] = mm(n2_s[...], wu[...])
            gate = gate_s[...]
            inner_s[...] = (gate * jax.nn.sigmoid(gate) * upper_s[...]).astype(BF)

        @pl.when((q >= 0) & (k == 2))
        def _():
            f_s[...] = mm(inner_s[...], wd[...]).astype(BF)
            gf = (keep[r, :] * g[r, :].astype(F32)).astype(BF)
            back = nt(gf, wd[...])
            gate = gate_s[...]
            s = jax.nn.sigmoid(gate)
            both_s[:, :hidden] = (back * upper_s[...] * s * (1.0 + gate * (1.0 - s))).astype(BF)
            both_s[:, hidden:] = (back * (gate * s)).astype(BF)

        @pl.when((q >= 0) & (k == 3))
        def _():
            dn2_s[...] = (nt(both_s[:, :hidden], wg[...]) + nt(both_s[:, hidden:], wu[...])).astype(BF)
            for copy in saves(d):
                copy.start()

        return 0

    lax.fori_loop(0, first + 4 * (rows // tile), body, 0)
    ends = [pltpu.make_async_copy(a, b, late.at[i]) for i, (a, b) in enumerate(((total, a_far), (g, g_far)))]
    for copy in ends:
        copy.start()
    line_sum_drain(n, z, part, up, total, sums)
    line_gather_drain(n, z, g_part, g, ss, rs)
    for copy in saves(rows // tile - 1) + ends:
        copy.wait()


def middle(n, part, x, g_part, keep, gain, wg, wu, wd):
    rows, width = part.shape
    hidden = wg.shape[1]
    tile = 2 * BLOCK
    blocks = rows // BLOCK
    widths = (width, width, width, hidden, 2 * hidden, width, width)
    return pl.pallas_call(
        functools.partial(middle_kernel, n),
        out_shape=[jax.ShapeDtypeStruct((rows, k), BF) for k in widths],
        in_specs=[VM] * 5 + [ANY] * 3,
        out_specs=[ANY] * 7,
        scratch_shapes=[
            pltpu.VMEM(wg.shape, BF),
            pltpu.VMEM(wu.shape, BF),
            pltpu.VMEM(wd.shape, BF),
            pltpu.VMEM((rows, width), BF),
            pltpu.VMEM((rows, width), BF),
            pltpu.VMEM((rows, width), BF),
            pltpu.VMEM((tile, hidden), F32),
            pltpu.VMEM((tile, hidden), F32),
            pltpu.VMEM((tile, width), BF),
            pltpu.VMEM((tile, hidden), BF),
            pltpu.VMEM((tile, 2 * hidden), BF),
            pltpu.VMEM((tile, width), BF),
            pltpu.VMEM((tile, width), BF),
            *line_sum_sems(rows),
            pltpu.SemaphoreType.DMA((2, n, blocks)),
            pltpu.SemaphoreType.DMA((2, n, blocks)),
            pltpu.SemaphoreType.DMA((3,)),
            pltpu.SemaphoreType.DMA,
            pltpu.SemaphoreType.DMA((5,)),
            pltpu.SemaphoreType.DMA((2,)),
        ],
        compiler_params=pltpu.CompilerParams(collective_id=3, has_side_effects=True, vmem_limit_bytes=62 << 20),
    )(part, x, g_part, keep, gain, wg, wu, wd)


def second_back_kernel(n, part, x, a, g, keep, gain, ga, dh, gain_grad, up, total, us, ur, ds, dr):
    z = lax.axis_index("tensor")
    rows, width = part.shape
    w = dh.shape[1]
    piece = BLOCK // 2
    sums = (us, ur, ds, dr)
    neighbour_barrier(z, n, "tensor")
    gain_grad[...] = jnp.zeros_like(gain_grad)
    first = BLOCK // CHUNK - 1 + 2 * LAG * (n - 1)

    def body(t, _):
        line_sum_step(n, z, t, part, up, total, sums)
        q = t - first

        @pl.when(q >= 0)
        def _():
            r = pl.ds(pl.multiple_of(q * piece, piece), piece)
            h = x[r, :].astype(F32) + keep[r, :] * a[r, :].astype(F32)
            scale = lax.rsqrt(jnp.mean(h * h, axis=1, keepdims=True) + eps)
            back = total[r, :].astype(F32)
            gain_grad[...] += jnp.sum(back * h * scale, axis=0, keepdims=True)
            e = back * gain[...]
            along = jnp.mean(e * h, axis=1, keepdims=True)
            full = g[r, :].astype(F32) + scale * e - h * (scale * scale * scale * along)
            ga[r, :] = (keep[r, :] * full).astype(BF)
            for b in range(n):

                @pl.when(z == b)
                def _():
                    dh[r, :] = full[:, b * w : (b + 1) * w]

        return 0

    lax.fori_loop(0, first + rows // piece, body, 0)
    line_sum_drain(n, z, part, up, total, sums)


def second_back_of(n, part, x, a, g, keep, gain):
    rows, width = part.shape
    return pl.pallas_call(
        functools.partial(second_back_kernel, n),
        out_shape=[
            jax.ShapeDtypeStruct((rows, width), BF),
            jax.ShapeDtypeStruct((rows, width // n), F32),
            jax.ShapeDtypeStruct((1, width), F32),
        ],
        in_specs=[VM] * 6,
        out_specs=[VM] * 3,
        scratch_shapes=[pltpu.VMEM((rows, width), BF), pltpu.VMEM((rows, width), BF), *line_sum_sems(rows)],
        compiler_params=pltpu.CompilerParams(collective_id=4, has_side_effects=True, vmem_limit_bytes=56 << 20),
    )(part, x, a, g, keep, gain)


def rotary_tables(token_positions, head_size):
    half = head_size // 2
    freqs = rope_base ** (-(jnp.arange(half).astype(jnp.float32) * 2.0) / head_size)
    angles = token_positions.astype(jnp.float32)[:, None] * freqs[None, :]
    angles = jnp.concatenate([angles, angles], axis=1)
    return (jnp.cos(angles), jnp.sin(angles))


def matmul(left, right):
    return jnp.dot(left, right, preferred_element_type=jnp.float32)


def per_device(
    tokens,
    cotangent,
    first_gain,
    query_weight,
    key_matrix,
    value_matrix,
    output_weight,
    second_gain,
    gate_weight,
    up_weight,
    down_weight,
    seq_lengths,
    owner_order,
    skip_mask,
):
    groups = lax.axis_size("dp")
    member = lax.axis_index("dp")
    width_part = tokens.shape[1]
    row_count = tokens.shape[0]
    per_owner = row_count // groups
    seq_count = seq_lengths.shape[0]
    seq_index = jnp.arange(seq_count, dtype=jnp.int32)
    before = (seq_index[None, :] < seq_index[:, None]).astype(jnp.int32)
    unit_lengths = seq_lengths // groups
    unit_starts = jnp.sum(before * unit_lengths[None, :], axis=1)
    placed = (owner_order[:, None] == seq_index[None, :]).astype(jnp.int32)
    order_lengths = jnp.sum(placed * unit_lengths[None, :], axis=1)
    order_starts = jnp.sum(placed * unit_starts[None, :], axis=1)
    order_keep = jnp.sum(placed * skip_mask[None, :], axis=1)
    order_before = jnp.sum(before * order_lengths[None, :], axis=1)
    places = jnp.arange(row_count, dtype=jnp.int32)
    covers = (
        (places[:, None] >= order_before[None, :])
        & (places[:, None] < (order_before + order_lengths)[None, :])
    ).astype(jnp.int32)
    send_rows = places + jnp.sum(covers * (order_starts - order_before)[None, :], axis=1)
    given_before = jnp.sum(placed * order_before[:, None], axis=0)
    given_covers = (
        (places[:, None] >= unit_starts[None, :])
        & (places[:, None] < (unit_starts + unit_lengths)[None, :])
    ).astype(jnp.int32)
    slot_of = places + jnp.sum(given_covers * (given_before - unit_starts)[None, :], axis=1)
    my_places = member * per_owner + jnp.arange(per_owner, dtype=jnp.int32)
    my_covers = (
        (my_places[:, None] >= order_before[None, :])
        & (my_places[:, None] < (order_before + order_lengths)[None, :])
    ).astype(jnp.int32)
    slot_seq = jnp.sum(my_covers * seq_index[None, :], axis=1)
    slot_step = my_places - jnp.sum(my_covers * order_before[None, :], axis=1)
    slot_keep = jnp.sum(my_covers * order_keep[None, :], axis=1)
    tiles = max(1, per_owner // 32)
    sources = jnp.arange(groups, dtype=jnp.int32)[None, :, None]

    def spread(values):
        values = values.reshape(tiles, 1, per_owner // tiles)
        return jnp.broadcast_to(values, (tiles, groups, per_owner // tiles)).reshape(row_count)

    token_positions = (
        sources + groups * slot_step.reshape(tiles, 1, per_owner // tiles)
    ).reshape(row_count)
    lowest = spread(slot_seq) * row_count
    code = lowest + token_positions
    keep_rows = spread(slot_keep).reshape(row_count, 1).astype(jnp.float32)
    chosen = (send_rows[:, None] == places[None, :]).astype(jnp.bfloat16)
    put_back = (slot_of[:, None] == places[None, :]).astype(jnp.bfloat16)

    def swap(values, first, second):
        return (
            values.reshape(first, second, per_owner // tiles, width_part)
            .transpose(1, 0, 2, 3)
            .reshape(row_count, width_part)
        )

    def to_owner(values):
        dealt = matmul(chosen, values).astype(jnp.bfloat16)
        return swap(
            lax.all_to_all(dealt, "dp", split_axis=0, concat_axis=0, tiled=True), groups, tiles
        )

    def to_given(values):
        back = lax.all_to_all(
            swap(values, tiles, groups), "dp", split_axis=0, concat_axis=0, tiled=True
        )
        return matmul(put_back, back).astype(jnp.bfloat16)

    owned_tokens = lax.all_gather(to_owner(tokens), "tensor", axis=1, tiled=True)
    part_cotangent = to_owner(cotangent)
    tensor_member = lax.axis_index("tensor")
    inputs = owned_tokens.astype(jnp.float32)

    def my_part(values):
        return lax.dynamic_slice_in_dim(values, tensor_member * width_part, width_part, 1)

    cosine, sine = rotary_tables(token_positions, HEAD_WIDTH)
    half = HEAD_WIDTH // 2
    tables = (
        cosine,
        jnp.concatenate([-sine[:, :half], sine[:, half:]], axis=1),
        code[None, :],
        code[:, None],
        lowest[:, None],
    )
    tensor_count = lax.axis_size("tensor")
    weights = (query_weight, key_matrix, value_matrix, output_weight)
    attn_part, normed_one, *kept = attend(
        tiles, owned_tokens, first_gain[None, :], *weights, *tables
    )
    attn_sum, owned_cotangent, normed_two, inner_low, both, ffn_term, second_term = middle(
        tensor_count,
        attn_part,
        owned_tokens,
        part_cotangent,
        keep_rows,
        second_gain[None, :],
        gate_weight,
        up_weight,
        down_weight,
    )
    ffn_out = lax.psum_scatter(ffn_term, "tensor", scatter_dimension=1, tiled=True)
    hidden_res = my_part(owned_tokens).astype(F32) + keep_rows * my_part(attn_sum).astype(F32)
    grad_ffn = (keep_rows * owned_cotangent.astype(F32)).astype(BF)
    hidden = gate_weight.shape[1]

    def shared(values):
        return lax.psum_scatter(
            values.astype(jnp.bfloat16), "dp", scatter_dimension=0, tiled=True
        ).astype(jnp.float32)

    both_grad = matmul(normed_two.T, both).astype(BF)
    down_grad = matmul(grad_ffn.T, inner_low).astype(BF)
    second_term, both_grad, down_grad = lax.optimization_barrier(
        (second_term, both_grad, down_grad)
    )
    both_share = shared(both_grad)
    grad_attn, grad_res, second_gain_grad = second_back_of(
        tensor_count,
        second_term,
        owned_tokens,
        attn_sum,
        owned_cotangent,
        keep_rows,
        second_gain[None, :],
    )
    grad_attn, ffn_out, both_share, down_grad = lax.optimization_barrier(
        (grad_attn, ffn_out, both_share, down_grad)
    )
    result = hidden_res + keep_rows * ffn_out.astype(F32)
    down_share = shared(down_grad)
    output_grad = matmul(grad_attn.T, kept[3])
    first_part, grad_joined = attend_back(tiles, grad_attn, *weights, *kept, *tables)
    first_back, down_share = lax.optimization_barrier((rs(first_part, tensor_count), down_share))
    first_back = first_back.astype(jnp.float32)
    joined_grad = matmul(normed_one.T, grad_joined)
    scale_one = lax.rsqrt(jnp.mean(inputs * inputs, axis=1, keepdims=True) + eps)
    my_inputs = my_part(inputs)
    first_gain_part = jnp.sum(first_back * my_inputs * scale_one, axis=0)
    scaled_one = first_back * lax.dynamic_slice_in_dim(
        first_gain, tensor_member * width_part, width_part, 0
    )
    along = lax.psum(jnp.sum(scaled_one * my_inputs, axis=1, keepdims=True), "tensor") / inputs.shape[1]
    grad_in = grad_res + scale_one * scaled_one - my_inputs * scale_one**3 * along
    out_part = result.astype(jnp.bfloat16)
    grad_part = grad_in.astype(jnp.bfloat16)
    out_part, grad_part = lax.optimization_barrier((out_part, grad_part))
    layer_output = to_given(out_part)
    input_grad = to_given(grad_part)
    gains = jnp.stack([first_gain_part, my_part(second_gain_grad)[0]])
    gains = lax.dynamic_update_slice_in_dim(
        jnp.zeros((2, inputs.shape[1]), jnp.float32), gains, tensor_member * width_part, 1
    )
    gains = lax.dynamic_slice_in_dim(
        lax.psum(gains, ("dp", "tensor")),
        member * (inputs.shape[1] // groups),
        inputs.shape[1] // groups,
        1,
    )

    output_share, first = shared(output_grad), shared(joined_grad)
    a = query_weight.shape[1]
    b = a + key_matrix.shape[1]
    summed = (
        gains[0],
        first[:, :a],
        first[:, a:b],
        first[:, b:],
        output_share.T,
        both_share[:, :hidden],
        both_share[:, hidden:],
        down_share.T,
        gains[1],
    )
    return (
        layer_output,
        input_grad,
        summed[0],
        summed[1],
        summed[2],
        summed[3],
        summed[4],
        summed[8],
        summed[5],
        summed[6],
        summed[7],
    )


def solution(mesh):
    placed = (
        P(None, ("dp", "tensor")),
        P(None, ("dp", "tensor")),
        P(),
        P(None, "tensor"),
        P(None, "tensor"),
        P(None, "tensor"),
        P("tensor", None),
        P(),
        P(None, "tensor"),
        P(None, "tensor"),
        P("tensor", None),
        P(),
        P(),
        P(),
    )
    return jax.shard_map(
        per_device,
        mesh=mesh,
        in_specs=placed,
        out_specs=(
            P(None, ("dp", "tensor")),
            P(None, ("dp", "tensor")),
            P("dp"),
            P("dp", "tensor"),
            P("dp", "tensor"),
            P("dp", "tensor"),
            P("tensor", "dp"),
            P("dp"),
            P("dp", "tensor"),
            P("dp", "tensor"),
            P("tensor", "dp"),
        ),
        check_vma=False,
    )
```

time: 1010 us -> 770 us (0.76)
  waiting for transfers between devices: 239 us -> 80.6 us
  matrix products: 191 us -> 51.3 us
  Pallas kernels: 372 us -> 482 us
  other arithmetic: 71.8 us -> 30.6 us
  local copies, waits for them, and re-layouts: 59.6 us -> 20.6 us
  blocking collectives: 41.4 us -> 72.8 us
    reduce_scatter x6 -> x5, waiting for transfers between devices: 155 us -> 5.81 us  [the longest x1 5.75 us: per_device(): lax.psum_scatter(ffn_term, 'tensor', scatter_dimension=1, tiled=True)]
    pallas_call x2 -> x4, Pallas kernels: 260 us -> 404 us  [the longest x1 188 us: middle(): pl.pallas_call(functools.partial(middle_kernel, n), out_shape=[jax.ShapeD...]
    dot_general x21 -> x8, matrix products: 148 us -> 51.3 us  [matmul(): return jnp.dot(left, right, preferred_element_type=jnp.float32)]
    dot_general x6 -> x0, matrix products: 43.1 us -> none  [the longest x1 13.8 us: per_device(): jnp.einsum('qcgd,kcd->cgqk', grad_attended_low, value_low, preferred_elem...]
    psum x0 -> x1, blocking collectives: none -> 40.7 us  [per_device(): lax.psum(gains, ('dp', 'tensor'))]
    pallas_call x1, Pallas kernels: 112 us -> 78.8 us  [rs(): pl.pallas_call(functools.partial(rs_kernel, n, R, lag), out_shape=jax.Sha...]
    gather x4 -> x0, local copies, waits for them, and re-layouts: 21.8 us -> none  [the longest x1 6.57 us: per_device(): tokens[send_rows]]
    reduce_sum x3 -> x0, other arithmetic: 19.8 us -> none  [the longest x1 8.07 us: per_device(): denominator = jnp.sum(expo, axis=-1, keepdims=True)]
  transfers between devices with their start and end apart: 11 -> 9, of which waited for: 6 -> 4; matrix products, arithmetic and copies ran while one was open for 24% -> 8% of each run, Pallas kernels for 26% -> 36%
where the time goes in v3:
time: 770 us; the launch traced here: 765 us
  Pallas kernels  482 us (63%)
  waiting for transfers between devices  80.6 us (10%)
  blocking collectives  72.8 us (9%)
  matrix products  51.3 us (7%)
  other arithmetic  30.6 us (4%)
  local copies, waits for them, and re-layouts  20.6 us (3%)
  between operations  14.6 us (2%)
  starting transfers between devices  12.1 us (2%)
    pallas_call x1, Pallas kernels, middle(): pl.pallas_call(functools.partial(middle_kernel, n), out_shape=[jax.ShapeD...  188 us
    pallas_call x1, Pallas kernels, second_back_of(): pl.pallas_call(functools.partial(second_back_kernel, n), out_shape=[jax.S...  169 us
    pallas_call x1, Pallas kernels, rs(): pl.pallas_call(functools.partial(rs_kernel, n, R, lag), out_shape=jax.Sha...  78.8 us
    all_gather x1, waiting for transfers between devices, per_device(): lax.all_gather(to_owner(tokens), 'tensor', axis=1, tiled=True)  58.1 us
    dot_general x8, matrix products, matmul(): return jnp.dot(left, right, preferred_element_type=jnp.float32)  51.3 us
    psum x1, blocking collectives, per_device(): lax.psum(gains, ('dp', 'tensor'))  40.7 us
    pallas_call x1, Pallas kernels, attend_back(): pl.pallas_call(functools.partial(attend_back_kernel, tiles), out_shape=[j...  24.9 us
    pallas_call x1, Pallas kernels, attend(): pl.pallas_call(functools.partial(attend_kernel, tiles), out_shape=[jax.Sh...  22 us
  transfers between devices with their start and end apart: 9, of which 4 were waited for; matrix products, arithmetic and copies ran while one was open for 8% of the time, Pallas kernels for 36%

profile of v3, /device:TPU:0, one launch (start us, length us, event | category | flops | bytes accessed | tf_op | source)
XLA Modules:
  0.0 764.9 jit_solution(9425813350316108580)
XLA Ops:
  7.2 0.7 and_select_fusion
  8.0 0.8 select_reduce_fusion.9
  8.8 0.1 select_reduce_fusion.8
  8.9 0.9 select_reduce_fusion.7
  9.8 0.1 select_reduce_fusion
  9.9 1.3 fusion.19
  11.3 20.5 %all_to_all.42 = bf16[8,128,512]{2,1,0:T(8,128)(2,1)S(1)} all-to-all(bf16[8,128,512]{2,1,0:T(8,128)(2,1)S(1)} %bitcast.49), channel_id=1, replica_groups=mesh['dp'=8,'tensor'=4] {'dp'}, dimensions={0} | all-to-all | bytes 2097152 | tf_op jit(solution)/shard_map/all_to_all | solution.py:647
  31.7 1.1 copy.51
  32.8 2.3 fusion.20
  35.1 3.6 all-to-all-start.1
  38.7 0.1 select_reduce_fusion.4
  38.8 0.1 reduce_sum.138
  38.9 0.1 mul.269
  39.1 1.3 convert_element_type.121.keep
  40.6 0.7 add.169.code_row
  41.5 1.0 copy.53.low_col
  42.5 1.0 copy.52.code_col
  43.5 0.2 broadcast_multiply_fusion
  43.7 3.0 fusion.21
  46.7 0.2 slice_negate_fusion
  47.0 1.0 pad_maximum_fusion.1.sine
  48.0 6.1 all-to-all-done.1
  54.0 1.0 copy.54
  55.1 58.1 %all-gather.2.cloned.1.call-done.x = bf16[1024,2048]{1,0:T(8,128)(2,1)} async-done(((bf16[1024,512]{1,0:T(8,128)(2,1)}), bf16[1024,2048]{1,0:T(8,128)(2,1)}) %all-gather.2.cloned.1.call-update) | async-done | bytes 4194320 | tf_op jit(solution)/shard_map/all_gather | solution.py:656
  113.1 22.0 %shard_map.221 = (bf16[1024,2048]{1,0:T(8,128)(2,1)}, bf16[1024,2048]{1,0:T(8,128)(2,1)}, bf16[1024,512]{1,0:T(8,128)(2,1)}, bf16[1024,128]{1,0:T(8,128)(2,1)}, ...) custom-call(bf16[1024,2048]{1,0:T(8,128)(2,1)} %all-gather.2.cloned.1.call-done.x, ...), custom_call_target="tpu_custom_call" | custom-call | tf_op jit(solution)/shard_map/pallas_call | solution.py:167
  135.1 188.0 %shard_map.222 = (bf16[1024,2048]{1,0:T(8,128)(2,1)}, bf16[1024,2048]{1,0:T(8,128)(2,1)}, bf16[1024,2048]{1,0:T(8,128)(2,1)}, bf16[1024,1408]{1,0:T(8,128)(2,1)}...) custom-call(bf16[1024,2048]{1,0:T(8,128)(2,1)} %get-tuple-element.41.part, ...), custom_call_target="tpu_custom_call" | custom-call | tf_op jit(solution)/shard_map/pallas_call | solution.py:474
  323.1 18.5 %convolution_convert_fusion = bf16[2048,2816]{1,0:T(8,128)(2,1)} fusion(bf16[1024,2048]{1,0:T(8,128)(2,1)} %get-tuple-element.44, bf16[1024,2816]{1,0:T(8,128)(2,1)} %get-tuple-element.45), kind=kOutput, calls=%fused_computation | convolution fusion | flops 11816927232 | bytes 21495808 | tf_op jit(solution)/shard_map/dot_general | solution.py:567
  341.6 11.2 %convolution_convert_fusion.1 = bf16[2048,1408]{1,0:T(8,128)(2,1)} fusion(bf16[1024,1408]{1,0:T(8,128)(2,1)} %get-tuple-element.47, bf16[1024,2048]{1,0:T(8,128)(2,1)} %get-tuple-element.46.g, f32[1024]{0:T(1024)S(1)} %convert_element_type.98), kind=kOutput, calls=%fused_computation.3 | convolution fusion | flops 5914755072 | bytes 12849152 | tf_op jit(solution)/shard_map/dot_general | solution.py:567
  352.8 0.7 reduce-scatter.6.cloned.1.call-update
  353.6 168.6 %shard_map.223 = (bf16[1024,2048]{1,0:T(8,128)(2,1)}, f32[1024,512]{1,0:T(8,128)}, f32[1,2048]{1,0:T(1,128)}) custom-call(bf16[1024,2048]{1,0:T(8,128)(2,1)} %get-tuple-element.48.part, bf16[1024,2048]{1,0:T(8,128)(2,1)} %all-gather.2.cloned.1.call-done.x, bf16[1024,2048]{1,0:T(8,128)(2,1)} %get-tuple-element.42.a, bf16[1024,2048]{1,0:T(8,128)(2,1)} %get-tuple-element.46.g, ...), custom_call_target="tpu_custom_call" | custom-call | tf_op jit(solution)/shard_map/pallas_call | solution.py:544
  522.2 3.2 convert_element_type.109
  525.4 5.7 reduce-scatter.6.cloned.1.call-done
  531.3 5.9 convolution_convert_fusion.3
  537.2 0.3 reduce-scatter.12.cloned.1.call-start
  537.5 24.9 %shard_map.224 = (bf16[1024,2048]{1,0:T(8,128)(2,1)}, bf16[1024,768]{1,0:T(8,128)(2,1)}) custom-call(bf16[1024,2048]{1,0:T(8,128)(2,1)} %get-tuple-element.55.ga, bf16[2048,512]{1,0:T(8,128)(2,1)} %wq.3, bf16[2048,128]{1,0:T(8,128)(2,1)} %wk.3, bf16[2048,128]{1,0:T(8,128)(2,1)} %wv.3, bf16[512,2048]{1,0:T(8,128)(2,1)} %wo.3, ...), custom_call_target="tpu_custom_call" | custom-call | tf_op jit(solution)/shard_map/pallas_call | solution.py:233
  562.4 6.3 convolution_convert_fusion.2
  568.8 0.8 dynamic_slice.20
  569.5 0.1 select_reduce_fusion.1
  569.7 6.6 convert_element_type.112
  576.3 0.9 multiply_reduce_fusion
  577.2 0.6 multiply_multiply_fusion
  577.8 78.8 %shard_map.225 = bf16[1024,512]{1,0:T(8,128)(2,1)} custom-call(bf16[1024,2048]{1,0:T(8,128)(2,1)} %get-tuple-element.61.part), custom_call_target="tpu_custom_call" | custom-call | tf_op jit(solution)/shard_map/pallas_call | solution.py:89
  656.6 2.2 add_convert_fusion
  658.9 1.2 convert_element_type.113
  660.1 3.0 fusion.12
  663.1 11.6 %psum.14 = f32[1024,1]{0,1:T(1,128)} all-reduce(f32[1024,1]{0,1:T(1,128)S(1)} %bitcast.52), channel_id=1, replica_groups=mesh['dp'=8,'tensor'=4] {'tensor'}, use_global_device_ids=true, to_apply=%region_16.17 | all-reduce | flops 1024 | bytes 8192 | tf_op jit(solution)/shard_map/psum | solution.py:730
  674.8 0.7 broadcast_multiply_fusion.1
  675.4 3.8 fusion.9
  679.2 1.0 copy.59
  680.3 3.7 all-to-all-start.2
  684.0 0.7 constant_dynamic-slice_fusion
  684.7 3.6 fusion.27
  688.3 1.1 copy.60
  689.4 9.9 %all-to-all-done.2 = bf16[8,128,512]{2,1,0:T(8,128)(2,1)S(1)} async-done(((bf16[8,128,512]{2,1,0:T(8,128)(2,1)}), bf16[8,128,512]{2,1,0:T(8,128)(2,1)S(1)}, u32[]{:S(2)}, u32[]{:S(2)}) %all-to-all-start.2) | async-done | bytes 1048608 | tf_op jit(solution)/shard_map/all_to_all | solution.py:651
  699.3 4.4 all-to-all-start.3
  703.7 1.0 convert_bitcast_fusion
  704.7 1.0 copy.61
  705.7 1.8 slice.38
  707.5 1.6 fusion.28
  709.1 1.5 copy.62
  710.7 40.7 %psum.15 = f32[2,2048]{1,0:T(2,128)S(1)} all-reduce(f32[2,2048]{1,0:T(2,128)S(1)} %maximum_dynamic-update-slice_fusion), channel_id=1, replica_groups=mesh['dp'=8,'tensor'=4] {'dp','tensor'}, use_global_device_ids=true, to_apply=%region_18.19 | all-reduce | flops 4096 | bytes 32768 | tf_op jit(solution)/shard_map/psum | solution.py:742
  751.4 0.6 fusion.29
  752.0 2.3 fusion.17
  754.3 3.6 fusion.18
  (57 shorter events, 0.9 us)
Async XLA Ops:
  7.2 2.8 copy-start
  7.2 105.9 %all-gather.2.cloned.1.call-start = ((), (), s32[]{:S(2)}) async-start(), calls=%async_computation.9 | async-start | bytes 5242880 | tf_op jit(solution)/shard_map/all_gather | solution.py:656
  11.2 21.6 %copy-start.10 = (bf16[1024,512]{1,0:T(8,128)(2,1)S(1)}, bf16[1024,512]{1,0:T(8,128)(2,1)}, u32[]{:S(2)}) copy-start(bf16[1024,512]{1,0:T(8,128)(2,1)} %param.15) | copy-start | bytes 3145732
  35.1 18.9 %all-to-all-start.1 = ((bf16[8,128,512]{2,1,0:T(8,128)(2,1)}), bf16[8,128,512]{2,1,0:T(8,128)(2,1)S(1)}, u32[]{:S(2)}, u32[]{:S(2)}) async-start(bf16[8,128,512]{2,1,0:T(8,128)(2,1)} %bitcast.5), calls=%async_computation.1 | async-start | bytes 2097152 | tf_op jit(solution)/shard_map/all_to_all | solution.py:647
  38.7 483.6 %reduce-scatter.8.cloned.1.call-start = ((), (), s32[]{:S(2)}) async-start(), calls=%async_computation.11 | async-start | bytes 12976128 | tf_op jit(solution)/shard_map/reduce_scatter | solution.py:695
  352.8 178.4 %reduce-scatter.6.cloned.1.call-start = ((), (), s32[]{:S(2)}) async-start(), calls=%async_computation.10 | async-start | bytes 5242880 | tf_op jit(solution)/shard_map/reduce_scatter | solution.py:689
  353.5 305.3 %reduce-scatter.10.cloned.1.call-start = ((), (), s32[]{:S(2)}) async-start(), calls=%async_computation.12 | async-start | bytes 6488064 | tf_op jit(solution)/shard_map/reduce_scatter | solution.py:695
  522.2 9.1 %copy-start.6 = (bf16[1024,512]{1,0:T(8,128)(2,1)S(1)}, bf16[1024,512]{1,0:T(8,128)(2,1)}, u32[]{:S(2)}) copy-start(bf16[1024,512]{1,0:T(8,128)(2,1)} %get-tuple-element.59.o) | copy-start | bytes 3145732
  531.2 172.5 %reduce-scatter.14.cloned.1.call-start = ((), (), s32[]{:S(2)}) async-start(), calls=%async_computation.14 | async-start | bytes 2359296 | tf_op jit(solution)/shard_map/reduce_scatter | solution.py:695
  537.2 168.5 %reduce-scatter.12.cloned.1.call-start = ((), (), s32[]{:S(2)}) async-start(), calls=%async_computation.13 | async-start | bytes 3538944 | tf_op jit(solution)/shard_map/reduce_scatter | solution.py:695
  537.5 24.9 %copy-start.9 = (bf16[1024,2048]{1,0:T(8,128)(2,1)S(1)}, bf16[1024,2048]{1,0:T(8,128)(2,1)}, u32[]{:S(2)}) copy-start(bf16[1024,2048]{1,0:T(8,128)(2,1)} %get-tuple-element.67) | copy-start | bytes 12582916
  562.4 7.1 copy-start.8
  569.6 6.6 copy-start.2
  576.3 80.3 %copy-start.5 = (bf16[1024,512]{1,0:T(8,128)(2,1)S(1)}, bf16[1024,512]{1,0:T(8,128)(2,1)}, u32[]{:S(2)}) copy-start(bf16[1024,512]{1,0:T(8,128)(2,1)} %reduce-scatter.6.cloned.1.call-done) | copy-start | bytes 3145732
  656.6 3.5 copy-start.3
  680.3 8.0 %copy-start.4 = (bf16[1024,512]{1,0:T(8,128)(2,1)S(1)}, bf16[1024,512]{1,0:T(8,128)(2,1)}, u32[]{:S(2)}) copy-start(bf16[1024,512]{1,0:T(8,128)(2,1)} %fusion.9) | copy-start | bytes 3145732
  680.3 19.0 %all-to-all-start.2 = ((bf16[8,128,512]{2,1,0:T(8,128)(2,1)}), bf16[8,128,512]{2,1,0:T(8,128)(2,1)S(1)}, u32[]{:S(2)}, u32[]{:S(2)}) async-start(bf16[8,128,512]{2,1,0:T(8,128)(2,1)} %bitcast.14), calls=%async_computation.5 | async-start | bytes 2097152 | tf_op jit(solution)/shard_map/all_to_all | solution.py:651
  699.3 11.3 %copy-start.7 = (f32[512]{0:T(512)S(1)}, f32[512]{0:T(512)}, u32[]{:S(2)}) copy-start(f32[512]{0:T(512)} %get-tuple-element.115) | copy-start | bytes 6148
  699.3 55.0 %all-to-all-start.3 = ((bf16[8,128,512]{2,1,0:T(8,128)(2,1)}), bf16[8,128,512]{2,1,0:T(8,128)(2,1)}, u32[]{:S(2)}, u32[]{:S(2)}) async-start(bf16[8,128,512]{2,1,0:T(8,128)(2,1)} %bitcast.18), calls=%async_computation.6 | async-start | bytes 2097152 | tf_op jit(solution)/shard_map/all_to_all | solution.py:651
  754.3 3.6 copy-start.1
Sparse Core Ops, SparseCore 0:
  32.9 80.1 all-gather.1
  352.9 84.9 reduce-scatter.7
  440.2 90.9 reduce-scatter.5
  534.9 58.3 reduce-scatter.9
  596.4 41.1 reduce-scatter.13
  641.2 46.2 reduce-scatter.11

commit v4 on v3

--- a/solution.py
+++ b/solution.py
@@ -29,71 +29,6 @@
 def rcopy(src, dst, ss, rs, dev):
     return pltpu.make_async_remote_copy(src_ref=src, dst_ref=dst, send_sem=ss, recv_sem=rs, device_id={"tensor": dev}, device_id_type=MESH)
 
-def rs_kernel(n, R, lag, part, out, right, left, ss, rs):
-    z = lax.axis_index("tensor")
-    rows, w = out.shape; C = rows // R
-    neighbour_barrier(z, n, "tensor")
-    def at(ref, c, b):
-        return ref.at[pl.ds(pl.multiple_of(c * R, R), R), pl.ds(b * w, w)]
-    def body(t, _):
-        for d, buf, step in ((0, right, 1), (1, left, -1)):
-            p = z if d == 0 else n - 1 - z
-            c = t - lag * p
-            @pl.when((c >= 0) & (c < C))
-            def _():
-                r = pl.ds(pl.multiple_of(c * R, R), R)
-                for b in (range(n - 1, 0, -1) if d == 0 else range(n - 1)):
-                    on = (b > z) if d == 0 else (b < z)
-                    k = pl.ds(b * w, w)
-                    @pl.when(on)
-                    def _():
-                        @pl.when(p == 0)
-                        def _():
-                            rcopy(at(part, c, b), at(buf, c, b), ss.at[d, b, c], rs.at[d, b, c], z + step).start()
-                        @pl.when(p > 0)
-                        def _():
-                            rcopy(at(buf, c, b), at(buf, c, b), ss.at[d, b, c], rs.at[d, b, c], z).wait_recv()
-                            buf[r, k] = (part[r, k].astype(F32) + buf[r, k].astype(F32)).astype(BF)
-                            rcopy(at(buf, c, b), at(buf, c, b), ss.at[d, b, c], rs.at[d, b, c], z + step).start()
-        c = t - lag * (n - 1)
-        @pl.when((c >= 0) & (c < C))
-        def _():
-            r = pl.ds(pl.multiple_of(c * R, R), R)
-            for b in range(n):
-                k = pl.ds(b * w, w)
-                @pl.when(z == b)
-                def _():
-                    s = part[r, k].astype(F32)
-                    if b > 0:
-                        rcopy(at(right, c, b), at(right, c, b), ss.at[0, b, c], rs.at[0, b, c], z).wait_recv()
-                        s = s + right[r, k].astype(F32)
-                    if b < n - 1:
-                        rcopy(at(left, c, b), at(left, c, b), ss.at[1, b, c], rs.at[1, b, c], z).wait_recv()
-                        s = s + left[r, k].astype(F32)
-                    out[r, :] = s.astype(BF)
-        return 0
-    lax.fori_loop(0, C + lag * (n - 1), body, 0)
-    def drain(c, _):
-        for d, buf in ((0, right), (1, left)):
-            for b in range(n):
-                @pl.when((b > z) if d == 0 else (b < z))
-                def _():
-                    rcopy(at(buf, c, b), at(buf, c, b), ss.at[d, b, c], rs.at[d, b, c], z).wait_send()
-        return 0
-    lax.fori_loop(0, C, drain, 0)
-
-def rs(part, n, R=64, lag=1, cid=5):
-    rows, nw = part.shape
-    w = nw // n
-    C = rows // R
-    return pl.pallas_call(
-        functools.partial(rs_kernel, n, R, lag),
-        out_shape=jax.ShapeDtypeStruct((rows, w), BF),
-        in_specs=[VM], out_specs=VM,
-        scratch_shapes=[pltpu.VMEM((rows, nw), BF), pltpu.VMEM((rows, nw), BF)] + [pltpu.SemaphoreType.DMA((2, n, C))] * 2,
-        compiler_params=pltpu.CompilerParams(collective_id=cid, has_side_effects=True, vmem_limit_bytes=60 << 20),
-    )(part)
-
 
 eps = 1e-05
 rope_base = 10000.0
@@ -120,7 +55,7 @@
 
 
 def attend_kernel(tiles, x, gain, wq, wk, wv, wo, cosine, sine, code_row, code_col, low_col,
-                  part, normed, q, k, v, o, lse):
+                  part, normed, q, k, v, o, lse, scales):
     rows = x.shape[0]
     tile = rows // tiles
     heads = wq.shape[1] // HEAD_WIDTH
@@ -131,6 +66,7 @@
         r = pl.ds(t * tile, tile)
         xt = x[r, :].astype(F32)
         scale = lax.rsqrt(jnp.mean(xt * xt, axis=1, keepdims=True) + eps)
+        scales[r, :] = scale
         n1 = (xt * scale * gain[...]).astype(BF)
         normed[r, :] = n1
         c, s = cosine[r, :], sine[r, :]
@@ -166,15 +102,15 @@
     shapes = [(rows, width), (rows, width), (rows, wq.shape[1]), (rows, wk.shape[1]), (rows, wv.shape[1]), (rows, wq.shape[1])]
     return pl.pallas_call(
         functools.partial(attend_kernel, tiles),
-        out_shape=[jax.ShapeDtypeStruct(s, BF) for s in shapes] + [jax.ShapeDtypeStruct((rows, heads), F32)],
+        out_shape=[jax.ShapeDtypeStruct(s, BF) for s in shapes] + [jax.ShapeDtypeStruct((rows, heads), F32), jax.ShapeDtypeStruct((rows, 1), F32)],
         in_specs=[VM] * 11,
-        out_specs=[VM] * 7,
+        out_specs=[VM] * 8,
         compiler_params=pltpu.CompilerParams(vmem_limit_bytes=56 << 20),
     )(x, gain, wq, wk, wv, wo, *tables)
 
 
-def attend_back_kernel(tiles, ga, wq, wk, wv, wo, q, k, v, o, lse, cosine, sine, code_row, code_col, low_col,
-                       part, dqkv, dk, dv):
+def attend_back_tile(t, tiles, ga, wq, wk, wv, wo, q, k, v, o, lse, cosine, sine, code_row, code_col, low_col,
+                     part, dqkv, dk, dv):
     rows = ga.shape[0]
     tile = rows // tiles
     heads = wq.shape[1] // HEAD_WIDTH
@@ -184,11 +120,12 @@
     narrow = kv * HEAD_WIDTH
     score_scale = 1.0 / math.sqrt(HEAD_WIDTH)
     factor = math.log2(math.e) / math.sqrt(HEAD_WIDTH)
-    for t in range(tiles):
-        r = pl.ds(t * tile, tile)
+    seen = (t + 1) * tile
+    block = min(tile, 256)
+    for at in range(t * tile, (t + 1) * tile, block):
+        r = pl.ds(at, block)
         do = nt(ga[r, :], wo[...]).astype(BF)
         c, s = cosine[r, :], sine[r, :]
-        seen = (t + 1) * tile
         bias = visible(code_row[:, :seen], code_col[r, :], low_col[r, :])
         logs = lse[r, :]
         for h in range(heads):
@@ -204,40 +141,25 @@
             dqkv[r, cut] = spin(dq, c, -s).astype(BF)
             more_k = tn(ds, qh)
             more_v = tn(pb, do_h)
-            if h % group == 0:
-                if t > 0:
-                    dk[: t * tile, mine] += more_k[: t * tile]
-                    dv[: t * tile, mine] += more_v[: t * tile]
-                dk[r, mine] = more_k[t * tile :]
-                dv[r, mine] = more_v[t * tile :]
+            if t == tiles - 1 and at == t * tile and h % group == 0:
+                dk[:seen, mine] = more_k
+                dv[:seen, mine] = more_v
             else:
                 dk[:seen, mine] += more_k
                 dv[:seen, mine] += more_v
-    for t in range(tiles):
-        r = pl.ds(t * tile, tile)
+    for at in range(t * tile, (t + 1) * tile, block):
+        r = pl.ds(at, block)
         c, s = cosine[r, :], sine[r, :]
         for h in range(kv):
             cut = slice(h * HEAD_WIDTH, (h + 1) * HEAD_WIDTH)
-            dqkv[r, wide + h * HEAD_WIDTH : wide + (h + 1) * HEAD_WIDTH] = spin(dk[r, cut] * score_scale, c, -s).astype(BF)
+            low = wide + h * HEAD_WIDTH
+            dqkv[r, low : low + HEAD_WIDTH] = spin(dk[r, cut] * score_scale, c, -s).astype(BF)
         dqkv[r, wide + narrow :] = dv[r, :].astype(BF)
         part[r, :] = (
             nt(dqkv[r, :wide], wq[...])
             + nt(dqkv[r, wide : wide + narrow], wk[...])
             + nt(dqkv[r, wide + narrow :], wv[...])
         ).astype(BF)
-
-
-def attend_back(tiles, ga, wq, wk, wv, wo, *rest):
-    rows, width = ga.shape
-    joined = wq.shape[1] + wk.shape[1] + wv.shape[1]
-    return pl.pallas_call(
-        functools.partial(attend_back_kernel, tiles),
-        out_shape=[jax.ShapeDtypeStruct((rows, width), BF), jax.ShapeDtypeStruct((rows, joined), BF)],
-        in_specs=[VM] * 15,
-        out_specs=[VM] * 2,
-        scratch_shapes=[pltpu.VMEM((rows, wk.shape[1]), F32), pltpu.VMEM((rows, wv.shape[1]), F32)],
-        compiler_params=pltpu.CompilerParams(vmem_limit_bytes=56 << 20),
-    )(ga, wq, wk, wv, wo, *rest)
 
 
 ANY = pl.BlockSpec(memory_space=pl.ANY)
@@ -382,9 +304,9 @@
 
 
 def middle_kernel(n, part, x, g_part, keep, gain, wg_far, wu_far, wd_far,
-                  a_far, g_far, n2_far, inner_far, both_far, f_far, dn2_far,
-                  wg, wu, wd, up, total, g, gate_s, upper_s, n2_s, inner_s, both_s, f_s, dn2_s,
-                  us, ur, ds, dr, ss, rs, load, own, save, late):
+                  result, a_far, g_far, n2_far, inner_far, both_far, dn2_far,
+                  wg, wu, wd, up, total, g, right, left, gate_s, upper_s, n2_s, inner_s, both_s, f_s, dn2_s,
+                  us, ur, ds, dr, ss, rs, fs, fr, load, own, save, late):
     z = lax.axis_index("tensor")
     rows, width = part.shape
     w = g_part.shape[1]
@@ -400,20 +322,24 @@
 
     def saves(d):
         r = pl.ds(pl.multiple_of(d * tile, tile), tile)
-        pairs = ((n2_s, n2_far), (inner_s, inner_far), (both_s, both_far), (f_s, f_far), (dn2_s, dn2_far))
+        pairs = ((n2_s, n2_far), (inner_s, inner_far), (both_s, both_far), (dn2_s, dn2_far))
         return [pltpu.make_async_copy(a, b.at[r], save.at[i]) for i, (a, b) in enumerate(pairs)]
 
     first = BLOCK // CHUNK - 1 + 2 * LAG * (n - 1)
 
     def body(t, _):
         line_sum_step(n, z, t, part, up, total, sums)
-        line_gather_step(n, z, t, g_part, g, ss, rs)
+
+        @pl.when(lax.rem(t, 2) == 0)
+        def _():
+            line_gather_step(n, z, lax.div(t, 2), g_part, g, ss, rs)
+
         q = t - first
         d = lax.div(jnp.maximum(q, 0), 4)
         k = lax.rem(jnp.maximum(q, 0), 4)
         r = pl.ds(pl.multiple_of(d * tile, tile), tile)
 
-        @pl.when((q >= 0) & (k == 0))
+        @pl.when((q >= 0) & (d < rows // tile) & (k == 0))
         def _():
             @pl.when(d == 0)
             def _():
@@ -431,15 +357,15 @@
             n2_s[...] = (h * scale * gain[...]).astype(BF)
             gate_s[...] = mm(n2_s[...], wg[...])
 
-        @pl.when((q >= 0) & (k == 1))
+        @pl.when((q >= 0) & (d < rows // tile) & (k == 1))
         def _():
             upper_s[...] = mm(n2_s[...], wu[...])
             gate = gate_s[...]
             inner_s[...] = (gate * jax.nn.sigmoid(gate) * upper_s[...]).astype(BF)
 
-        @pl.when((q >= 0) & (k == 2))
-        def _():
-            f_s[...] = mm(inner_s[...], wd[...]).astype(BF)
+        @pl.when((q >= 0) & (d < rows // tile) & (k == 2))
+        def _():
+            f_s[lax.rem(d, 2)] = mm(inner_s[...], wd[...]).astype(BF)
             gf = (keep[r, :] * g[r, :].astype(F32)).astype(BF)
             back = nt(gf, wd[...])
             gate = gate_s[...]
@@ -447,15 +373,86 @@
             both_s[:, :hidden] = (back * upper_s[...] * s * (1.0 + gate * (1.0 - s))).astype(BF)
             both_s[:, hidden:] = (back * (gate * s)).astype(BF)
 
-        @pl.when((q >= 0) & (k == 3))
+        @pl.when((q >= 0) & (d < rows // tile) & (k == 3))
         def _():
             dn2_s[...] = (nt(both_s[:, :hidden], wg[...]) + nt(both_s[:, hidden:], wu[...])).astype(BF)
             for copy in saves(d):
                 copy.start()
 
-        return 0
-
-    lax.fori_loop(0, first + 4 * (rows // tile), body, 0)
+        scatter_step(t - first - 2)
+        return 0
+
+    chunk = tile // 4
+    count = rows // chunk
+
+    def at(ref, c, b):
+        return ref.at[pl.ds(pl.multiple_of(c * chunk, chunk), chunk), pl.ds(b * w, w)]
+
+    def scatter_copy(buf, d, c, b, to):
+        return rcopy(at(buf, c, b), at(buf, c, b), fs.at[d, b, c], fr.at[d, b, c], to)
+
+    def scatter_step(s):
+        for d, buf, step in ((0, right, 1), (1, left, -1)):
+            p = z if d == 0 else n - 1 - z
+            c = s - p
+
+            @pl.when((c >= 0) & (c < count))
+            def _():
+                r = pl.ds(pl.multiple_of(c * chunk, chunk), chunk)
+                slot = lax.rem(lax.div(c, 4), 2)
+                inner = pl.ds(pl.multiple_of(lax.rem(c, 4) * chunk, chunk), chunk)
+                for b in range(n - 1, 0, -1) if d == 0 else range(n - 1):
+                    k = pl.ds(b * w, w)
+
+                    @pl.when((b > z) if d == 0 else (b < z))
+                    def _():
+                        @pl.when(p == 0)
+                        def _():
+                            buf[r, k] = f_s[slot, inner, k]
+
+                        @pl.when(p > 0)
+                        def _():
+                            scatter_copy(buf, d, c, b, z).wait_recv()
+                            buf[r, k] = (f_s[slot, inner, k].astype(F32) + buf[r, k].astype(F32)).astype(BF)
+
+                        scatter_copy(buf, d, c, b, z + step).start()
+
+        c = s - (n - 1)
+
+        @pl.when((c >= 0) & (c < count))
+        def _():
+            r = pl.ds(pl.multiple_of(c * chunk, chunk), chunk)
+            slot = lax.rem(lax.div(c, 4), 2)
+            inner = pl.ds(pl.multiple_of(lax.rem(c, 4) * chunk, chunk), chunk)
+            for b in range(n):
+                k = pl.ds(b * w, w)
+
+                @pl.when(z == b)
+                def _():
+                    f = f_s[slot, inner, k].astype(F32)
+                    if b > 0:
+                        scatter_copy(right, 0, c, b, z).wait_recv()
+                        f = f + right[r, k].astype(F32)
+                    if b < n - 1:
+                        scatter_copy(left, 1, c, b, z).wait_recv()
+                        f = f + left[r, k].astype(F32)
+                    kept = keep[r, :]
+                    h = x[r, k].astype(F32) + kept * total[r, k].astype(F32)
+                    result[r, :] = (h + kept * f).astype(BF)
+
+    lax.fori_loop(0, first + 2 + count + n, body, 0)
+
+    def drain(c, _):
+        for d, buf in ((0, right), (1, left)):
+            for b in range(n):
+
+                @pl.when((b > z) if d == 0 else (b < z))
+                def _():
+                    scatter_copy(buf, d, c, b, z).wait_send()
+
+        return 0
+
+    lax.fori_loop(0, count, drain, 0)
     ends = [pltpu.make_async_copy(a, b, late.at[i]) for i, (a, b) in enumerate(((total, a_far), (g, g_far)))]
     for copy in ends:
         copy.start()
@@ -470,16 +467,19 @@
     hidden = wg.shape[1]
     tile = 2 * BLOCK
     blocks = rows // BLOCK
-    widths = (width, width, width, hidden, 2 * hidden, width, width)
+    w = g_part.shape[1]
+    widths = (w, width, width, width, hidden, 2 * hidden, width)
     return pl.pallas_call(
         functools.partial(middle_kernel, n),
         out_shape=[jax.ShapeDtypeStruct((rows, k), BF) for k in widths],
         in_specs=[VM] * 5 + [ANY] * 3,
-        out_specs=[ANY] * 7,
+        out_specs=[VM] + [ANY] * 6,
         scratch_shapes=[
             pltpu.VMEM(wg.shape, BF),
             pltpu.VMEM(wu.shape, BF),
             pltpu.VMEM(wd.shape, BF),
+            pltpu.VMEM((rows, width), BF),
+            pltpu.VMEM((rows, width), BF),
             pltpu.VMEM((rows, width), BF),
             pltpu.VMEM((rows, width), BF),
             pltpu.VMEM((rows, width), BF),
@@ -488,17 +488,19 @@
             pltpu.VMEM((tile, width), BF),
             pltpu.VMEM((tile, hidden), BF),
             pltpu.VMEM((tile, 2 * hidden), BF),
-            pltpu.VMEM((tile, width), BF),
+            pltpu.VMEM((2, tile, width), BF),
             pltpu.VMEM((tile, width), BF),
             *line_sum_sems(rows),
             pltpu.SemaphoreType.DMA((2, n, blocks)),
             pltpu.SemaphoreType.DMA((2, n, blocks)),
+            pltpu.SemaphoreType.DMA((2, n, rows // tile * 4)),
+            pltpu.SemaphoreType.DMA((2, n, rows // tile * 4)),
             pltpu.SemaphoreType.DMA((3,)),
             pltpu.SemaphoreType.DMA,
-            pltpu.SemaphoreType.DMA((5,)),
+            pltpu.SemaphoreType.DMA((4,)),
             pltpu.SemaphoreType.DMA((2,)),
         ],
-        compiler_params=pltpu.CompilerParams(collective_id=3, has_side_effects=True, vmem_limit_bytes=62 << 20),
+        compiler_params=pltpu.CompilerParams(collective_id=3, has_side_effects=True, vmem_limit_bytes=63 << 20),
     )(part, x, g_part, keep, gain, wg, wu, wd)
 
 
@@ -553,6 +555,480 @@
         scratch_shapes=[pltpu.VMEM((rows, width), BF), pltpu.VMEM((rows, width), BF), *line_sum_sems(rows)],
         compiler_params=pltpu.CompilerParams(collective_id=4, has_side_effects=True, vmem_limit_bytes=56 << 20),
     )(part, x, a, g, keep, gain)
+
+
+def peers_barrier(z, n, me, groups, everyone):
+    barrier = pltpu.get_barrier_semaphore()
+
+    def greet(off, _):
+        peer = lax.rem(me + off, groups)
+        pl.semaphore_signal(barrier, inc=1, device_id={"dp": peer}, device_id_type=MESH)
+        return 0
+
+    lax.fori_loop(1, groups, greet, 0)
+    if everyone:
+        for off in range(1, n):
+            other = lax.rem(z + off, n)
+            pl.semaphore_signal(barrier, inc=1, device_id={"tensor": other}, device_id_type=MESH)
+        pl.semaphore_wait(barrier, groups - 1 + n - 1)
+    else:
+
+        @pl.when(z > 0)
+        def _():
+            pl.semaphore_signal(barrier, inc=1, device_id={"tensor": z - 1}, device_id_type=MESH)
+
+        @pl.when(z < n - 1)
+        def _():
+            pl.semaphore_signal(barrier, inc=1, device_id={"tensor": z + 1}, device_id_type=MESH)
+
+        ends = jnp.where(z > 0, 1, 0) + jnp.where(z < n - 1, 1, 0)
+        pl.semaphore_wait(barrier, groups - 1 + ends)
+
+
+def pcopy(src, dst, ss, rs, peer):
+    return pltpu.make_async_remote_copy(
+        src_ref=src, dst_ref=dst, send_sem=ss, recv_sem=rs, device_id={"dp": peer}, device_id_type=MESH
+    )
+
+
+def deal_in_kernel(n, groups, dealt_x, dealt_g, full, g_part, xs, xr, gs, gr, ss, rs, own):
+    z = lax.axis_index("tensor")
+    me = lax.axis_index("dp")
+    tiles, sub, w = dealt_x.shape[1:]
+    cols = pl.ds(pl.multiple_of(z * w, w), w)
+
+    def place(t, i):
+        return full.at[t, i, :, cols]
+
+    for t in range(tiles):
+        pltpu.make_async_copy(dealt_x.at[me, t], place(t, me), own.at[t]).start()
+    pltpu.make_async_copy(dealt_g.at[me], g_part.at[:, me], own.at[tiles]).start()
+    peers_barrier(z, n, me, groups, False)
+
+    def send(t):
+        def one(off, _):
+            peer = lax.rem(me + off, groups)
+            pcopy(dealt_x.at[peer, t], place(t, me), xs.at[t, peer], xr.at[t, me], peer).start()
+            return 0
+
+        lax.fori_loop(1, groups, one, 0)
+
+    def cut(o, t):
+        return full.at[t, :, :, pl.ds(pl.multiple_of(o * w, w), w)]
+
+    for t in range(tiles):
+        send(t)
+
+    def send_g(off, _):
+        peer = lax.rem(me + off, groups)
+        pcopy(dealt_g.at[peer], g_part.at[:, me], gs.at[peer], gr.at[me], peer).start()
+        return 0
+
+    lax.fori_loop(1, groups, send_g, 0)
+    for s in range(tiles + n - 1):
+        if s < tiles:
+
+            def got(off, _):
+                peer = lax.rem(me + off, groups)
+                pcopy(dealt_x.at[peer, s], place(s, peer), xs.at[s, peer], xr.at[s, peer], peer).wait_recv()
+                return 0
+
+            lax.fori_loop(1, groups, got, 0)
+            pltpu.make_async_copy(dealt_x.at[me, s], place(s, me), own.at[s]).wait()
+
+            @pl.when(z < n - 1)
+            def _():
+                rcopy(cut(z, s), cut(z, s), ss.at[0, z, s], rs.at[0, z, s], z + 1).start()
+
+            @pl.when(z > 0)
+            def _():
+                rcopy(cut(z, s), cut(z, s), ss.at[1, z, s], rs.at[1, z, s], z - 1).start()
+
+        for hop in range(1, n):
+            c = s - hop
+            if 0 <= c < tiles:
+                for d, step in ((0, 1), (1, -1)):
+                    o = z - hop * step
+
+                    @pl.when((o >= 0) & (o < n))
+                    def _():
+                        rcopy(cut(o, c), cut(o, c), ss.at[d, o, c], rs.at[d, o, c], z).wait_recv()
+                        after = z + step
+
+                        @pl.when((after >= 0) & (after < n))
+                        def _():
+                            rcopy(cut(o, c), cut(o, c), ss.at[d, o, c], rs.at[d, o, c], after).start()
+
+    def finish(off, _):
+        peer = lax.rem(me + off, groups)
+        copy = pcopy(dealt_g.at[peer], g_part.at[:, peer], gs.at[peer], gr.at[peer], peer)
+        copy.wait_recv()
+        copy.wait_send()
+        for t in range(tiles):
+            pcopy(dealt_x.at[peer, t], place(t, peer), xs.at[t, peer], xr.at[t, peer], peer).wait_send()
+        return 0
+
+    lax.fori_loop(1, groups, finish, 0)
+    pltpu.make_async_copy(dealt_g.at[me], g_part.at[:, me], own.at[tiles]).wait()
+    for c in range(tiles):
+        for d in range(2):
+            for o in range(n):
+
+                @pl.when((o <= z) & (z < n - 1) if d == 0 else (o >= z) & (z > 0))
+                def _():
+                    rcopy(cut(o, c), cut(o, c), ss.at[d, o, c], rs.at[d, o, c], z).wait_send()
+
+
+def deal_in(n, groups, dealt_x, dealt_g):
+    tiles, sub, w = dealt_x.shape[1:]
+    dma = pltpu.SemaphoreType.DMA
+    return pl.pallas_call(
+        functools.partial(deal_in_kernel, n, groups),
+        out_shape=[
+            jax.ShapeDtypeStruct((tiles, groups, sub, n * w), BF),
+            jax.ShapeDtypeStruct((tiles, groups, sub, w), BF),
+        ],
+        in_specs=[VM] * 2,
+        out_specs=[VM] * 2,
+        scratch_shapes=[
+            dma((tiles, groups)),
+            dma((tiles, groups)),
+            dma((groups,)),
+            dma((groups,)),
+            dma((2, n, tiles)),
+            dma((2, n, tiles)),
+            dma((tiles + 1,)),
+        ],
+        compiler_params=pltpu.CompilerParams(collective_id=6, has_side_effects=True, vmem_limit_bytes=48 << 20),
+    )(dealt_x, dealt_g)
+
+
+def exact(left, right, contract):
+    return lax.dot_general(
+        left, right, (contract, ((), ())), preferred_element_type=F32, precision=lax.Precision.HIGHEST
+    )
+
+
+def deal_out_kernel(n, groups, tiles, chunk, lag, x, dh, scale1, gain1, result, gain2, normed, *refs):
+    attention = refs[:15]
+    (back_out, back_dx, gains, shares, part, dqkv, dk, dv, right, left, fb, dx, lines, widths, gsrc, gdst, wsrc, wdst,
+     ss, rs, os, orr, xs, xr, ls, lr, ws, wr, es, er, qs, qr, own) = refs[15:]
+    ga, o = attention[0], attention[8]
+    z = lax.axis_index("tensor")
+    me = lax.axis_index("dp")
+    rows, w = x.shape
+    tile = rows // tiles
+    count = rows // chunk
+    per = tile // chunk
+    sub = result.shape[2]
+    pltpu.make_async_copy(result.at[:, me], back_out.at[me], own.at[0]).start()
+    peers_barrier(z, n, me, groups, True)
+
+    def send_out(off, _):
+        peer = lax.rem(me + off, groups)
+        pcopy(result.at[:, peer], back_out.at[me], os.at[peer], orr.at[me], peer).start()
+        return 0
+
+    lax.fori_loop(1, groups, send_out, 0)
+
+    def chunk_rows(c):
+        t = tiles - 1 - lax.div(c, per)
+        return pl.ds(pl.multiple_of(t * tile + lax.rem(c, per) * chunk, chunk), chunk)
+
+    def at(ref, c, b):
+        return ref.at[chunk_rows(c), pl.ds(b * w, w)]
+
+    widths[...] = jnp.zeros_like(widths)
+
+    def others(f):
+        for off in range(1, n):
+            f(lax.rem(z + off, n))
+
+    def line_copy(t, slot, other):
+        cut = lines.at[slot, :, pl.ds(pl.multiple_of(t * tile, tile), tile)]
+        return rcopy(cut, cut, ls.at[other, t], lr.at[slot, t], other)
+
+    def width_copy(slot, other):
+        cut = widths.at[slot]
+        return rcopy(cut, cut, ws.at[other], wr.at[slot], other)
+
+    def open_tile(t):
+        r = pl.ds(pl.multiple_of(t * tile, tile), tile)
+        e = fb[r, :] * gain1[...]
+        xt = x[r, :].astype(F32)
+        lines[z, :, r] = exact(jnp.ones((8, w), F32), e * xt, ((1,), (1,)))
+        others(lambda other: line_copy(t, z, other).start())
+        grown = jnp.sum(fb[r, :] * xt * scale1[r, :], axis=0, keepdims=True)
+        widths[z, :, :] += jnp.broadcast_to(grown, (8, w))
+
+        @pl.when(t == 0)
+        def _():
+            others(lambda other: width_copy(z, other).start())
+
+    def close_tile(t):
+        r = pl.ds(pl.multiple_of(t * tile, tile), tile)
+        others(lambda other: line_copy(t, other, other).wait_recv())
+        total = lines[0, :, r]
+        for j in range(1, n):
+            total = total + lines[j, :, r]
+        along = exact(total * (1.0 / (8 * n * w)), jnp.ones((8, w), F32), ((0,), (0,)))
+        e = fb[r, :] * gain1[...]
+        s = scale1[r, :]
+        full = dh[r, :] + s * e - x[r, :].astype(F32) * (s * s * s * along)
+        dx[t] = full.astype(BF).reshape(groups, sub, w)
+        pltpu.make_async_copy(dx.at[t, me], back_dx.at[me, t], own.at[1 + t]).start()
+
+        def one(off, _):
+            peer = lax.rem(me + off, groups)
+            pcopy(dx.at[t, peer], back_dx.at[me, t], xs.at[t, peer], xr.at[t, me], peer).start()
+            return 0
+
+        lax.fori_loop(1, groups, one, 0)
+
+    ow = o.shape[1]
+    share = normed.shape[1] // groups
+    span = max(share, 256)
+
+    def weigh(left_ref, right_ref, at_column, kind):
+        def one(j, _):
+            base = lax.rem(j + lax.div(me * share, span), normed.shape[1] // span) * span
+            cut = pl.ds(pl.multiple_of(base, span), span)
+            wide = right_ref.shape[1]
+            wsrc[cut, at_column : at_column + wide] = tn(left_ref[:, cut], right_ref[...]).astype(BF)
+            for i in range(span // share):
+                peer = lax.div(base, share) + i
+
+                @pl.when(peer != me)
+                def _():
+                    weight_copy(kind, peer, me, peer, at_column, wide).start()
+
+                @pl.when(peer == me)
+                def _():
+                    weight_own(kind, at_column, wide).start()
+
+            return 0
+
+        lax.fori_loop(0, normed.shape[1] // span, one, 0)
+
+    def weight_copy(kind, block, slot, peer, at_column, wide):
+        columns = pl.ds(at_column, wide)
+        return pltpu.make_async_remote_copy(
+            src_ref=wsrc.at[pl.ds(pl.multiple_of(block * share, share), share), columns],
+            dst_ref=wdst.at[slot, :, columns],
+            send_sem=qs.at[kind, block],
+            recv_sem=qr.at[kind, slot],
+            device_id={"dp": peer},
+            device_id_type=MESH,
+        )
+
+    def weight_own(kind, at_column, wide):
+        columns = pl.ds(at_column, wide)
+        return pltpu.make_async_copy(
+            wsrc.at[pl.ds(pl.multiple_of(me * share, share), share), columns],
+            wdst.at[me, :, columns],
+            own.at[2 + tiles + kind],
+        )
+
+    def flows(s, _):
+        for k in range(tiles):
+
+            @pl.when(s == k * per)
+            def _():
+                attend_back_tile(tiles - 1 - k, tiles, *attention, part, dqkv, dk, dv)
+
+        @pl.when(s == 2)
+        def _():
+            weigh(ga, o, 0, 0)
+
+        @pl.when(s == (tiles - 1) * per + 1)
+        def _():
+            weigh(normed, dqkv, ow, 1)
+
+        for d, buf, step in ((0, right, 1), (1, left, -1)):
+            p = z if d == 0 else n - 1 - z
+            c = s - lag * p
+
+            @pl.when((c >= 0) & (c < count))
+            def _():
+                r = chunk_rows(c)
+                for b in range(n - 1, 0, -1) if d == 0 else range(n - 1):
+                    k = pl.ds(b * w, w)
+
+                    @pl.when((b > z) if d == 0 else (b < z))
+                    def _():
+                        @pl.when(p == 0)
+                        def _():
+                            rcopy(at(part, c, b), at(buf, c, b), ss.at[d, b, c], rs.at[d, b, c], z + step).start()
+
+                        @pl.when(p > 0)
+                        def _():
+                            rcopy(at(buf, c, b), at(buf, c, b), ss.at[d, b, c], rs.at[d, b, c], z).wait_recv()
+                            buf[r, k] = (part[r, k].astype(F32) + buf[r, k].astype(F32)).astype(BF)
+                            rcopy(at(buf, c, b), at(buf, c, b), ss.at[d, b, c], rs.at[d, b, c], z + step).start()
+
+        c = s - lag * (n - 1)
+
+        @pl.when((c >= 0) & (c < count))
+        def _():
+            r = chunk_rows(c)
+            for b in range(n):
+                k = pl.ds(b * w, w)
+
+                @pl.when(z == b)
+                def _():
+                    total = part[r, k].astype(F32)
+                    if b > 0:
+                        rcopy(at(right, c, b), at(right, c, b), ss.at[0, b, c], rs.at[0, b, c], z).wait_recv()
+                        total = total + right[r, k].astype(F32)
+                    if b < n - 1:
+                        rcopy(at(left, c, b), at(left, c, b), ss.at[1, b, c], rs.at[1, b, c], z).wait_recv()
+                        total = total + left[r, k].astype(F32)
+                    fb[r, :] = total
+
+        @pl.when((c >= 0) & (c < count) & (lax.rem(jnp.maximum(c, 0), per) == per - 1))
+        def _():
+            open_tile(tiles - 1 - lax.div(c, per))
+
+        c = c - 2
+
+        @pl.when((c >= 0) & (lax.rem(jnp.maximum(c, 0), per) == per - 1))
+        def _():
+            close_tile(tiles - 1 - lax.div(c, per))
+
+        return 0
+
+    lax.fori_loop(0, count + lag * (n - 1) + 2, flows, 0)
+
+    others(lambda other: width_copy(other, other).wait_recv())
+    cols = gsrc.shape[2]
+    first_gain = jnp.concatenate([widths[j] for j in range(n)], axis=1)
+    second_gain = jnp.broadcast_to(gain2[...], first_gain.shape)
+    for i in range(groups):
+        gsrc[i, :8, :] = first_gain[:, i * cols : (i + 1) * cols]
+        gsrc[i, 8:, :] = second_gain[:, i * cols : (i + 1) * cols]
+    pltpu.make_async_copy(gsrc.at[me], gdst.at[me], own.at[1 + tiles]).start()
+
+    def send_gain(off, _):
+        peer = lax.rem(me + off, groups)
+        pcopy(gsrc.at[peer], gdst.at[me], es.at[peer], er.at[me], peer).start()
+        return 0
+
+    lax.fori_loop(1, groups, send_gain, 0)
+
+    def got_gain(off, _):
+        peer = lax.rem(me + off, groups)
+        copy = pcopy(gsrc.at[peer], gdst.at[peer], es.at[peer], er.at[peer], peer)
+        copy.wait_recv()
+        copy.wait_send()
+        return 0
+
+    lax.fori_loop(1, groups, got_gain, 0)
+    pltpu.make_async_copy(gsrc.at[me], gdst.at[me], own.at[1 + tiles]).wait()
+    total = gdst[0]
+    for i in range(1, groups):
+        total = total + gdst[i]
+    gains[...] = total
+
+    def got_weight(off, _):
+        peer = lax.rem(me + off, groups)
+        for kind, (at_column, wide) in enumerate(((0, ow), (ow, dqkv.shape[1]))):
+            copy = weight_copy(kind, peer, peer, peer, at_column, wide)
+            copy.wait_recv()
+            copy.wait_send()
+        return 0
+
+    lax.fori_loop(1, groups, got_weight, 0)
+    weight_own(0, 0, ow).wait()
+    weight_own(1, ow, dqkv.shape[1]).wait()
+    shares[...] = wdst[0].astype(F32)
+    for i in range(1, groups):
+        shares[...] += wdst[i].astype(F32)
+
+    def finish(off, _):
+        peer = lax.rem(me + off, groups)
+        copy = pcopy(result.at[:, peer], back_out.at[peer], os.at[peer], orr.at[peer], peer)
+        copy.wait_recv()
+        copy.wait_send()
+        for t in range(tiles):
+            copy = pcopy(dx.at[t, peer], back_dx.at[peer, t], xs.at[t, peer], xr.at[t, peer], peer)
+            copy.wait_recv()
+            copy.wait_send()
+        return 0
+
+    lax.fori_loop(1, groups, finish, 0)
+    pltpu.make_async_copy(result.at[:, me], back_out.at[me], own.at[0]).wait()
+    for t in range(tiles):
+        pltpu.make_async_copy(dx.at[t, me], back_dx.at[me, t], own.at[1 + t]).wait()
+        others(lambda other: line_copy(t, z, other).wait_send())
+    others(lambda other: width_copy(z, other).wait_send())
+
+    def drain(c, _):
+        for d, buf in ((0, right), (1, left)):
+            for b in range(n):
+
+                @pl.when((b > z) if d == 0 else (b < z))
+                def _():
+                    rcopy(at(buf, c, b), at(buf, c, b), ss.at[d, b, c], rs.at[d, b, c], z).wait_send()
+
+        return 0
+
+    lax.fori_loop(0, count, drain, 0)
+
+
+def deal_out(n, groups, tiles, x, dh, scale1, gain1, result, gain2, normed, *attention, chunk=64, lag=2):
+    rows, w = x.shape
+    width = n * w
+    sub = rows // tiles // groups
+    count = rows // chunk
+    cols = width // groups
+    joined = sum(a.shape[1] for a in attention[1:4])
+    narrow = attention[2].shape[1]
+    both = attention[8].shape[1] + joined
+    dma = pltpu.SemaphoreType.DMA
+    dealt = (groups, tiles, sub, w)
+    return pl.pallas_call(
+        functools.partial(deal_out_kernel, n, groups, tiles, chunk, lag),
+        out_shape=[
+            jax.ShapeDtypeStruct(dealt, BF),
+            jax.ShapeDtypeStruct(dealt, BF),
+            jax.ShapeDtypeStruct((16, cols), F32),
+            jax.ShapeDtypeStruct((cols, both), F32),
+        ],
+        in_specs=[VM] * 22,
+        out_specs=[VM] * 4,
+        scratch_shapes=[
+            pltpu.VMEM((rows, width), BF),
+            pltpu.VMEM((rows, joined), BF),
+            pltpu.VMEM((rows, narrow), F32),
+            pltpu.VMEM((rows, narrow), F32),
+            pltpu.VMEM((rows, width), BF),
+            pltpu.VMEM((rows, width), BF),
+            pltpu.VMEM((rows, w), F32),
+            pltpu.VMEM((tiles, groups, sub, w), BF),
+            pltpu.VMEM((n, 8, rows), F32),
+            pltpu.VMEM((n, 8, w), F32),
+            pltpu.VMEM((groups, 16, cols), F32),
+            pltpu.VMEM((groups, 16, cols), F32),
+            pltpu.VMEM((width, both), BF),
+            pltpu.VMEM((groups, cols, both), BF),
+            dma((2, n, count)),
+            dma((2, n, count)),
+            dma((groups,)),
+            dma((groups,)),
+            dma((tiles, groups)),
+            dma((tiles, groups)),
+            dma((n, tiles)),
+            dma((n, tiles)),
+            dma((n,)),
+            dma((n,)),
+            dma((groups,)),
+            dma((groups,)),
+            dma((2, groups)),
+            dma((2, groups)),
+            dma((tiles + 4,)),
+        ],
+        compiler_params=pltpu.CompilerParams(collective_id=5, has_side_effects=True, vmem_limit_bytes=62 << 20),
+    )(x, dh, scale1, gain1, result.reshape(tiles, groups, sub, w), gain2, normed, *attention)
 
 
 def rotary_tables(token_positions, head_size):
@@ -634,29 +1110,19 @@
     chosen = (send_rows[:, None] == places[None, :]).astype(jnp.bfloat16)
     put_back = (slot_of[:, None] == places[None, :]).astype(jnp.bfloat16)
 
-    def swap(values, first, second):
-        return (
-            values.reshape(first, second, per_owner // tiles, width_part)
-            .transpose(1, 0, 2, 3)
-            .reshape(row_count, width_part)
-        )
-
-    def to_owner(values):
-        dealt = matmul(chosen, values).astype(jnp.bfloat16)
-        return swap(
-            lax.all_to_all(dealt, "dp", split_axis=0, concat_axis=0, tiled=True), groups, tiles
-        )
-
-    def to_given(values):
-        back = lax.all_to_all(
-            swap(values, tiles, groups), "dp", split_axis=0, concat_axis=0, tiled=True
-        )
-        return matmul(put_back, back).astype(jnp.bfloat16)
-
-    owned_tokens = lax.all_gather(to_owner(tokens), "tensor", axis=1, tiled=True)
-    part_cotangent = to_owner(cotangent)
+    tensor_count = lax.axis_size("tensor")
     tensor_member = lax.axis_index("tensor")
-    inputs = owned_tokens.astype(jnp.float32)
+    dealt_shape = (groups, tiles, per_owner // tiles, width_part)
+    owned_tokens, part_cotangent = deal_in(
+        tensor_count,
+        groups,
+        *(
+            matmul(chosen, values).astype(BF).reshape(dealt_shape)
+            for values in (tokens, cotangent)
+        ),
+    )
+    owned_tokens = owned_tokens.reshape(row_count, -1)
+    part_cotangent = part_cotangent.reshape(row_count, width_part)
 
     def my_part(values):
         return lax.dynamic_slice_in_dim(values, tensor_member * width_part, width_part, 1)
@@ -670,12 +1136,11 @@
         code[:, None],
         lowest[:, None],
     )
-    tensor_count = lax.axis_size("tensor")
     weights = (query_weight, key_matrix, value_matrix, output_weight)
-    attn_part, normed_one, *kept = attend(
+    attn_part, normed_one, *kept, scale_one = attend(
         tiles, owned_tokens, first_gain[None, :], *weights, *tables
     )
-    attn_sum, owned_cotangent, normed_two, inner_low, both, ffn_term, second_term = middle(
+    result, attn_sum, owned_cotangent, normed_two, inner_low, both, second_term = middle(
         tensor_count,
         attn_part,
         owned_tokens,
@@ -686,8 +1151,6 @@
         up_weight,
         down_weight,
     )
-    ffn_out = lax.psum_scatter(ffn_term, "tensor", scatter_dimension=1, tiled=True)
-    hidden_res = my_part(owned_tokens).astype(F32) + keep_rows * my_part(attn_sum).astype(F32)
     grad_ffn = (keep_rows * owned_cotangent.astype(F32)).astype(BF)
     hidden = gate_weight.shape[1]
 
@@ -696,12 +1159,13 @@
             values.astype(jnp.bfloat16), "dp", scatter_dimension=0, tiled=True
         ).astype(jnp.float32)
 
+    down_grad = matmul(grad_ffn.T, inner_low).astype(BF)
+    down_grad, normed_two = lax.optimization_barrier((down_grad, normed_two))
     both_grad = matmul(normed_two.T, both).astype(BF)
-    down_grad = matmul(grad_ffn.T, inner_low).astype(BF)
     second_term, both_grad, down_grad = lax.optimization_barrier(
         (second_term, both_grad, down_grad)
     )
-    both_share = shared(both_grad)
+    both_share, down_share = shared(both_grad), shared(down_grad)
     grad_attn, grad_res, second_gain_grad = second_back_of(
         tensor_count,
         second_term,
@@ -711,53 +1175,39 @@
         keep_rows,
         second_gain[None, :],
     )
-    grad_attn, ffn_out, both_share, down_grad = lax.optimization_barrier(
-        (grad_attn, ffn_out, both_share, down_grad)
+    down_share, grad_attn = lax.optimization_barrier((down_share, grad_attn))
+    back_out, back_grad, gains, first = deal_out(
+        tensor_count,
+        groups,
+        tiles,
+        my_part(owned_tokens),
+        grad_res,
+        scale_one,
+        my_part(first_gain[None, :]),
+        result,
+        second_gain_grad,
+        normed_one,
+        grad_attn,
+        *weights,
+        *kept,
+        *tables,
     )
-    result = hidden_res + keep_rows * ffn_out.astype(F32)
-    down_share = shared(down_grad)
-    output_grad = matmul(grad_attn.T, kept[3])
-    first_part, grad_joined = attend_back(tiles, grad_attn, *weights, *kept, *tables)
-    first_back, down_share = lax.optimization_barrier((rs(first_part, tensor_count), down_share))
-    first_back = first_back.astype(jnp.float32)
-    joined_grad = matmul(normed_one.T, grad_joined)
-    scale_one = lax.rsqrt(jnp.mean(inputs * inputs, axis=1, keepdims=True) + eps)
-    my_inputs = my_part(inputs)
-    first_gain_part = jnp.sum(first_back * my_inputs * scale_one, axis=0)
-    scaled_one = first_back * lax.dynamic_slice_in_dim(
-        first_gain, tensor_member * width_part, width_part, 0
-    )
-    along = lax.psum(jnp.sum(scaled_one * my_inputs, axis=1, keepdims=True), "tensor") / inputs.shape[1]
-    grad_in = grad_res + scale_one * scaled_one - my_inputs * scale_one**3 * along
-    out_part = result.astype(jnp.bfloat16)
-    grad_part = grad_in.astype(jnp.bfloat16)
-    out_part, grad_part = lax.optimization_barrier((out_part, grad_part))
-    layer_output = to_given(out_part)
-    input_grad = to_given(grad_part)
-    gains = jnp.stack([first_gain_part, my_part(second_gain_grad)[0]])
-    gains = lax.dynamic_update_slice_in_dim(
-        jnp.zeros((2, inputs.shape[1]), jnp.float32), gains, tensor_member * width_part, 1
-    )
-    gains = lax.dynamic_slice_in_dim(
-        lax.psum(gains, ("dp", "tensor")),
-        member * (inputs.shape[1] // groups),
-        inputs.shape[1] // groups,
-        1,
-    )
-
-    output_share, first = shared(output_grad), shared(joined_grad)
-    a = query_weight.shape[1]
+    both_share, back_out = lax.optimization_barrier((both_share, back_out))
+    layer_output = matmul(put_back, back_out.reshape(row_count, width_part)).astype(BF)
+    input_grad = matmul(put_back, back_grad.reshape(row_count, width_part)).astype(BF)
+    o = output_weight.shape[0]
+    a = o + query_weight.shape[1]
     b = a + key_matrix.shape[1]
     summed = (
         gains[0],
-        first[:, :a],
+        first[:, o:a],
         first[:, a:b],
         first[:, b:],
-        output_share.T,
+        first[:, :o].T,
         both_share[:, :hidden],
         both_share[:, hidden:],
         down_share.T,
-        gains[1],
+        gains[8],
     )
     return (
         layer_output,

time: 770 us -> 649 us (0.84)
  waiting for transfers between devices: 80.6 us -> 0.71 us
  Pallas kernels: 482 us -> 561 us
  blocking collectives: 72.8 us -> 0 us
  other arithmetic: 30.6 us -> 10.6 us
  matrix products: 51.3 us -> 38 us
  starting transfers between devices: 12.1 us -> 0.08 us
    pallas_call x2, Pallas kernels: 104 us -> 201 us  [the longest x1 119 us: deal_out(): pl.pallas_call(functools.partial(deal_out_kernel, n, groups, tiles, chunk...]
    all_gather x1 -> x0, waiting for transfers between devices: 58.1 us -> none  [per_device(): lax.all_gather(to_owner(tokens), 'tensor', axis=1, tiled=True)]
    psum x2 -> x0, blocking collectives: 52.3 us -> none  [the longest x1 40.7 us: per_device(): lax.psum(gains, ('dp', 'tensor'))]
    pallas_call x1, Pallas kernels: 169 us -> 116 us  [second_back_of(): pl.pallas_call(functools.partial(second_back_kernel, n), out_shape=[jax.S...]
    pallas_call x1, Pallas kernels: 188 us -> 222 us  [middle(): pl.pallas_call(functools.partial(middle_kernel, n), out_shape=[jax.ShapeD...]
    all_to_all x1 -> x0, blocking collectives: 20.5 us -> none  [to_owner(): lax.all_to_all(dealt, 'dp', split_axis=0, concat_axis=0, tiled=True)]
    all_to_all x3 -> x0, waiting for transfers between devices: 16 us -> none  [the longest x2 9.9 us: to_given(): lax.all_to_all(swap(values, tiles, groups), 'dp', split_axis=0, concat_ax...]
    dot_general x8 -> x6, matrix products: 51.3 us -> 38 us  [matmul(): return jnp.dot(left, right, preferred_element_type=jnp.float32)]
  transfers between devices with their start and end apart: 9 -> 2, of which waited for: 4 -> 0; matrix products, arithmetic and copies ran while one was open for 8% -> 2% of each run, Pallas kernels for 36% -> 37%
where the time goes in v4:
time: 649 us; the launch traced here: 644 us
  Pallas kernels  561 us (86%)
  matrix products  38 us (6%)
  local copies, waits for them, and re-layouts  18.6 us (3%)
  between operations  14.7 us (2%)
  other arithmetic  10.6 us (2%)
    pallas_call x1, Pallas kernels, middle(): pl.pallas_call(functools.partial(middle_kernel, n), out_shape=[jax.ShapeD...  222 us
    pallas_call x1, Pallas kernels, deal_out(): pl.pallas_call(functools.partial(deal_out_kernel, n, groups, tiles, chunk...  119 us
    pallas_call x1, Pallas kernels, second_back_of(): pl.pallas_call(functools.partial(second_back_kernel, n), out_shape=[jax.S...  116 us
    pallas_call x1, Pallas kernels, deal_in(): pl.pallas_call(functools.partial(deal_in_kernel, n, groups), out_shape=[j...  81.8 us
    dot_general x6, matrix products, matmul(): return jnp.dot(left, right, preferred_element_type=jnp.float32)  38 us
    pallas_call x1, Pallas kernels, attend(): pl.pallas_call(functools.partial(attend_kernel, tiles), out_shape=[jax.Sh...  21.5 us
  transfers between devices with their start and end apart: 2, of which 0 were waited for; matrix products, arithmetic and copies ran while one was open for 2% of the time, Pallas kernels for 37%

profile of v4, /device:TPU:0, one launch (start us, length us, event | category | flops | bytes accessed | tf_op | source)
XLA Modules:
  0.0 643.7 jit_solution(17759770185005339328)
XLA Ops:
  7.2 0.0 copy-start.1
  7.2 0.0 reduce-scatter.5.cloned.1.call-start
  7.2 0.7 and_select_fusion
  8.0 0.8 select_reduce_fusion.9
  8.8 0.1 select_reduce_fusion.8
  9.0 0.9 select_reduce_fusion.7
  9.8 0.7 fusion.22
  10.5 0.1 select_reduce_fusion.2
  10.6 0.1 convert_element_type.69
  10.7 1.3 convert_element_type.80.keep
  12.0 0.1 convert_element_type.71
  12.1 0.1 reduce_sum.109
  12.2 0.1 mul.193
  12.3 0.1 convert_element_type.66
  12.4 0.2 broadcast_multiply_fusion
  12.6 2.7 fusion.13
  15.3 0.2 slice_negate_fusion
  15.5 0.1 add.129
  15.6 0.1 mul.194
  15.7 1.0 copy.44.low_col.refs_14_
  16.7 1.0 copy.43.code_col.refs_13_
  17.8 0.1 select_reduce_fusion
  17.9 0.0 copy-done.1
  17.9 0.0 copy-start.2
  17.9 1.3 fusion.11
  19.2 0.0 copy-done.2
  19.2 1.3 fusion.12
  20.5 0.7 add.128.code_row.refs_12_
  21.2 1.0 pad_maximum_fusion.1.sine.refs_11_
  22.2 81.8 %shard_map.221 = (bf16[4,8,32,2048]{3,2,1,0:T(8,128)(2,1)}, bf16[4,8,32,512]{3,2,1,0:T(8,128)(2,1)S(1)}) custom-call(bf16[8,4,32,512]{3,2,1,0:T(8,128)(2,1)S(1)} %bitcast.23, bf16[8,4,32,512]{3,2,1,0:T(8,128)(2,1)S(1)} %bitcast.24), custom_call_target="tpu_custom_call" | custom-call | tf_op jit(solution)/shard_map/pallas_call | solution.py:685
  104.0 0.0 copy-start
  104.0 1.0 copy-done
  105.0 21.5 %shard_map.222 = (bf16[1024,2048]{1,0:T(8,128)(2,1)}, bf16[1024,2048]{1,0:T(8,128)(2,1)}, bf16[1024,512]{1,0:T(8,128)(2,1)}, bf16[1024,128]{1,0:T(8,128)(2,1)}, ...) custom-call(bf16[1024,2048]{1,0:T(8,128)(2,1)} %bitcast.25, ...), custom_call_target="tpu_custom_call" | custom-call | tf_op jit(solution)/shard_map/pallas_call | solution.py:103
  126.5 222.4 %shard_map.223 = (bf16[1024,512]{1,0:T(8,128)(2,1)}, bf16[1024,2048]{1,0:T(8,128)(2,1)}, bf16[1024,2048]{1,0:T(8,128)(2,1)}, bf16[1024,2048]{1,0:T(8,128)(2,1)},...) custom-call(bf16[1024,2048]{1,0:T(8,128)(2,1)} %get-tuple-element.45.part, ...), custom_call_target="tpu_custom_call" | custom-call | tf_op jit(solution)/shard_map/pallas_call | solution.py:472
  348.9 11.4 %convolution_convert_fusion.1 = bf16[2048,1408]{1,0:T(8,128)(2,1)} fusion(bf16[1024,1408]{1,0:T(8,128)(2,1)} %get-tuple-element.49, bf16[1024,2048]{1,0:T(8,128)(2,1)} %get-tuple-element.48.g, f32[1024]{0:T(1024)S(1)} %convert_element_type.71), kind=kOutput, calls=%fused_computation.2 | convolution fusion | flops 5914755072 | bytes 12849152 | tf_op jit(solution)/shard_map/dot_general | solution.py:1043
  360.3 18.3 %convolution_convert_fusion = bf16[2048,2816]{1,0:T(8,128)(2,1)} fusion(bf16[1024,2048]{1,0:T(8,128)(2,1)} %get-tuple-element.51, bf16[1024,2816]{1,0:T(8,128)(2,1)} %get-tuple-element.52), kind=kOutput, calls=%fused_computation | convolution fusion | flops 11816927232 | bytes 21495808 | tf_op jit(solution)/shard_map/dot_general | solution.py:1043
  378.6 0.0 reduce-scatter.5.cloned.1.call-update
  378.6 0.0 reduce-scatter.3.cloned.1.call-start
  378.7 0.7 reduce-scatter.3.cloned.1.call-update
  379.4 1.3 dynamic-slice.3
  380.7 116.3 %shard_map.224 = (bf16[1024,2048]{1,0:T(8,128)(2,1)}, f32[1024,512]{1,0:T(8,128)}, f32[1,2048]{1,0:T(1,128)}) custom-call(bf16[1024,2048]{1,0:T(8,128)(2,1)} %get-tuple-element.55.part, bf16[1024,2048]{1,0:T(8,128)(2,1)} %bitcast.27, bf16[1024,2048]{1,0:T(8,128)(2,1)} %get-tuple-element.56.a, bf16[1024,2048]{1,0:T(8,128)(2,1)} %get-tuple-element.48.g, ...), custom_call_target="tpu_custom_call" | custom-call | tf_op jit(solution)/shard_map/pallas_call | solution.py:546
  497.0 0.1 select_reduce_fusion.1
  497.2 2.3 constant_dynamic-slice_fusion.x
  499.4 0.0 reduce-scatter.5.cloned.1.call-done
  499.4 1.2 convert_element_type.77
  500.7 119.0 %shard_map.225 = (bf16[8,4,32,512]{3,2,1,0:T(8,128)(2,1)}, bf16[8,4,32,512]{3,2,1,0:T(8,128)(2,1)}, f32[16,256]{1,0:T(8,128)}, f32[256,1280]{1,0:T(8,128)}) custom-call(bf16[1024,512]{1,0:T(8,128)(2,1)} %constant_dynamic-slice_fusion.x, f32[1024,512]{1,0:T(8,128)} %get-tuple-element.57.dh, f32[1024,1]{1,0:T(8,128)} %get-tuple-element.58.scale1, ...), custom_call_target="tpu_custom_call" | custom-call | tf_op jit(solution)/shard_map/pallas_call | solution.py:989
  619.7 2.1 slice_bitcast_fusion
  621.7 1.0 copy.49
  622.7 1.5 copy.50
  624.3 1.3 fusion.21
  625.6 1.7 fusion.20
  627.2 3.5 fusion.10
  630.7 0.0 copy-start.3
  630.7 0.0 reduce-scatter.3.cloned.1.call-done
  630.7 1.6 convert_element_type.76
  632.4 1.8 fusion.19
  634.1 0.0 copy-done.3
  634.1 2.3 fusion.9
  (11 shorter events, 0.1 us)
Async XLA Ops:
  7.2 10.7 %copy-start.1 = (bf16[1024,512]{1,0:T(8,128)(2,1)S(1)}, bf16[1024,512]{1,0:T(8,128)(2,1)}, u32[]{:S(2)}) copy-start(bf16[1024,512]{1,0:T(8,128)(2,1)} %param.14) | copy-start | bytes 3145732
  7.2 492.2 %reduce-scatter.5.cloned.1.call-start = ((), (), s32[]{:S(2)}) async-start(), calls=%async_computation.3 | async-start | bytes 6488064 | tf_op jit(solution)/shard_map/reduce_scatter | solution.py:1158
  17.9 1.3 copy-start.2
  104.0 1.0 copy-start
  378.6 252.1 %reduce-scatter.3.cloned.1.call-start = ((), (), s32[]{:S(2)}) async-start(), calls=%async_computation.2 | async-start | bytes 12976128 | tf_op jit(solution)/shard_map/reduce_scatter | solution.py:1158
  630.7 3.4 copy-start.3
Sparse Core Ops, SparseCore 0:
  378.8 59.2 reduce-scatter.4
  441.9 118.3 reduce-scatter.2

commit v5 on v4

--- a/solution.py
+++ b/solution.py
@@ -504,18 +504,47 @@
     )(part, x, g_part, keep, gain, wg, wu, wd)
 
 
-def second_back_kernel(n, part, x, a, g, keep, gain, ga, dh, gain_grad, up, total, us, ur, ds, dr):
+def second_back_kernel(n, part, x, a, g, keep, gain, inner_far, ga, dh, gain_grad, grad_far,
+                       up, total, inner, stage, us, ur, ds, dr, load, save):
     z = lax.axis_index("tensor")
     rows, width = part.shape
     w = dh.shape[1]
     piece = BLOCK // 2
     sums = (us, ur, ds, dr)
+    loads = [pltpu.make_async_copy(inner_far, inner, load.at[0])]
+    for copy in loads:
+        copy.start()
     neighbour_barrier(z, n, "tensor")
+    span = stage.shape[1]
+    spans = width // span
+
+    def saved(j):
+        slot = lax.rem(j, 2)
+        return pltpu.make_async_copy(stage.at[slot], grad_far.at[pl.ds(pl.multiple_of(j * span, span), span)], save.at[slot])
+
     gain_grad[...] = jnp.zeros_like(gain_grad)
     first = BLOCK // CHUNK - 1 + 2 * LAG * (n - 1)
 
     def body(t, _):
         line_sum_step(n, z, t, part, up, total, sums)
+        j = t - 3
+
+        @pl.when((j >= 0) & (j < spans))
+        def _():
+            @pl.when(j == 0)
+            def _():
+                for copy in loads:
+                    copy.wait()
+
+            @pl.when(j >= 2)
+            def _():
+                saved(j - 2).wait()
+
+            cut = pl.ds(pl.multiple_of(j * span, span), span)
+            gf = (keep[...] * g[:, cut].astype(F32)).astype(BF)
+            stage[lax.rem(j, 2)] = tn(gf, inner[...]).astype(BF)
+            saved(j).start()
+
         q = t - first
 
         @pl.when(q >= 0)
@@ -539,9 +568,11 @@
 
     lax.fori_loop(0, first + rows // piece, body, 0)
     line_sum_drain(n, z, part, up, total, sums)
-
-
-def second_back_of(n, part, x, a, g, keep, gain):
+    for j in range(spans - 2, spans):
+        saved(j).wait()
+
+
+def second_back_of(n, part, x, a, g, keep, gain, inner):
     rows, width = part.shape
     return pl.pallas_call(
         functools.partial(second_back_kernel, n),
@@ -549,12 +580,21 @@
             jax.ShapeDtypeStruct((rows, width), BF),
             jax.ShapeDtypeStruct((rows, width // n), F32),
             jax.ShapeDtypeStruct((1, width), F32),
+            jax.ShapeDtypeStruct((width, inner.shape[1]), BF),
         ],
-        in_specs=[VM] * 6,
-        out_specs=[VM] * 3,
-        scratch_shapes=[pltpu.VMEM((rows, width), BF), pltpu.VMEM((rows, width), BF), *line_sum_sems(rows)],
-        compiler_params=pltpu.CompilerParams(collective_id=4, has_side_effects=True, vmem_limit_bytes=56 << 20),
-    )(part, x, a, g, keep, gain)
+        in_specs=[VM] * 6 + [ANY],
+        out_specs=[VM] * 3 + [ANY],
+        scratch_shapes=[
+            pltpu.VMEM((rows, width), BF),
+            pltpu.VMEM((rows, width), BF),
+            pltpu.VMEM(inner.shape, BF),
+            pltpu.VMEM((2, 256, inner.shape[1]), BF),
+            *line_sum_sems(rows),
+            pltpu.SemaphoreType.DMA((2,)),
+            pltpu.SemaphoreType.DMA((2,)),
+        ],
+        compiler_params=pltpu.CompilerParams(collective_id=4, has_side_effects=True, vmem_limit_bytes=60 << 20),
+    )(part, x, a, g, keep, gain, inner)
 
 
 def peers_barrier(z, n, me, groups, everyone):
@@ -711,8 +751,8 @@
 
 def deal_out_kernel(n, groups, tiles, chunk, lag, x, dh, scale1, gain1, result, gain2, normed, *refs):
     attention = refs[:15]
-    (back_out, back_dx, gains, shares, part, dqkv, dk, dv, right, left, fb, dx, lines, widths, gsrc, gdst, wsrc, wdst,
-     ss, rs, os, orr, xs, xr, ls, lr, ws, wr, es, er, qs, qr, own) = refs[15:]
+    (back_out, back_dx, gains, shares, part, dqkv, dk, dv, right, left, fb, dx, lines, widths, gsrc, gdst, wsrc, wdst, pair,
+     ss, rs, os, orr, xs, xr, ls, lr, ws, wr, es, er, qs, qr, ps, pr, own) = refs[15:]
     ga, o = attention[0], attention[8]
     z = lax.axis_index("tensor")
     me = lax.axis_index("dp")
@@ -789,45 +829,67 @@
     share = normed.shape[1] // groups
     span = max(share, 256)
 
+    half = groups // 2
+    seat = lax.div(me, 2)
+    parity = lax.rem(me, 2)
+    partner = me + 1 - 2 * parity
+
+    def rows_of(owner):
+        return pl.ds(pl.multiple_of(owner * share, share), share)
+
+    def weight_copy(kind, src, dst, sems, to, slot, at_column, wide):
+        columns = pl.ds(at_column, wide)
+        return pltpu.make_async_remote_copy(
+            src_ref=wsrc.at[rows_of(src), columns],
+            dst_ref=dst.at[slot, :, columns],
+            send_sem=sems[0].at[kind, lax.div(src, 2)],
+            recv_sem=sems[1].at[kind, slot],
+            device_id={"dp": to},
+            device_id_type=MESH,
+        )
+
     def weigh(left_ref, right_ref, at_column, kind):
+        wide = right_ref.shape[1]
+
         def one(j, _):
-            base = lax.rem(j + lax.div(me * share, span), normed.shape[1] // span) * span
-            cut = pl.ds(pl.multiple_of(base, span), span)
-            wide = right_ref.shape[1]
+            base = pl.multiple_of(j * span, span)
+            cut = pl.ds(base, span)
             wsrc[cut, at_column : at_column + wide] = tn(left_ref[:, cut], right_ref[...]).astype(BF)
             for i in range(span // share):
-                peer = lax.div(base, share) + i
-
-                @pl.when(peer != me)
+                owner = lax.div(base, share) + i
+
+                @pl.when(lax.rem(owner, 2) != parity)
                 def _():
-                    weight_copy(kind, peer, me, peer, at_column, wide).start()
-
-                @pl.when(peer == me)
-                def _():
-                    weight_own(kind, at_column, wide).start()
+                    weight_copy(kind, owner, pair, (ps, pr), partner, lax.div(owner, 2), at_column, wide).start()
 
             return 0
 
         lax.fori_loop(0, normed.shape[1] // span, one, 0)
 
-    def weight_copy(kind, block, slot, peer, at_column, wide):
-        columns = pl.ds(at_column, wide)
-        return pltpu.make_async_remote_copy(
-            src_ref=wsrc.at[pl.ds(pl.multiple_of(block * share, share), share), columns],
-            dst_ref=wdst.at[slot, :, columns],
-            send_sem=qs.at[kind, block],
-            recv_sem=qr.at[kind, slot],
-            device_id={"dp": peer},
-            device_id_type=MESH,
-        )
-
-    def weight_own(kind, at_column, wide):
-        columns = pl.ds(at_column, wide)
-        return pltpu.make_async_copy(
-            wsrc.at[pl.ds(pl.multiple_of(me * share, share), share), columns],
-            wdst.at[me, :, columns],
-            own.at[2 + tiles + kind],
-        )
+    def join(at_column, wide, kind):
+        columns = slice(at_column, at_column + wide)
+
+        def one(off, _):
+            m = lax.rem(seat + off, half)
+            owner = 2 * m + parity
+            weight_copy(kind, owner, pair, (ps, pr), partner, m, at_column, wide).wait_recv()
+            r = rows_of(owner)
+            total = (wsrc[r, columns].astype(F32) + pair[m, :, columns].astype(F32)).astype(BF)
+
+            @pl.when(owner == me)
+            def _():
+                wdst[seat, :, columns] = total
+
+            @pl.when(owner != me)
+            def _():
+                wsrc[r, columns] = total
+                weight_copy(kind, owner, wdst, (qs, qr), owner, seat, at_column, wide).start()
+
+            return 0
+
+        lax.fori_loop(1, half + 1, one, 0)
+
+    joined = ((0, ow), (ow, dqkv.shape[1]))
 
     def flows(s, _):
         for k in range(tiles):
@@ -839,6 +901,14 @@
         @pl.when(s == 2)
         def _():
             weigh(ga, o, 0, 0)
+
+        @pl.when(s == 5)
+        def _():
+            join(*joined[0], 0)
+
+        @pl.when(s == (tiles - 1) * per + 3)
+        def _():
+            join(*joined[1], 1)
 
         @pl.when(s == (tiles - 1) * per + 1)
         def _():
@@ -930,18 +1000,22 @@
     gains[...] = total
 
     def got_weight(off, _):
-        peer = lax.rem(me + off, groups)
-        for kind, (at_column, wide) in enumerate(((0, ow), (ow, dqkv.shape[1]))):
-            copy = weight_copy(kind, peer, peer, peer, at_column, wide)
+        m = lax.rem(seat + off, half)
+        for kind, (at_column, wide) in enumerate(joined):
+            copy = weight_copy(kind, 2 * m + parity, wdst, (qs, qr), me, m, at_column, wide)
             copy.wait_recv()
             copy.wait_send()
         return 0
 
-    lax.fori_loop(1, groups, got_weight, 0)
-    weight_own(0, 0, ow).wait()
-    weight_own(1, ow, dqkv.shape[1]).wait()
+    def sent_weight(m, _):
+        for kind, (at_column, wide) in enumerate(joined):
+            weight_copy(kind, 2 * m + 1 - parity, pair, (ps, pr), partner, m, at_column, wide).wait_send()
+        return 0
+
+    lax.fori_loop(1, half, got_weight, 0)
+    lax.fori_loop(0, half, sent_weight, 0)
     shares[...] = wdst[0].astype(F32)
-    for i in range(1, groups):
+    for i in range(1, half):
         shares[...] += wdst[i].astype(F32)
 
     def finish(off, _):
@@ -1010,7 +1084,8 @@
             pltpu.VMEM((groups, 16, cols), F32),
             pltpu.VMEM((groups, 16, cols), F32),
             pltpu.VMEM((width, both), BF),
-            pltpu.VMEM((groups, cols, both), BF),
+            pltpu.VMEM((groups // 2, cols, both), BF),
+            pltpu.VMEM((groups // 2, cols, both), BF),
             dma((2, n, count)),
             dma((2, n, count)),
             dma((groups,)),
@@ -1023,9 +1098,11 @@
             dma((n,)),
             dma((groups,)),
             dma((groups,)),
-            dma((2, groups)),
-            dma((2, groups)),
-            dma((tiles + 4,)),
+            dma((2, groups // 2)),
+            dma((2, groups // 2)),
+            dma((2, groups // 2)),
+            dma((2, groups // 2)),
+            dma((tiles + 2,)),
         ],
         compiler_params=pltpu.CompilerParams(collective_id=5, has_side_effects=True, vmem_limit_bytes=62 << 20),
     )(x, dh, scale1, gain1, result.reshape(tiles, groups, sub, w), gain2, normed, *attention)
@@ -1151,7 +1228,6 @@
         up_weight,
         down_weight,
     )
-    grad_ffn = (keep_rows * owned_cotangent.astype(F32)).astype(BF)
     hidden = gate_weight.shape[1]
 
     def shared(values):
@@ -1159,14 +1235,10 @@
             values.astype(jnp.bfloat16), "dp", scatter_dimension=0, tiled=True
         ).astype(jnp.float32)
 
-    down_grad = matmul(grad_ffn.T, inner_low).astype(BF)
-    down_grad, normed_two = lax.optimization_barrier((down_grad, normed_two))
     both_grad = matmul(normed_two.T, both).astype(BF)
-    second_term, both_grad, down_grad = lax.optimization_barrier(
-        (second_term, both_grad, down_grad)
-    )
-    both_share, down_share = shared(both_grad), shared(down_grad)
-    grad_attn, grad_res, second_gain_grad = second_back_of(
+    second_term, both_grad = lax.optimization_barrier((second_term, both_grad))
+    both_share = shared(both_grad)
+    grad_attn, grad_res, second_gain_grad, down_grad = second_back_of(
         tensor_count,
         second_term,
         owned_tokens,
@@ -1174,8 +1246,12 @@
         owned_cotangent,
         keep_rows,
         second_gain[None, :],
+        inner_low,
     )
-    down_share, grad_attn = lax.optimization_barrier((down_share, grad_attn))
+    both_share, down_grad, grad_attn = lax.optimization_barrier(
+        (both_share, down_grad, grad_attn)
+    )
+    down_share = shared(down_grad)
     back_out, back_grad, gains, first = deal_out(
         tensor_count,
         groups,
@@ -1192,7 +1268,7 @@
         *kept,
         *tables,
     )
-    both_share, back_out = lax.optimization_barrier((both_share, back_out))
+    down_share, back_out = lax.optimization_barrier((down_share, back_out))
     layer_output = matmul(put_back, back_out.reshape(row_count, width_part)).astype(BF)
     input_grad = matmul(put_back, back_grad.reshape(row_count, width_part)).astype(BF)
     o = output_weight.shape[0]

time: 649 us -> 630 us (0.971)
  Pallas kernels: 561 us -> 551 us
  matrix products: 38 us -> 28.3 us
    dot_general x6 -> x5, matrix products: 38 us -> 28.3 us  [matmul(): return jnp.dot(left, right, preferred_element_type=jnp.float32)]
    pallas_call x1, Pallas kernels: 119 us -> 110 us  [deal_out(): pl.pallas_call(functools.partial(deal_out_kernel, n, groups, tiles, chunk...]
  transfers between devices with their start and end apart: 2 -> 2, of which waited for: 0 -> 0; matrix products, arithmetic and copies ran while one was open for 2% -> 2% of each run, Pallas kernels for 37% -> 36%
where the time goes in v5:
time: 630 us; the launch traced here: 625 us
  Pallas kernels  551 us (87%)
  matrix products  28.3 us (4%)
  local copies, waits for them, and re-layouts  18.5 us (3%)
  between operations  14.7 us (2%)
  other arithmetic  12 us (2%)
    pallas_call x1, Pallas kernels, middle(): pl.pallas_call(functools.partial(middle_kernel, n), out_shape=[jax.ShapeD...  223 us
    pallas_call x1, Pallas kernels, second_back_of(): pl.pallas_call(functools.partial(second_back_kernel, n), out_shape=[jax.S...  116 us
    pallas_call x1, Pallas kernels, deal_out(): pl.pallas_call(functools.partial(deal_out_kernel, n, groups, tiles, chunk...  110 us
    pallas_call x1, Pallas kernels, deal_in(): pl.pallas_call(functools.partial(deal_in_kernel, n, groups), out_shape=[j...  81.8 us
    dot_general x5, matrix products, matmul(): return jnp.dot(left, right, preferred_element_type=jnp.float32)  28.3 us
    pallas_call x1, Pallas kernels, attend(): pl.pallas_call(functools.partial(attend_kernel, tiles), out_shape=[jax.Sh...  21.6 us
  transfers between devices with their start and end apart: 2, of which 0 were waited for; matrix products, arithmetic and copies ran while one was open for 2% of the time, Pallas kernels for 36%

profile of v5, /device:TPU:0, one launch (start us, length us, event | category | flops | bytes accessed | tf_op | source)
XLA Modules:
  0.0 625.0 jit_solution(16777979099596475247)
XLA Ops:
  7.2 0.0 reduce-scatter.3.cloned.1.call-start
  7.2 0.7 and_select_fusion
  7.9 0.8 select_reduce_fusion.9
  8.7 0.1 select_reduce_fusion.8
  8.9 0.9 select_reduce_fusion.7
  9.7 0.7 fusion.21
  10.4 0.1 select_reduce_fusion
  10.5 0.0 copy-start.2
  10.5 2.6 fusion.10
  13.1 0.0 copy-done.2
  13.2 1.3 fusion.11
  14.5 0.1 select_reduce_fusion.2
  14.6 0.1 reduce_sum.109
  14.7 0.1 mul.185
  14.8 0.1 convert_element_type.55
  14.8 0.2 broadcast_multiply_fusion
  15.1 2.7 fusion.12
  17.8 0.2 slice_negate_fusion
  18.0 0.7 add.128.code_row.refs_12_
  18.7 0.1 mul.186
  18.7 0.1 add.129
  18.8 1.0 copy.44.low_col.refs_14_
  19.9 1.0 copy.43.code_col.refs_13_
  20.9 0.1 convert_element_type.58
  21.0 1.3 convert_element_type.65.keep
  22.3 81.8 %shard_map.221 = (bf16[4,8,32,2048]{3,2,1,0:T(8,128)(2,1)}, bf16[4,8,32,512]{3,2,1,0:T(8,128)(2,1)S(1)}) custom-call(bf16[8,4,32,512]{3,2,1,0:T(8,128)(2,1)S(1)} %bitcast.22, bf16[8,4,32,512]{3,2,1,0:T(8,128)(2,1)S(1)} %bitcast.23), custom_call_target="tpu_custom_call" | custom-call | tf_op jit(solution)/shard_map/pallas_call | solution.py:725
  104.1 0.0 copy-start
  104.2 1.0 copy-done
  105.1 1.0 pad_maximum_fusion.1.sine.refs_11_
  106.1 21.6 %shard_map.222 = (bf16[1024,2048]{1,0:T(8,128)(2,1)}, bf16[1024,2048]{1,0:T(8,128)(2,1)}, bf16[1024,512]{1,0:T(8,128)(2,1)}, bf16[1024,128]{1,0:T(8,128)(2,1)}, ...) custom-call(bf16[1024,2048]{1,0:T(8,128)(2,1)} %bitcast.24, ...), custom_call_target="tpu_custom_call" | custom-call | tf_op jit(solution)/shard_map/pallas_call | solution.py:103
  127.7 222.5 %shard_map.223 = (bf16[1024,512]{1,0:T(8,128)(2,1)}, bf16[1024,2048]{1,0:T(8,128)(2,1)}, bf16[1024,2048]{1,0:T(8,128)(2,1)}, bf16[1024,2048]{1,0:T(8,128)(2,1)},...) custom-call(bf16[1024,2048]{1,0:T(8,128)(2,1)} %get-tuple-element.44.part, ...), custom_call_target="tpu_custom_call" | custom-call | tf_op jit(solution)/shard_map/pallas_call | solution.py:472
  350.2 18.5 %convolution_convert_fusion = bf16[2048,2816]{1,0:T(8,128)(2,1)} fusion(bf16[1024,2048]{1,0:T(8,128)(2,1)} %get-tuple-element.47, bf16[1024,2816]{1,0:T(8,128)(2,1)} %get-tuple-element.48), kind=kOutput, calls=%fused_computation | convolution fusion | flops 11816927232 | bytes 21495808 | tf_op jit(solution)/shard_map/dot_general | solution.py:1120
  368.7 0.0 reduce-scatter.3.cloned.1.call-update
  368.7 0.0 reduce-scatter.5.cloned.1.call-start
  368.8 115.8 %shard_map.224 = (bf16[1024,2048]{1,0:T(8,128)(2,1)}, f32[1024,512]{1,0:T(8,128)}, f32[1,2048]{1,0:T(1,128)}, bf16[2048,1408]{1,0:T(8,128)(2,1)}) custom-call(bf16[1024,2048]{1,0:T(8,128)(2,1)} %get-tuple-element.50.part, bf16[1024,2048]{1,0:T(8,128)(2,1)} %bitcast.26, bf16[1024,2048]{1,0:T(8,128)(2,1)} %get-tuple-element.51.a, ...), custom_call_target="tpu_custom_call" | custom-call | tf_op jit(solution)/shard_map/pallas_call | solution.py:577
  484.6 0.0 reduce-scatter.3.cloned.1.call-done
  484.7 3.1 convert_element_type.61
  487.8 0.0 reduce-scatter.5.cloned.1.call-update
  487.8 1.3 dynamic-slice.3
  489.2 0.1 select_reduce_fusion.1
  489.3 2.3 constant_dynamic-slice_fusion.x
  491.5 109.7 %shard_map.225 = (bf16[8,4,32,512]{3,2,1,0:T(8,128)(2,1)}, bf16[8,4,32,512]{3,2,1,0:T(8,128)(2,1)}, f32[16,256]{1,0:T(8,128)}, f32[256,1280]{1,0:T(8,128)}) custom-call(bf16[1024,512]{1,0:T(8,128)(2,1)} %constant_dynamic-slice_fusion.x, f32[1024,512]{1,0:T(8,128)} %get-tuple-element.57.dh, f32[1024,1]{1,0:T(8,128)} %get-tuple-element.58.scale1, ...), custom_call_target="tpu_custom_call" | custom-call | tf_op jit(solution)/shard_map/pallas_call | solution.py:1063
  601.3 2.1 slice_bitcast_fusion
  603.3 1.0 copy.49
  604.3 1.3 fusion.20
  605.6 1.7 fusion.19
  607.3 0.0 copy-start.1
  607.3 3.6 fusion.9
  610.9 0.0 copy-done.1
  610.9 0.0 copy-start.3
  610.9 1.8 fusion.18
  612.7 0.0 reduce-scatter.5.cloned.1.call-done
  612.7 1.2 convert_element_type.62
  613.9 0.0 copy-done.3
  613.9 2.3 fusion.8
  616.2 1.5 copy.50
  (11 shorter events, 0.1 us)
Async XLA Ops:
  7.2 477.5 %reduce-scatter.3.cloned.1.call-start = ((), (), s32[]{:S(2)}) async-start(), calls=%async_computation.2 | async-start | bytes 12976128 | tf_op jit(solution)/shard_map/reduce_scatter | solution.py:1234
  10.5 2.6 copy-start.2
  104.1 1.0 copy-start
  368.7 243.9 %reduce-scatter.5.cloned.1.call-start = ((), (), s32[]{:S(2)}) async-start(), calls=%async_computation.3 | async-start | bytes 6488064 | tf_op jit(solution)/shard_map/reduce_scatter | solution.py:1234
  607.3 3.6 copy-start.1
  610.9 3.0 copy-start.3
Sparse Core Ops, SparseCore 0:
  368.9 86.9 reduce-scatter.2
  487.9 76.2 reduce-scatter.4

commit v6 on v5

--- a/solution.py
+++ b/solution.py
@@ -54,32 +54,34 @@
     return jnp.where((code_row <= code_col) & (code_row >= low_col), 0.0, -1e30)
 
 
-def attend_kernel(tiles, x, gain, wq, wk, wv, wo, cosine, sine, code_row, code_col, low_col,
-                  part, normed, q, k, v, o, lse, scales):
-    rows = x.shape[0]
+def attend_tile(t, tiles, xt, gain, wq, wk, wv, wo, cosine, sine, code_row, code_col, low_col,
+                part, normed, q, k, v, o, lse, scales):
+    rows = normed.shape[0]
     tile = rows // tiles
     heads = wq.shape[1] // HEAD_WIDTH
     kv = wk.shape[1] // HEAD_WIDTH
     group = heads // kv
     factor = math.log2(math.e) / math.sqrt(HEAD_WIDTH)
-    for t in range(tiles):
-        r = pl.ds(t * tile, tile)
-        xt = x[r, :].astype(F32)
-        scale = lax.rsqrt(jnp.mean(xt * xt, axis=1, keepdims=True) + eps)
-        scales[r, :] = scale
-        n1 = (xt * scale * gain[...]).astype(BF)
-        normed[r, :] = n1
-        c, s = cosine[r, :], sine[r, :]
-        pre = mm(n1, wq[...])
-        for h in range(heads):
-            cut = slice(h * HEAD_WIDTH, (h + 1) * HEAD_WIDTH)
-            q[r, cut] = spin(pre[:, cut], c, s).astype(BF)
-        pre = mm(n1, wk[...])
-        for h in range(kv):
-            cut = slice(h * HEAD_WIDTH, (h + 1) * HEAD_WIDTH)
-            k[r, cut] = spin(pre[:, cut], c, s).astype(BF)
-        v[r, :] = mm(n1, wv[...]).astype(BF)
-        seen = (t + 1) * tile
+    r = pl.ds(t * tile, tile)
+    xt = xt.astype(F32)
+    scale = lax.rsqrt(jnp.mean(xt * xt, axis=1, keepdims=True) + eps)
+    scales[r, :] = scale
+    n1 = (xt * scale * gain[...]).astype(BF)
+    normed[r, :] = n1
+    c, s = cosine[r, :], sine[r, :]
+    pre = mm(n1, wq[...])
+    for h in range(heads):
+        cut = slice(h * HEAD_WIDTH, (h + 1) * HEAD_WIDTH)
+        q[r, cut] = spin(pre[:, cut], c, s).astype(BF)
+    pre = mm(n1, wk[...])
+    for h in range(kv):
+        cut = slice(h * HEAD_WIDTH, (h + 1) * HEAD_WIDTH)
+        k[r, cut] = spin(pre[:, cut], c, s).astype(BF)
+    v[r, :] = mm(n1, wv[...]).astype(BF)
+    seen = (t + 1) * tile
+    block = min(tile, 256)
+    for at in range(t * tile, (t + 1) * tile, block):
+        r = pl.ds(at, block)
         bias = visible(code_row[:, :seen], code_col[r, :], low_col[r, :])
         logs = []
         for h in range(heads):
@@ -94,19 +96,6 @@
             logs.append(top + jnp.log2(total))
         lse[r, :] = jnp.concatenate(logs, axis=1)
         part[r, :] = mm(o[r, :], wo[...]).astype(BF)
-
-
-def attend(tiles, x, gain, wq, wk, wv, wo, *tables):
-    rows, width = x.shape
-    heads = wq.shape[1] // HEAD_WIDTH
-    shapes = [(rows, width), (rows, width), (rows, wq.shape[1]), (rows, wk.shape[1]), (rows, wv.shape[1]), (rows, wq.shape[1])]
-    return pl.pallas_call(
-        functools.partial(attend_kernel, tiles),
-        out_shape=[jax.ShapeDtypeStruct(s, BF) for s in shapes] + [jax.ShapeDtypeStruct((rows, heads), F32), jax.ShapeDtypeStruct((rows, 1), F32)],
-        in_specs=[VM] * 11,
-        out_specs=[VM] * 8,
-        compiler_params=pltpu.CompilerParams(vmem_limit_bytes=56 << 20),
-    )(x, gain, wq, wk, wv, wo, *tables)
 
 
 def attend_back_tile(t, tiles, ga, wq, wk, wv, wo, q, k, v, o, lse, cosine, sine, code_row, code_col, low_col,
@@ -631,7 +620,12 @@
     )
 
 
-def deal_in_kernel(n, groups, dealt_x, dealt_g, full, g_part, xs, xr, gs, gr, ss, rs, own):
+def deal_in_kernel(n, groups, dealt_x, dealt_g, gain, cosine, sine, code_row, code_col, low_col, *refs):
+    far, (full, g_part, x_part), results = refs[:4], refs[4:7], refs[7:15]
+    near, (xs, xr, gs, gr, ss, rs, own, load) = refs[15:19], refs[19:]
+    loads = [pltpu.make_async_copy(a, b, load.at[i]) for i, (a, b) in enumerate(zip(far, near))]
+    for copy in loads:
+        copy.start()
     z = lax.axis_index("tensor")
     me = lax.axis_index("dp")
     tiles, sub, w = dealt_x.shape[1:]
@@ -698,6 +692,27 @@
                         @pl.when((after >= 0) & (after < n))
                         def _():
                             rcopy(cut(o, c), cut(o, c), ss.at[d, o, c], rs.at[d, o, c], after).start()
+
+        if s == tiles - 1:
+            pltpu.make_async_copy(full.at[:, :, :, cols], x_part, own.at[tiles + 1]).start()
+        t = s - (n - 1)
+        if t >= 0:
+            if t == 0:
+                for copy in loads:
+                    copy.wait()
+            attend_tile(
+                t,
+                tiles,
+                full[t].reshape(groups * sub, n * w),
+                gain,
+                *near,
+                cosine,
+                sine,
+                code_row,
+                code_col,
+                low_col,
+                *results,
+            )
 
     def finish(off, _):
         peer = lax.rem(me + off, groups)
@@ -710,6 +725,7 @@
 
     lax.fori_loop(1, groups, finish, 0)
     pltpu.make_async_copy(dealt_g.at[me], g_part.at[:, me], own.at[tiles]).wait()
+    pltpu.make_async_copy(full.at[:, :, :, cols], x_part, own.at[tiles + 1]).wait()
     for c in range(tiles):
         for d in range(2):
             for o in range(n):
@@ -719,28 +735,37 @@
                     rcopy(cut(o, c), cut(o, c), ss.at[d, o, c], rs.at[d, o, c], z).wait_send()
 
 
-def deal_in(n, groups, dealt_x, dealt_g):
+def deal_in(n, groups, dealt_x, dealt_g, gain, weights, tables):
     tiles, sub, w = dealt_x.shape[1:]
+    rows = tiles * groups * sub
+    wq, wk, wv, wo = weights
     dma = pltpu.SemaphoreType.DMA
+    widths = (n * w, n * w, wq.shape[1], wk.shape[1], wv.shape[1], wq.shape[1])
     return pl.pallas_call(
         functools.partial(deal_in_kernel, n, groups),
         out_shape=[
             jax.ShapeDtypeStruct((tiles, groups, sub, n * w), BF),
             jax.ShapeDtypeStruct((tiles, groups, sub, w), BF),
+            jax.ShapeDtypeStruct((tiles, groups, sub, w), BF),
+            *(jax.ShapeDtypeStruct((rows, k), BF) for k in widths),
+            jax.ShapeDtypeStruct((rows, wq.shape[1] // HEAD_WIDTH), F32),
+            jax.ShapeDtypeStruct((rows, 1), F32),
         ],
-        in_specs=[VM] * 2,
-        out_specs=[VM] * 2,
+        in_specs=[VM] * 8 + [ANY] * 4,
+        out_specs=[VM] * 11,
         scratch_shapes=[
+            *(pltpu.VMEM(a.shape, BF) for a in weights),
             dma((tiles, groups)),
             dma((tiles, groups)),
             dma((groups,)),
             dma((groups,)),
             dma((2, n, tiles)),
             dma((2, n, tiles)),
-            dma((tiles + 1,)),
+            dma((tiles + 2,)),
+            dma((4,)),
         ],
-        compiler_params=pltpu.CompilerParams(collective_id=6, has_side_effects=True, vmem_limit_bytes=48 << 20),
-    )(dealt_x, dealt_g)
+        compiler_params=pltpu.CompilerParams(collective_id=6, has_side_effects=True, vmem_limit_bytes=60 << 20),
+    )(dealt_x, dealt_g, gain, *tables, *weights)
 
 
 def exact(left, right, contract):
@@ -751,7 +776,7 @@
 
 def deal_out_kernel(n, groups, tiles, chunk, lag, x, dh, scale1, gain1, result, gain2, normed, *refs):
     attention = refs[:15]
-    (back_out, back_dx, gains, shares, part, dqkv, dk, dv, right, left, fb, dx, lines, widths, gsrc, gdst, wsrc, wdst, pair,
+    (back_out, back_dx, gains, o_share, q_share, k_share, v_share, part, dqkv, dk, dv, right, left, fb, dx, lines, widths, gsrc, gdst, wsrc, wdst, pair,
      ss, rs, os, orr, xs, xr, ls, lr, ws, wr, es, er, qs, qr, ps, pr, own) = refs[15:]
     ga, o = attention[0], attention[8]
     z = lax.axis_index("tensor")
@@ -794,7 +819,7 @@
 
     def open_tile(t):
         r = pl.ds(pl.multiple_of(t * tile, tile), tile)
-        e = fb[r, :] * gain1[...]
+        e = fb[r, :] * gain1[pl.ds(z, 1), :]
         xt = x[r, :].astype(F32)
         lines[z, :, r] = exact(jnp.ones((8, w), F32), e * xt, ((1,), (1,)))
         others(lambda other: line_copy(t, z, other).start())
@@ -812,7 +837,7 @@
         for j in range(1, n):
             total = total + lines[j, :, r]
         along = exact(total * (1.0 / (8 * n * w)), jnp.ones((8, w), F32), ((0,), (0,)))
-        e = fb[r, :] * gain1[...]
+        e = fb[r, :] * gain1[pl.ds(z, 1), :]
         s = scale1[r, :]
         full = dh[r, :] + s * e - x[r, :].astype(F32) * (s * s * s * along)
         dx[t] = full.astype(BF).reshape(groups, sub, w)
@@ -1014,9 +1039,14 @@
 
     lax.fori_loop(1, half, got_weight, 0)
     lax.fori_loop(0, half, sent_weight, 0)
-    shares[...] = wdst[0].astype(F32)
-    for i in range(1, half):
-        shares[...] += wdst[i].astype(F32)
+    at_column = 0
+    for share_ref in (o_share, q_share, k_share, v_share):
+        columns = slice(at_column, at_column + share_ref.shape[1])
+        at_column += share_ref.shape[1]
+        total = wdst[0, :, columns].astype(F32)
+        for i in range(1, half):
+            total = total + wdst[i, :, columns].astype(F32)
+        share_ref[...] = total
 
     def finish(off, _):
         peer = lax.rem(me + off, groups)
@@ -1066,10 +1096,11 @@
             jax.ShapeDtypeStruct(dealt, BF),
             jax.ShapeDtypeStruct(dealt, BF),
             jax.ShapeDtypeStruct((16, cols), F32),
-            jax.ShapeDtypeStruct((cols, both), F32),
+            jax.ShapeDtypeStruct((cols, attention[8].shape[1]), F32),
+            *(jax.ShapeDtypeStruct((cols, a.shape[1]), F32) for a in attention[1:4]),
         ],
         in_specs=[VM] * 22,
-        out_specs=[VM] * 4,
+        out_specs=[VM] * 7,
         scratch_shapes=[
             pltpu.VMEM((rows, width), BF),
             pltpu.VMEM((rows, joined), BF),
@@ -1190,20 +1221,6 @@
     tensor_count = lax.axis_size("tensor")
     tensor_member = lax.axis_index("tensor")
     dealt_shape = (groups, tiles, per_owner // tiles, width_part)
-    owned_tokens, part_cotangent = deal_in(
-        tensor_count,
-        groups,
-        *(
-            matmul(chosen, values).astype(BF).reshape(dealt_shape)
-            for values in (tokens, cotangent)
-        ),
-    )
-    owned_tokens = owned_tokens.reshape(row_count, -1)
-    part_cotangent = part_cotangent.reshape(row_count, width_part)
-
-    def my_part(values):
-        return lax.dynamic_slice_in_dim(values, tensor_member * width_part, width_part, 1)
-
     cosine, sine = rotary_tables(token_positions, HEAD_WIDTH)
     half = HEAD_WIDTH // 2
     tables = (
@@ -1214,9 +1231,24 @@
         lowest[:, None],
     )
     weights = (query_weight, key_matrix, value_matrix, output_weight)
-    attn_part, normed_one, *kept, scale_one = attend(
-        tiles, owned_tokens, first_gain[None, :], *weights, *tables
+    dealt_tokens, dealt_cotangent = (
+        matmul(chosen, values).astype(BF).reshape(dealt_shape) for values in (tokens, cotangent)
     )
+    owned_tokens, part_cotangent, part_tokens, attn_part, normed_one, *kept, scale_one = deal_in(
+        tensor_count,
+        groups,
+        dealt_tokens,
+        dealt_cotangent,
+        first_gain[None, :],
+        weights,
+        tables,
+    )
+    owned_tokens = owned_tokens.reshape(row_count, -1)
+    part_cotangent = part_cotangent.reshape(row_count, width_part)
+
+    def my_part(values):
+        return lax.dynamic_slice_in_dim(values, tensor_member * width_part, width_part, 1)
+
     result, attn_sum, owned_cotangent, normed_two, inner_low, both, second_term = middle(
         tensor_count,
         attn_part,
@@ -1233,7 +1265,7 @@
     def shared(values):
         return lax.psum_scatter(
             values.astype(jnp.bfloat16), "dp", scatter_dimension=0, tiled=True
-        ).astype(jnp.float32)
+        )
 
     both_grad = matmul(normed_two.T, both).astype(BF)
     second_term, both_grad = lax.optimization_barrier((second_term, both_grad))
@@ -1252,14 +1284,14 @@
         (both_share, down_grad, grad_attn)
     )
     down_share = shared(down_grad)
-    back_out, back_grad, gains, first = deal_out(
+    back_out, back_grad, gains, o_share, q_share, k_share, v_share = deal_out(
         tensor_count,
         groups,
         tiles,
-        my_part(owned_tokens),
+        part_tokens.reshape(row_count, width_part),
         grad_res,
         scale_one,
-        my_part(first_gain[None, :]),
+        first_gain.reshape(tensor_count, width_part),
         result,
         second_gain_grad,
         normed_one,
@@ -1271,18 +1303,15 @@
     down_share, back_out = lax.optimization_barrier((down_share, back_out))
     layer_output = matmul(put_back, back_out.reshape(row_count, width_part)).astype(BF)
     input_grad = matmul(put_back, back_grad.reshape(row_count, width_part)).astype(BF)
-    o = output_weight.shape[0]
-    a = o + query_weight.shape[1]
-    b = a + key_matrix.shape[1]
     summed = (
         gains[0],
-        first[:, o:a],
-        first[:, a:b],
-        first[:, b:],
-        first[:, :o].T,
-        both_share[:, :hidden],
-        both_share[:, hidden:],
-        down_share.T,
+        q_share,
+        k_share,
+        v_share,
+        o_share.T,
+        both_share[:, :hidden].astype(F32),
+        both_share[:, hidden:].astype(F32),
+        down_share.T.astype(F32),
         gains[8],
     )
     return (

time: 630 us -> 616 us (0.978)
  Pallas kernels: 551 us -> 540 us
    pallas_call x1 -> x0, Pallas kernels: 21.6 us -> none  [attend(): pl.pallas_call(functools.partial(attend_kernel, tiles), out_shape=[jax.Sh...]
    pallas_call x1, Pallas kernels: 81.8 us -> 92.7 us  [deal_in(): pl.pallas_call(functools.partial(deal_in_kernel, n, groups), out_shape=[j...]
  transfers between devices with their start and end apart: 2 -> 2, of which waited for: 0 -> 0; matrix products, arithmetic and copies ran while one was open for 2% -> 2% of each run, Pallas kernels for 36% -> 37%
where the time goes in v6:
time: 616 us; the launch traced here: 607 us
  Pallas kernels  540 us (88%)
  matrix products  30.2 us (5%)
  between operations  14.6 us (2%)
  local copies, waits for them, and re-layouts  12.8 us (2%)
  other arithmetic  9.5 us (2%)
    pallas_call x1, Pallas kernels, middle(): pl.pallas_call(functools.partial(middle_kernel, n), out_shape=[jax.ShapeD...  223 us
    pallas_call x1, Pallas kernels, second_back_of(): pl.pallas_call(functools.partial(second_back_kernel, n), out_shape=[jax.S...  116 us
    pallas_call x1, Pallas kernels, deal_out(): pl.pallas_call(functools.partial(deal_out_kernel, n, groups, tiles, chunk...  108 us
    pallas_call x1, Pallas kernels, deal_in(): pl.pallas_call(functools.partial(deal_in_kernel, n, groups), out_shape=[j...  92.7 us
    dot_general x5, matrix products, matmul(): return jnp.dot(left, right, preferred_element_type=jnp.float32)  30.2 us
  transfers between devices with their start and end apart: 2, of which 0 were waited for; matrix products, arithmetic and copies ran while one was open for 2% of the time, Pallas kernels for 37%

profile of v6, /device:TPU:0, one launch (start us, length us, event | category | flops | bytes accessed | tf_op | source)
XLA Modules:
  0.0 607.0 jit_solution(2545366637699184881)
XLA Ops:
  7.2 0.0 reduce-scatter.3.cloned.1.call-start
  7.2 0.7 and_select_fusion
  7.9 0.8 select_reduce_fusion.9
  8.7 0.1 select_reduce_fusion.8
  8.9 0.9 select_reduce_fusion.7
  9.7 0.7 fusion.19
  10.4 0.1 select_reduce_fusion
  10.5 0.0 copy-start.6
  10.5 3.6 fusion.10
  14.1 0.0 copy-done.6
  14.1 2.3 fusion.11
  16.4 0.1 select_reduce_fusion.2
  16.5 0.1 reduce_sum.109
  16.6 0.1 mul.181
  16.7 0.1 convert_element_type.61
  16.7 0.2 broadcast_multiply_fusion
  17.0 2.7 fusion.12
  19.7 0.2 slice_negate_fusion
  19.9 0.7 add.124.code_row.refs_12_
  20.6 0.1 mul.182
  20.6 0.1 add.125
  20.7 1.0 copy.44.low_col.refs_14_
  21.8 1.0 copy.43.code_col.refs_13_
  22.8 0.1 convert_element_type.64
  22.9 1.3 convert_element_type.74.keep
  24.2 1.0 pad_maximum_fusion.1.sine.refs_11_
  25.2 92.7 %shard_map.221 = (bf16[4,8,32,2048]{3,2,1,0:T(8,128)(2,1)}, bf16[4,8,32,512]{3,2,1,0:T(8,128)(2,1)}, bf16[4,8,32,512]{3,2,1,0:T(8,128)(2,1)}, bf16[1024,2048]{1,...) custom-call(bf16[8,4,32,512]{3,2,1,0:T(8,128)(2,1)} %bitcast.23, ...), custom_call_target="tpu_custom_call" | custom-call | tf_op jit(solution)/shard_map/pallas_call | solution.py:744
  118.0 222.9 %shard_map.222 = (bf16[1024,512]{1,0:T(8,128)(2,1)}, bf16[1024,2048]{1,0:T(8,128)(2,1)}, bf16[1024,2048]{1,0:T(8,128)(2,1)}, bf16[1024,2048]{1,0:T(8,128)(2,1)},...) custom-call(bf16[1024,2048]{1,0:T(8,128)(2,1)} %get-tuple-element.47.part, ...), custom_call_target="tpu_custom_call" | custom-call | tf_op jit(solution)/shard_map/pallas_call | solution.py:461
  340.9 18.5 %convolution_convert_fusion = bf16[2048,2816]{1,0:T(8,128)(2,1)} fusion(bf16[1024,2048]{1,0:T(8,128)(2,1)} %get-tuple-element.51, bf16[1024,2816]{1,0:T(8,128)(2,1)} %get-tuple-element.52), kind=kOutput, calls=%fused_computation | convolution fusion | flops 11816927232 | bytes 21495808 | tf_op jit(solution)/shard_map/dot_general | solution.py:1151
  359.4 0.0 reduce-scatter.3.cloned.1.call-update
  359.4 0.0 reduce-scatter.5.cloned.1.call-start
  359.4 115.9 %shard_map.223 = (bf16[1024,2048]{1,0:T(8,128)(2,1)}, f32[1024,512]{1,0:T(8,128)}, f32[1,2048]{1,0:T(1,128)}, bf16[2048,1408]{1,0:T(8,128)(2,1)}) custom-call(bf16[1024,2048]{1,0:T(8,128)(2,1)} %get-tuple-element.54.part, bf16[1024,2048]{1,0:T(8,128)(2,1)} %bitcast.22, bf16[1024,2048]{1,0:T(8,128)(2,1)} %get-tuple-element.55.a, ...), custom_call_target="tpu_custom_call" | custom-call | tf_op jit(solution)/shard_map/pallas_call | solution.py:566
  475.3 0.0 copy-start.5
  475.3 0.0 reduce-scatter.3.cloned.1.call-done
  475.4 0.0 reduce-scatter.5.cloned.1.call-update
  475.4 0.6 copy-done.5
  476.0 0.6 reshape.227.gain1
  476.6 0.1 select_reduce_fusion.1
  476.7 108.3 %shard_map.224 = (bf16[8,4,32,512]{3,2,1,0:T(8,128)(2,1)}, bf16[8,4,32,512]{3,2,1,0:T(8,128)(2,1)}, f32[16,256]{1,0:T(8,128)}, f32[256,512]{1,0:T(8,128)}, f32[2...) custom-call(bf16[1024,512]{1,0:T(8,128)(2,1)} %bitcast.25, f32[1024,512]{1,0:T(8,128)} %get-tuple-element.62.dh, ...), custom_call_target="tpu_custom_call" | custom-call | tf_op jit(solution)/shard_map/pallas_call | solution.py:1093
  585.0 2.0 copy.49
  587.0 1.3 fusion.18
  588.3 0.0 copy-start
  588.3 3.6 fusion.9
  591.9 0.0 copy-done
  591.9 0.0 copy-start.7
  591.9 1.8 slice_convert_fusion
  593.7 0.0 reduce-scatter.5.cloned.1.call-done
  593.7 0.0 copy-done.7
  593.7 0.0 copy-start.1
  593.7 2.3 fusion.8
  596.0 0.0 copy-done.1
  596.0 0.0 copy-start.2
  596.0 0.0 copy-start.4
  596.0 0.0 copy-start.3
  596.0 0.1 convert_bitcast_fusion
  596.1 1.5 copy.50
  597.6 0.0 copy-done.2
  597.6 0.8 copy.54
  598.4 0.0 copy-done.4
  598.4 0.7 copy.55
  599.1 0.0 copy-done.3
  599.1 0.7 copy.56
  (11 shorter events, 0.1 us)
Async XLA Ops:
  7.2 468.2 %reduce-scatter.3.cloned.1.call-start = ((), (), s32[]{:S(2)}) async-start(), calls=%async_computation.2 | async-start | bytes 12976128 | tf_op jit(solution)/shard_map/reduce_scatter | solution.py:1266
  10.5 3.6 copy-start.6
  359.4 234.3 %reduce-scatter.5.cloned.1.call-start = ((), (), s32[]{:S(2)}) async-start(), calls=%async_computation.3 | async-start | bytes 6488064 | tf_op jit(solution)/shard_map/reduce_scatter | solution.py:1266
  475.3 0.7 copy-start.5
  588.3 3.6 copy-start
  591.9 1.8 copy-start.7
  593.7 2.3 copy-start.1
  596.0 1.7 copy-start.2
  596.0 2.4 copy-start.4
  596.0 3.1 copy-start.3
Sparse Core Ops, SparseCore 0:
  359.5 86.9 reduce-scatter.2
  475.5 73.0 reduce-scatter.4

commit v7 on v6

--- a/solution.py
+++ b/solution.py
@@ -292,9 +292,9 @@
     lax.fori_loop(0, rows // BLOCK, drain, 0)
 
 
-def middle_kernel(n, part, x, g_part, keep, gain, wg_far, wu_far, wd_far,
+def middle_kernel(n, part, x_far, g_part, keep, gain, wg_far, wu_far, wd_far,
                   result, a_far, g_far, n2_far, inner_far, both_far, dn2_far,
-                  wg, wu, wd, up, total, g, right, left, gate_s, upper_s, n2_s, inner_s, both_s, f_s, dn2_s,
+                  wg, wu, wd, x, up, total, g, right, left, gate_s, upper_s, n2_s, inner_s, both_s, f_s, dn2_s,
                   us, ur, ds, dr, ss, rs, fs, fr, load, own, save, late):
     z = lax.axis_index("tensor")
     rows, width = part.shape
@@ -302,7 +302,7 @@
     hidden = wg.shape[1]
     tile = 2 * BLOCK
     sums = (us, ur, ds, dr)
-    loads = [pltpu.make_async_copy(a, b, load.at[i]) for i, (a, b) in enumerate(((wg_far, wg), (wu_far, wu), (wd_far, wd)))]
+    loads = [pltpu.make_async_copy(a, b, load.at[i]) for i, (a, b) in enumerate(((x_far, x), (wg_far, wg), (wu_far, wu), (wd_far, wd)))]
     for copy in loads:
         copy.start()
     mine = pltpu.make_async_copy(g_part, g.at[:, pl.ds(pl.multiple_of(z * w, w), w)], own)
@@ -461,12 +461,13 @@
     return pl.pallas_call(
         functools.partial(middle_kernel, n),
         out_shape=[jax.ShapeDtypeStruct((rows, k), BF) for k in widths],
-        in_specs=[VM] * 5 + [ANY] * 3,
+        in_specs=[VM, ANY] + [VM] * 3 + [ANY] * 3,
         out_specs=[VM] + [ANY] * 6,
         scratch_shapes=[
             pltpu.VMEM(wg.shape, BF),
             pltpu.VMEM(wu.shape, BF),
             pltpu.VMEM(wd.shape, BF),
+            pltpu.VMEM((rows, width), BF),
             pltpu.VMEM((rows, width), BF),
             pltpu.VMEM((rows, width), BF),
             pltpu.VMEM((rows, width), BF),
@@ -484,7 +485,7 @@
             pltpu.SemaphoreType.DMA((2, n, blocks)),
             pltpu.SemaphoreType.DMA((2, n, rows // tile * 4)),
             pltpu.SemaphoreType.DMA((2, n, rows // tile * 4)),
-            pltpu.SemaphoreType.DMA((3,)),
+            pltpu.SemaphoreType.DMA((4,)),
             pltpu.SemaphoreType.DMA,
             pltpu.SemaphoreType.DMA((4,)),
             pltpu.SemaphoreType.DMA((2,)),
@@ -493,14 +494,15 @@
     )(part, x, g_part, keep, gain, wg, wu, wd)
 
 
-def second_back_kernel(n, part, x, a, g, keep, gain, inner_far, ga, dh, gain_grad, grad_far,
-                       up, total, inner, stage, us, ur, ds, dr, load, save):
+def second_back_kernel(n, part, x_far, a_far, g_far, keep, gain, inner_far, ga, dh, gain_grad, grad_far,
+                       up, total, x, a, g, inner, stage, us, ur, ds, dr, load, save):
     z = lax.axis_index("tensor")
     rows, width = part.shape
     w = dh.shape[1]
     piece = BLOCK // 2
     sums = (us, ur, ds, dr)
-    loads = [pltpu.make_async_copy(inner_far, inner, load.at[0])]
+    pairs = ((g_far, g), (inner_far, inner), (x_far, x), (a_far, a))
+    loads = [pltpu.make_async_copy(far, near, load.at[i]) for i, (far, near) in enumerate(pairs)]
     for copy in loads:
         copy.start()
     neighbour_barrier(z, n, "tensor")
@@ -571,15 +573,16 @@
             jax.ShapeDtypeStruct((1, width), F32),
             jax.ShapeDtypeStruct((width, inner.shape[1]), BF),
         ],
-        in_specs=[VM] * 6 + [ANY],
+        in_specs=[VM] + [ANY] * 3 + [VM] * 2 + [ANY],
         out_specs=[VM] * 3 + [ANY],
         scratch_shapes=[
             pltpu.VMEM((rows, width), BF),
             pltpu.VMEM((rows, width), BF),
+            *(pltpu.VMEM((rows, width), BF) for _ in range(3)),
             pltpu.VMEM(inner.shape, BF),
             pltpu.VMEM((2, 256, inner.shape[1]), BF),
             *line_sum_sems(rows),
-            pltpu.SemaphoreType.DMA((2,)),
+            pltpu.SemaphoreType.DMA((4,)),
             pltpu.SemaphoreType.DMA((2,)),
         ],
         compiler_params=pltpu.CompilerParams(collective_id=4, has_side_effects=True, vmem_limit_bytes=60 << 20),
@@ -774,9 +777,9 @@
     )
 
 
-def deal_out_kernel(n, groups, tiles, chunk, lag, x, dh, scale1, gain1, result, gain2, normed, *refs):
+def deal_out_kernel(n, groups, tiles, chunk, lag, x, dh, scale1, gain1, result, gain2, normed_far, *refs):
     attention = refs[:15]
-    (back_out, back_dx, gains, o_share, q_share, k_share, v_share, part, dqkv, dk, dv, right, left, fb, dx, lines, widths, gsrc, gdst, wsrc, wdst, pair,
+    (back_out, back_dx, gains, o_share, q_share, k_share, v_share, part, dqkv, dk, dv, right, left, fb, dx, lines, widths, gsrc, gdst, wsrc, wdst, pair, normed,
      ss, rs, os, orr, xs, xr, ls, lr, ws, wr, es, er, qs, qr, ps, pr, own) = refs[15:]
     ga, o = attention[0], attention[8]
     z = lax.axis_index("tensor")
@@ -787,6 +790,8 @@
     per = tile // chunk
     sub = result.shape[2]
     pltpu.make_async_copy(result.at[:, me], back_out.at[me], own.at[0]).start()
+    fetch = pltpu.make_async_copy(normed_far, normed, own.at[2 + tiles])
+    fetch.start()
     peers_barrier(z, n, me, groups, True)
 
     def send_out(off, _):
@@ -919,7 +924,7 @@
     def flows(s, _):
         for k in range(tiles):
 
-            @pl.when(s == k * per)
+            @pl.when(s == k * 3)
             def _():
                 attend_back_tile(tiles - 1 - k, tiles, *attention, part, dqkv, dk, dv)
 
@@ -931,12 +936,13 @@
         def _():
             join(*joined[0], 0)
 
-        @pl.when(s == (tiles - 1) * per + 3)
+        @pl.when(s == (tiles - 1) * 3 + 3)
         def _():
             join(*joined[1], 1)
 
-        @pl.when(s == (tiles - 1) * per + 1)
-        def _():
+        @pl.when(s == (tiles - 1) * 3 + 1)
+        def _():
+            fetch.wait()
             weigh(normed, dqkv, ow, 1)
 
         for d, buf, step in ((0, right, 1), (1, left, -1)):
@@ -1099,7 +1105,7 @@
             jax.ShapeDtypeStruct((cols, attention[8].shape[1]), F32),
             *(jax.ShapeDtypeStruct((cols, a.shape[1]), F32) for a in attention[1:4]),
         ],
-        in_specs=[VM] * 22,
+        in_specs=[VM] * 6 + [ANY] + [VM] * 15,
         out_specs=[VM] * 7,
         scratch_shapes=[
             pltpu.VMEM((rows, width), BF),
@@ -1117,6 +1123,7 @@
             pltpu.VMEM((width, both), BF),
             pltpu.VMEM((groups // 2, cols, both), BF),
             pltpu.VMEM((groups // 2, cols, both), BF),
+            pltpu.VMEM(normed.shape, BF),
             dma((2, n, count)),
             dma((2, n, count)),
             dma((groups,)),
@@ -1133,7 +1140,7 @@
             dma((2, groups // 2)),
             dma((2, groups // 2)),
             dma((2, groups // 2)),
-            dma((tiles + 2,)),
+            dma((tiles + 3,)),
         ],
         compiler_params=pltpu.CompilerParams(collective_id=5, has_side_effects=True, vmem_limit_bytes=62 << 20),
     )(x, dh, scale1, gain1, result.reshape(tiles, groups, sub, w), gain2, normed, *attention)

time: 616 us -> 609 us (0.989)
  transfers between devices with their start and end apart: 2 -> 2, of which waited for: 0 -> 0; matrix products, arithmetic and copies ran while one was open for 2% -> 2% of each run, Pallas kernels for 37% -> 36%
where the time goes in v7:
time: 609 us; the launch traced here: 601 us
  Pallas kernels  534 us (88%)
  matrix products  30.2 us (5%)
  between operations  14.6 us (2%)
  local copies, waits for them, and re-layouts  12.8 us (2%)
  other arithmetic  9.5 us (2%)
    pallas_call x1, Pallas kernels, middle(): pl.pallas_call(functools.partial(middle_kernel, n), out_shape=[jax.ShapeD...  222 us
    pallas_call x1, Pallas kernels, second_back_of(): pl.pallas_call(functools.partial(second_back_kernel, n), out_shape=[jax.S...  112 us
    pallas_call x1, Pallas kernels, deal_out(): pl.pallas_call(functools.partial(deal_out_kernel, n, groups, tiles, chunk...  107 us
    pallas_call x1, Pallas kernels, deal_in(): pl.pallas_call(functools.partial(deal_in_kernel, n, groups), out_shape=[j...  92.7 us
    dot_general x5, matrix products, matmul(): return jnp.dot(left, right, preferred_element_type=jnp.float32)  30.2 us
  transfers between devices with their start and end apart: 2, of which 0 were waited for; matrix products, arithmetic and copies ran while one was open for 2% of the time, Pallas kernels for 36%

profile of v7, /device:TPU:0, one launch (start us, length us, event | category | flops | bytes accessed | tf_op | source)
XLA Modules:
  0.0 601.0 jit_solution(16489473793470613257)
XLA Ops:
  7.2 0.0 reduce-scatter.3.cloned.1.call-start
  7.2 0.7 and_select_fusion
  7.9 0.8 select_reduce_fusion.9
  8.7 0.1 select_reduce_fusion.8
  8.9 0.9 select_reduce_fusion.7
  9.7 0.7 fusion.19
  10.4 0.1 select_reduce_fusion
  10.5 0.0 copy-start.6
  10.5 3.6 fusion.10
  14.1 0.0 copy-done.6
  14.1 2.3 fusion.11
  16.4 0.1 select_reduce_fusion.2
  16.5 0.1 reduce_sum.109
  16.6 0.1 mul.181
  16.7 0.1 convert_element_type.61
  16.7 0.2 broadcast_multiply_fusion
  17.0 2.7 fusion.12
  19.7 0.2 slice_negate_fusion
  19.9 0.7 add.124.code_row.refs_12_
  20.6 0.1 mul.182
  20.6 0.1 add.125
  20.7 1.0 copy.44.low_col.refs_14_
  21.8 1.0 copy.43.code_col.refs_13_
  22.8 0.1 convert_element_type.64
  22.9 1.3 convert_element_type.74.keep
  24.2 1.0 pad_maximum_fusion.1.sine.refs_11_
  25.2 92.7 %shard_map.221 = (bf16[4,8,32,2048]{3,2,1,0:T(8,128)(2,1)}, bf16[4,8,32,512]{3,2,1,0:T(8,128)(2,1)}, bf16[4,8,32,512]{3,2,1,0:T(8,128)(2,1)}, bf16[1024,2048]{1,...) custom-call(bf16[8,4,32,512]{3,2,1,0:T(8,128)(2,1)} %bitcast.23, ...), custom_call_target="tpu_custom_call" | custom-call | tf_op jit(solution)/shard_map/pallas_call | solution.py:747
  118.0 221.7 %shard_map.222 = (bf16[1024,512]{1,0:T(8,128)(2,1)}, bf16[1024,2048]{1,0:T(8,128)(2,1)}, bf16[1024,2048]{1,0:T(8,128)(2,1)}, bf16[1024,2048]{1,0:T(8,128)(2,1)},...) custom-call(bf16[1024,2048]{1,0:T(8,128)(2,1)} %get-tuple-element.47.part, ...), custom_call_target="tpu_custom_call" | custom-call | tf_op jit(solution)/shard_map/pallas_call | solution.py:461
  339.7 18.5 %convolution_convert_fusion = bf16[2048,2816]{1,0:T(8,128)(2,1)} fusion(bf16[1024,2048]{1,0:T(8,128)(2,1)} %get-tuple-element.51, bf16[1024,2816]{1,0:T(8,128)(2,1)} %get-tuple-element.52), kind=kOutput, calls=%fused_computation | convolution fusion | flops 11816927232 | bytes 21495808 | tf_op jit(solution)/shard_map/dot_general | solution.py:1158
  358.1 0.0 reduce-scatter.3.cloned.1.call-update
  358.2 0.0 reduce-scatter.5.cloned.1.call-start
  358.2 111.9 %shard_map.223 = (bf16[1024,2048]{1,0:T(8,128)(2,1)}, f32[1024,512]{1,0:T(8,128)}, f32[1,2048]{1,0:T(1,128)}, bf16[2048,1408]{1,0:T(8,128)(2,1)}) custom-call(bf16[1024,2048]{1,0:T(8,128)(2,1)} %get-tuple-element.54.part, bf16[1024,2048]{1,0:T(8,128)(2,1)} %bitcast.22, bf16[1024,2048]{1,0:T(8,128)(2,1)} %get-tuple-element.55.a_far, ...), custom_call_target="tpu_custom_call" | custom-call | tf_op jit(solution)/shard_map/pallas_call | solution.py:568
  470.1 0.0 copy-start.5
  470.1 0.0 reduce-scatter.3.cloned.1.call-done
  470.2 0.0 reduce-scatter.5.cloned.1.call-update
  470.2 0.6 copy-done.5
  470.8 0.6 reshape.227.gain1
  471.4 0.1 select_reduce_fusion.1
  471.5 107.4 %shard_map.224 = (bf16[8,4,32,512]{3,2,1,0:T(8,128)(2,1)}, bf16[8,4,32,512]{3,2,1,0:T(8,128)(2,1)}, f32[16,256]{1,0:T(8,128)}, f32[256,512]{1,0:T(8,128)}, f32[2...) custom-call(bf16[1024,512]{1,0:T(8,128)(2,1)} %bitcast.25, f32[1024,512]{1,0:T(8,128)} %get-tuple-element.62.dh, ...), custom_call_target="tpu_custom_call" | custom-call | tf_op jit(solution)/shard_map/pallas_call | solution.py:1099
  578.9 2.0 copy.49
  581.0 1.3 fusion.18
  582.3 0.0 copy-start
  582.3 3.6 fusion.9
  585.9 0.0 copy-done
  585.9 0.0 copy-start.7
  585.9 1.8 slice_convert_fusion
  587.6 0.0 reduce-scatter.5.cloned.1.call-done
  587.6 0.0 copy-done.7
  587.7 0.0 copy-start.1
  587.7 2.3 fusion.8
  589.9 0.0 copy-done.1
  589.9 0.0 copy-start.2
  589.9 0.0 copy-start.4
  589.9 0.0 copy-start.3
  589.9 0.1 convert_bitcast_fusion
  590.0 1.5 copy.50
  591.6 0.0 copy-done.2
  591.6 0.8 copy.54
  592.4 0.0 copy-done.4
  592.4 0.7 copy.55
  593.0 0.0 copy-done.3
  593.0 0.7 copy.56
  (11 shorter events, 0.1 us)
Async XLA Ops:
  7.2 463.0 %reduce-scatter.3.cloned.1.call-start = ((), (), s32[]{:S(2)}) async-start(), calls=%async_computation.2 | async-start | bytes 12976128 | tf_op jit(solution)/shard_map/reduce_scatter | solution.py:1273
  10.5 3.6 copy-start.6
  358.2 229.5 %reduce-scatter.5.cloned.1.call-start = ((), (), s32[]{:S(2)}) async-start(), calls=%async_computation.3 | async-start | bytes 6488064 | tf_op jit(solution)/shard_map/reduce_scatter | solution.py:1273
  470.1 0.7 copy-start.5
  582.3 3.6 copy-start
  585.9 1.8 copy-start.7
  587.7 2.3 copy-start.1
  589.9 1.7 copy-start.2
  589.9 2.4 copy-start.4
  589.9 3.1 copy-start.3
Sparse Core Ops, SparseCore 0:
  358.3 86.9 reduce-scatter.2
  470.3 84.5 reduce-scatter.4

commit v8 on v7

--- a/solution.py
+++ b/solution.py
@@ -1085,7 +1085,7 @@
     lax.fori_loop(0, count, drain, 0)
 
 
-def deal_out(n, groups, tiles, x, dh, scale1, gain1, result, gain2, normed, *attention, chunk=64, lag=2):
+def deal_out(n, groups, tiles, x, dh, scale1, gain1, result, gain2, normed, *attention, chunk=64, lag=1):
     rows, w = x.shape
     width = n * w
     sub = rows // tiles // groups

time: 609 us -> 610 us (level)
  transfers between devices with their start and end apart: 2 -> 2, of which waited for: 0 -> 0; matrix products, arithmetic and copies ran while one was open for 2% -> 2% of each run, Pallas kernels for 36% -> 37%
where the time goes in v8:
time: 610 us; the launch traced here: 601 us
  Pallas kernels  534 us (88%)
  matrix products  30.2 us (5%)
  between operations  14.6 us (2%)
  local copies, waits for them, and re-layouts  12.8 us (2%)
  other arithmetic  9.5 us (2%)
    pallas_call x1, Pallas kernels, middle(): pl.pallas_call(functools.partial(middle_kernel, n), out_shape=[jax.ShapeD...  222 us
    pallas_call x1, Pallas kernels, second_back_of(): pl.pallas_call(functools.partial(second_back_kernel, n), out_shape=[jax.S...  112 us
    pallas_call x1, Pallas kernels, deal_out(): pl.pallas_call(functools.partial(deal_out_kernel, n, groups, tiles, chunk...  108 us
    pallas_call x1, Pallas kernels, deal_in(): pl.pallas_call(functools.partial(deal_in_kernel, n, groups), out_shape=[j...  92.7 us
    dot_general x5, matrix products, matmul(): return jnp.dot(left, right, preferred_element_type=jnp.float32)  30.2 us
  transfers between devices with their start and end apart: 2, of which 0 were waited for; matrix products, arithmetic and copies ran while one was open for 2% of the time, Pallas kernels for 37%

profile of v8, /device:TPU:0, one launch (start us, length us, event | category | flops | bytes accessed | tf_op | source)
XLA Modules:
  0.0 601.5 jit_solution(4158365025390362734)
XLA Ops:
  7.2 0.0 reduce-scatter.3.cloned.1.call-start
  7.2 0.7 and_select_fusion
  7.9 0.8 select_reduce_fusion.9
  8.7 0.1 select_reduce_fusion.8
  8.9 0.9 select_reduce_fusion.7
  9.7 0.7 fusion.19
  10.4 0.1 select_reduce_fusion
  10.5 0.0 copy-start.6
  10.5 3.6 fusion.10
  14.1 0.0 copy-done.6
  14.1 2.3 fusion.11
  16.4 0.1 select_reduce_fusion.2
  16.5 0.1 reduce_sum.109
  16.6 0.1 mul.181
  16.7 0.1 convert_element_type.61
  16.7 0.2 broadcast_multiply_fusion
  17.0 2.7 fusion.12
  19.7 0.2 slice_negate_fusion
  19.9 0.7 add.124.code_row.refs_12_
  20.6 0.1 mul.182
  20.6 0.1 add.125
  20.7 1.0 copy.44.low_col.refs_14_
  21.8 1.0 copy.43.code_col.refs_13_
  22.8 0.1 convert_element_type.64
  22.9 1.3 convert_element_type.74.keep
  24.2 1.0 pad_maximum_fusion.1.sine.refs_11_
  25.2 92.7 %shard_map.221 = (bf16[4,8,32,2048]{3,2,1,0:T(8,128)(2,1)}, bf16[4,8,32,512]{3,2,1,0:T(8,128)(2,1)}, bf16[4,8,32,512]{3,2,1,0:T(8,128)(2,1)}, bf16[1024,2048]{1,...) custom-call(bf16[8,4,32,512]{3,2,1,0:T(8,128)(2,1)} %bitcast.23, ...), custom_call_target="tpu_custom_call" | custom-call | tf_op jit(solution)/shard_map/pallas_call | solution.py:747
  118.0 221.7 %shard_map.222 = (bf16[1024,512]{1,0:T(8,128)(2,1)}, bf16[1024,2048]{1,0:T(8,128)(2,1)}, bf16[1024,2048]{1,0:T(8,128)(2,1)}, bf16[1024,2048]{1,0:T(8,128)(2,1)},...) custom-call(bf16[1024,2048]{1,0:T(8,128)(2,1)} %get-tuple-element.47.part, ...), custom_call_target="tpu_custom_call" | custom-call | tf_op jit(solution)/shard_map/pallas_call | solution.py:461
  339.7 18.5 %convolution_convert_fusion = bf16[2048,2816]{1,0:T(8,128)(2,1)} fusion(bf16[1024,2048]{1,0:T(8,128)(2,1)} %get-tuple-element.51, bf16[1024,2816]{1,0:T(8,128)(2,1)} %get-tuple-element.52), kind=kOutput, calls=%fused_computation | convolution fusion | flops 11816927232 | bytes 21495808 | tf_op jit(solution)/shard_map/dot_general | solution.py:1158
  358.1 0.0 reduce-scatter.3.cloned.1.call-update
  358.2 0.0 reduce-scatter.5.cloned.1.call-start
  358.2 111.9 %shard_map.223 = (bf16[1024,2048]{1,0:T(8,128)(2,1)}, f32[1024,512]{1,0:T(8,128)}, f32[1,2048]{1,0:T(1,128)}, bf16[2048,1408]{1,0:T(8,128)(2,1)}) custom-call(bf16[1024,2048]{1,0:T(8,128)(2,1)} %get-tuple-element.54.part, bf16[1024,2048]{1,0:T(8,128)(2,1)} %bitcast.22, bf16[1024,2048]{1,0:T(8,128)(2,1)} %get-tuple-element.55.a_far, ...), custom_call_target="tpu_custom_call" | custom-call | tf_op jit(solution)/shard_map/pallas_call | solution.py:568
  470.1 0.0 copy-start.5
  470.1 0.0 reduce-scatter.3.cloned.1.call-done
  470.2 0.0 reduce-scatter.5.cloned.1.call-update
  470.2 0.6 copy-done.5
  470.8 0.6 reshape.227.gain1
  471.4 0.1 select_reduce_fusion.1
  471.5 107.9 %shard_map.224 = (bf16[8,4,32,512]{3,2,1,0:T(8,128)(2,1)}, bf16[8,4,32,512]{3,2,1,0:T(8,128)(2,1)}, f32[16,256]{1,0:T(8,128)}, f32[256,512]{1,0:T(8,128)}, f32[2...) custom-call(bf16[1024,512]{1,0:T(8,128)(2,1)} %bitcast.25, f32[1024,512]{1,0:T(8,128)} %get-tuple-element.62.dh, ...), custom_call_target="tpu_custom_call" | custom-call | tf_op jit(solution)/shard_map/pallas_call | solution.py:1099
  579.5 2.0 copy.49
  581.5 1.3 fusion.18
  582.8 0.0 copy-start
  582.8 3.6 fusion.9
  586.4 0.0 copy-done
  586.4 0.0 copy-start.7
  586.4 1.8 slice_convert_fusion
  588.2 0.0 reduce-scatter.5.cloned.1.call-done
  588.2 0.0 copy-done.7
  588.2 0.0 copy-start.1
  588.2 2.3 fusion.8
  590.4 0.0 copy-done.1
  590.4 0.0 copy-start.2
  590.4 0.0 copy-start.4
  590.4 0.0 copy-start.3
  590.4 0.1 convert_bitcast_fusion
  590.5 1.5 copy.50
  592.1 0.0 copy-done.2
  592.1 0.8 copy.54
  592.9 0.0 copy-done.4
  592.9 0.7 copy.55
  593.5 0.0 copy-done.3
  593.5 0.7 copy.56
  (11 shorter events, 0.1 us)
Async XLA Ops:
  7.2 463.0 %reduce-scatter.3.cloned.1.call-start = ((), (), s32[]{:S(2)}) async-start(), calls=%async_computation.2 | async-start | bytes 12976128 | tf_op jit(solution)/shard_map/reduce_scatter | solution.py:1273
  10.5 3.6 copy-start.6
  358.2 230.0 %reduce-scatter.5.cloned.1.call-start = ((), (), s32[]{:S(2)}) async-start(), calls=%async_computation.3 | async-start | bytes 6488064 | tf_op jit(solution)/shard_map/reduce_scatter | solution.py:1273
  470.1 0.7 copy-start.5
  582.8 3.6 copy-start
  586.4 1.8 copy-start.7
  588.2 2.3 copy-start.1
  590.4 1.7 copy-start.2
  590.4 2.4 copy-start.4
  590.4 3.1 copy-start.3
Sparse Core Ops, SparseCore 0:
  358.3 86.9 reduce-scatter.2
  470.3 81.5 reduce-scatter.4
